TPU v7x, 256 devices: a whole 4x4x8 slice. The times are simulated.
256 devices in a mesh: dp: 32 (over y, z_hi, core), expert: 8 (over z_lo, x).
Axes of the slice: x: 4, y: 4, z: 8 (z_hi: 4, z_lo: 2; z = z_hi * 2 + z_lo), core: 2. Of those that a mesh axis runs over, the one named last changes fastest.
Arguments:
- tokens: bfloat16 [512, 256, 1280], P(('dp', 'expert')), may hold values from -6 to 6
- grad_out: bfloat16 [512, 256, 1280], P(('dp', 'expert')), may hold values from -3 to 3
- logits: float32 [512, 32, 256], P(('dp', 'expert')), may hold values from -320 to 320
- router: bfloat16 [32, 1280], replicated, may hold values from -0.15625 to 0.15625
- fc1_out: bfloat16 [32, 512, 5120], P('dp', None, 'expert'), may hold values from -6 to 6
- w_in: bfloat16 [32, 1280, 5120], P('dp', None, 'expert'), may hold values from -0.15625 to 0.15625
- w_out: bfloat16 [32, 5120, 1280], P('dp', 'expert'), may hold values from -0.078125 to 0.078125
Outputs:
- grad_tokens: bfloat16 [512, 256, 1280], P(('dp', 'expert'))
- grad_router: float32 [32, 1280], replicated
- grad_w_in: bfloat16 [32, 1280, 5120], P('dp', None, 'expert')
- grad_w_out: bfloat16 [32, 5120, 1280], P('dp', 'expert')
All inputs are finite; a program needn't handle non-finite values.
Results may differ from a plain program's by a relative error of at most 0.02.
Values may be sent and summed in bfloat16 or wider, within the bound.
No kernel may reach another device: no remote copies, remote signals or barrier semaphores. Data moves between devices by JAX's collectives and lax.ppermute only.
A program may use at most 64 MiB of HBM per device.

v0:
```python
import jax
import jax.numpy as jnp
from jax import lax
from jax.sharding import PartitionSpec as P


def gelu_slope(value):
    cdf = 0.5 * (1.0 + jax.scipy.special.erf(value * 0.7071067811865476))
    density = jnp.exp(-0.5 * value * value) * 0.3989422804014327
    return cdf + value * density


def on_device(tokens, grad_out, logits, router, fc1_out, w_in, w_out):
    over_tokens = jnp.exp(logits - jnp.max(logits, axis=2, keepdims=True))
    disp = over_tokens / jnp.sum(over_tokens, axis=2, keepdims=True)
    over_slots = jnp.exp(logits - jnp.max(logits, axis=1, keepdims=True))
    comb = over_slots / jnp.sum(over_slots, axis=1, keepdims=True)
    disp_b = disp.astype(jnp.bfloat16)
    comb_b = comb.astype(jnp.bfloat16)
    slot_in = jnp.einsum("bem,bmd->bed", disp_b, tokens, preferred_element_type=jnp.float32).astype(
        jnp.bfloat16
    )
    slot_grad = jnp.einsum(
        "bem,bmd->bed", comb_b, grad_out, preferred_element_type=jnp.float32
    ).astype(jnp.bfloat16)
    exp_local = w_in.shape[0]
    img_local = tokens.shape[0]
    dp_count = lax.axis_size("dp")
    ex_count = lax.axis_size("expert")
    moved_in, moved_grad = (
        lax.all_to_all(slot_in, "dp", split_axis=1, concat_axis=0, tiled=True),
        lax.all_to_all(slot_grad, "dp", split_axis=1, concat_axis=0, tiled=True),
    )
    all_in, all_grad = (
        lax.all_gather(moved_in, "expert", axis=0, tiled=True),
        lax.all_gather(moved_grad, "expert", axis=0, tiled=True),
    )
    hidden_local = fc1_out.shape[2]
    shaped_pre = fc1_out.reshape(exp_local, dp_count, ex_count, img_local, hidden_local)
    pre = jnp.transpose(shaped_pre, (0, 2, 1, 3, 4)).reshape(exp_local, -1, hidden_local)
    pre_f = pre.astype(jnp.float32)
    act = jax.nn.gelu(pre_f, approximate=False).astype(jnp.bfloat16)
    act_grad = jnp.einsum("red,efd->erf", all_grad, w_out, preferred_element_type=jnp.float32)
    hid_grad = (act_grad * gelu_slope(pre_f)).astype(jnp.bfloat16)
    grad_w_out = jnp.einsum(
        "erf,red->efd", act, all_grad, preferred_element_type=jnp.float32
    ).astype(jnp.bfloat16)
    grad_w_in = jnp.einsum(
        "red,erf->edf", all_in, hid_grad, preferred_element_type=jnp.float32
    ).astype(jnp.bfloat16)
    out_sum = lax.psum_scatter(
        jnp.einsum("erf,efd->red", act, w_out, preferred_element_type=jnp.float32).astype(
            jnp.bfloat16
        ),
        "expert",
        scatter_dimension=0,
        tiled=True,
    )
    back_sum = lax.psum_scatter(
        jnp.einsum("erf,edf->red", hid_grad, w_in, preferred_element_type=jnp.float32).astype(
            jnp.bfloat16
        ),
        "expert",
        scatter_dimension=0,
        tiled=True,
    )
    slot_out, slot_back = (
        lax.all_to_all(out_sum, "dp", split_axis=0, concat_axis=1, tiled=True),
        lax.all_to_all(back_sum, "dp", split_axis=0, concat_axis=1, tiled=True),
    )
    comb_grad = jnp.einsum("bed,bmd->bem", slot_out, grad_out, preferred_element_type=jnp.float32)
    disp_grad = jnp.einsum("bed,bmd->bem", slot_back, tokens, preferred_element_type=jnp.float32)
    through_comb = comb * (comb_grad - jnp.sum(comb * comb_grad, axis=1, keepdims=True))
    through_disp = disp * (disp_grad - jnp.sum(disp * disp_grad, axis=2, keepdims=True))
    logit_grad = (through_comb + through_disp).astype(jnp.bfloat16)
    grad_x = jnp.einsum("bem,bed->bmd", disp_b, slot_back, preferred_element_type=jnp.float32)
    grad_x = grad_x + jnp.einsum(
        "bem,ed->bmd", logit_grad, router, preferred_element_type=jnp.float32
    )
    router_part = jnp.einsum("bem,bmd->ed", logit_grad, tokens, preferred_element_type=jnp.float32)
    grad_router = lax.psum(router_part, ("dp", "expert"))
    return (grad_x.astype(jnp.bfloat16), grad_router, grad_w_in, grad_w_out)


def solution(mesh):
    return jax.shard_map(
        on_device,
        mesh=mesh,
        in_specs=(
            P(("dp", "expert"), None, None),
            P(("dp", "expert"), None, None),
            P(("dp", "expert"), None, None),
            P(),
            P("dp", None, "expert"),
            P("dp", None, "expert"),
            P("dp", "expert", None),
        ),
        out_specs=(
            P(("dp", "expert"), None, None),
            P(),
            P("dp", None, "expert"),
            P("dp", "expert", None),
        ),
        check_vma=False,
    )
```

profile of v0, /device:TPU:1, one launch (start us, length us, event | category | flops | bytes accessed | tf_op | source)
XLA Modules:
  0.0 475.6 jit_solution(13459673954518031261)
XLA Ops:
  7.2 1.6 fusion.73
  8.9 1.8 convolution_convert_fusion.5
  10.8 24.1 %all_to_all.72 = bf16[2,32,1280]{2,0,1:T(2,128)(2,1)S(1)} all-to-all(bf16[2,32,1280]{2,0,1:T(2,128)(2,1)S(1)} %copy.45), channel_id=1, replica_groups=mesh['dp'=32,'expert'=8] {'dp'}, dimensions={1} | all-to-all | bytes 327680 | tf_op jit(solution)/shard_map/all_to_all | solution.py:32
  35.7 1.7 negate_multiply_fusion
  37.4 2.5 mul.92
  39.9 3.3 reshape.144
  43.2 4.0 fusion.25
  48.1 2.2 fusion.8
  50.4 1.0 copy-done.3
  51.4 1.7 reshape.145
  53.1 1.8 copy.72
  54.9 2.0 reshape.142
  56.9 10.8 %all-gather.3.cloned.1.call-done = bf16[512,1,1280]{2,0,1:T(8,128)(2,1)} async-done(((bf16[64,1,1280]{2,0,1:T(8,128)(2,1)}), bf16[512,1,1280]{2,0,1:T(8,128)(2,1)}) %all-gather.3.cloned.1.call-update) | async-done | bytes 1310736 | tf_op jit(solution)/shard_map/all_gather | solution.py:36
  67.6 3.1 fusion.16
  71.6 2.3 fusion.7
  75.7 27.7 %all_to_all.73 = bf16[2,32,1280]{2,0,1:T(2,128)(2,1)S(1)} all-to-all(bf16[2,32,1280]{2,0,1:T(2,128)(2,1)S(1)} %copy.54), channel_id=1, replica_groups=mesh['dp'=32,'expert'=8] {'dp'}, dimensions={1} | all-to-all | bytes 327680 | tf_op jit(solution)/shard_map/all_to_all | solution.py:31
  104.1 10.2 %reduce-scatter.5.cloned.1.call-done = bf16[64,1,1280]{2,0,1:T(8,128)(2,1)} async-done(((bf16[512,1,1280]{2,0,1:T(8,128)(2,1)}), bf16[64,1,1280]{2,0,1:T(8,128)(2,1)}) %reduce-scatter.5.cloned.1.call-update) | async-done | bytes 163856 | tf_op jit(solution)/shard_map/reduce_scatter | solution.py:51
  114.8 1.6 reduce.3
  117.2 15.3 %all-to-all-start.2 = ((bf16[32,2,1280]{2,1,0:T(2,128)(2,1)}), bf16[32,2,1280]{2,1,0:T(2,128)(2,1)S(1)}, u32[]{:S(2)}, u32[]{:S(2)}) async-start(bf16[32,2,1280]{2,1,0:T(2,128)(2,1)} %reshape.152), calls=%async_computation.4 | async-start | bytes 327680 | tf_op jit(solution)/shard_map/all_to_all | solution.py:68
  132.5 3.8 fusion.6
  136.3 24.6 %reduce-scatter.3.cloned.1.call-done = bf16[64,1,1280]{2,0,1:T(8,128)(2,1)} async-done(((bf16[512,1,1280]{2,0,1:T(8,128)(2,1)}), bf16[64,1,1280]{2,0,1:T(8,128)(2,1)}) %reduce-scatter.3.cloned.1.call-update) | async-done | bytes 163856 | tf_op jit(solution)/shard_map/reduce_scatter | solution.py:59
  160.9 1.6 reduce.2
  163.3 13.5 %all-to-all-start.1 = ((bf16[32,2,1280]{2,1,0:T(2,128)(2,1)}), bf16[32,2,1280]{2,1,0:T(2,128)(2,1)}, u32[]{:S(2)}, u32[]{:S(2)}) async-start(bf16[32,2,1280]{2,1,0:T(2,128)(2,1)} %reshape.150), calls=%async_computation.2 | async-start | bytes 327680 | tf_op jit(solution)/shard_map/all_to_all | solution.py:69
  176.8 28.6 %all-gather.5.cloned.1.call-done = bf16[512,1,1280]{2,0,1:T(8,128)(2,1)} async-done(((bf16[64,1,1280]{2,0,1:T(8,128)(2,1)}), bf16[512,1,1280]{2,0,1:T(8,128)(2,1)}) %all-gather.5.cloned.1.call-update) | async-done | bytes 1310736 | tf_op jit(solution)/shard_map/all_gather | solution.py:35
  205.4 3.9 fusion.5
  210.4 2.4 fusion.54
  212.8 1.4 reshape.151
  216.5 1.0 convolution_bitcast_fusion
  217.5 2.1 fusion.53
  219.6 3.4 fusion.4
  223.0 244.4 %all-reduce.2.cloned.1.call-done = f32[32,1280]{1,0:T(8,128)} async-done(((f32[32,1280]{1,0:T(8,128)}), f32[32,1280]{1,0:T(8,128)}) %all-reduce.2.cloned.1.call-update) | async-done | bytes 163856 | tf_op jit(solution)/shard_map/psum | solution.py:81
  467.4 1.6 copy.78
  (53 shorter events, 10.6 us)
Async XLA Ops:
  7.2 40.9 %copy-start = (bf16[1,640,1280]{2,1,0:T(8,128)(2,1)S(1)}, bf16[1,640,1280]{2,1,0:T(8,128)(2,1)}, u32[]{:S(2)}) copy-start(bf16[1,640,1280]{2,1,0:T(8,128)(2,1)} %param.13) | copy-start | bytes 4915204
  7.2 60.5 %all-gather.3.cloned.1.call-start = ((), (), s32[]{:S(2)}) async-start(), calls=%async_computation.6 | async-start | bytes 1474560 | tf_op jit(solution)/shard_map/all_gather | solution.py:36
  8.9 26.8 %copy-start.2 = (bf16[1,512,640]{2,1,0:T(8,128)(2,1)S(1)}, bf16[1,512,640]{2,1,0:T(8,128)(2,1)}, u32[]{:S(2)}) copy-start(bf16[1,512,640]{2,1,0:T(8,128)(2,1)} %param.11) | copy-start | bytes 1966084
  35.6 78.7 %reduce-scatter.5.cloned.1.call-start = ((), (), s32[]{:S(2)}) async-start(), calls=%async_computation.8 | async-start | bytes 1474560 | tf_op jit(solution)/shard_map/reduce_scatter | solution.py:51
  48.1 2.3 copy-start.4
  50.3 1.1 copy-start.3
  50.4 110.5 %reduce-scatter.3.cloned.1.call-start = ((), (), s32[]{:S(2)}) async-start(), calls=%async_computation.7 | async-start | bytes 1474560 | tf_op jit(solution)/shard_map/reduce_scatter | solution.py:59
  56.9 14.7 %copy-start.10 = (bf16[1,1280,640]{2,1,0:T(8,128)(2,1)S(1)}, bf16[1,1280,640]{2,1,0:T(8,128)(2,1)}, u32[]{:S(2)}) copy-start(bf16[1,1280,640]{2,1,0:T(8,128)(2,1)} %param.12) | copy-start | bytes 4915204
  70.7 0.8 copy-start.11
  71.6 2.4 copy-start.5
  73.9 1.3 copy-start.1
  73.9 131.5 %all-gather.5.cloned.1.call-start = ((), (), s32[]{:S(2)}) async-start(), calls=%async_computation.10 | async-start | bytes 1474560 | tf_op jit(solution)/shard_map/all_gather | solution.py:35
  117.2 46.1 %all-to-all-start.2 = ((bf16[32,2,1280]{2,1,0:T(2,128)(2,1)}), bf16[32,2,1280]{2,1,0:T(2,128)(2,1)S(1)}, u32[]{:S(2)}, u32[]{:S(2)}) async-start(bf16[32,2,1280]{2,1,0:T(2,128)(2,1)} %reshape.152), calls=%async_computation.4 | async-start | bytes 327680 | tf_op jit(solution)/shard_map/all_to_all | solution.py:68
  163.3 49.6 %all-to-all-start.1 = ((bf16[32,2,1280]{2,1,0:T(2,128)(2,1)}), bf16[32,2,1280]{2,1,0:T(2,128)(2,1)}, u32[]{:S(2)}, u32[]{:S(2)}) async-start(bf16[32,2,1280]{2,1,0:T(2,128)(2,1)} %reshape.150), calls=%async_computation.2 | async-start | bytes 327680 | tf_op jit(solution)/shard_map/all_to_all | solution.py:69
  176.7 290.7 %all-reduce.2.cloned.1.call-start = ((), (), s32[]{:S(2)}) async-start(), calls=%async_computation.9 | async-start | bytes 327680 | tf_op jit(solution)/shard_map/psum | solution.py:81
  215.2 1.2 copy-start.6
  215.3 0.8 copy-start.9
  215.3 1.2 copy-start.7
  215.8 1.7 copy-start.8
Sparse Core Ops, SparseCore 0:
  35.8 31.8 all-gather.2
  70.8 43.5 reduce-scatter.4
  117.5 43.3 reduce-scatter.2
  162.5 42.7 all-gather.4
  219.7 247.6 all-reduce.1
where the time goes:
time: 476 us
  waiting for transfers between devices  319 us (67%)
  blocking collectives  51.7 us (11%)
  starting transfers between devices  29 us (6%)
  matrix products  26.8 us (6%)
  local copies, waits for them, and re-layouts  22 us (5%)
  between operations  14 us (3%)
  other arithmetic  13.4 us (3%)
    psum x1, waiting for transfers between devices, on_device(): grad_router = lax.psum(router_part, ('dp', 'expert'))  244 us
    all_gather x1, waiting for transfers between devices, on_device(): lax.all_gather(moved_in, 'expert', axis=0, tiled=True)  28.6 us
    all_to_all x1, blocking collectives, on_device(): lax.all_to_all(slot_in, 'dp', split_axis=1, concat_axis=0, tiled=True)  27.7 us
    reduce_scatter x1, waiting for transfers between devices, on_device(): lax.psum_scatter(jnp.einsum('erf,edf->red', hid_grad, w_in, preferred_ele...  24.6 us
    all_to_all x1, blocking collectives, on_device(): lax.all_to_all(slot_grad, 'dp', split_axis=1, concat_axis=0, tiled=True)  24.1 us
    all_to_all x1, starting transfers between devices, on_device(): lax.all_to_all(out_sum, 'dp', split_axis=0, concat_axis=1, tiled=True)  15.3 us
    all_to_all x1, starting transfers between devices, on_device(): lax.all_to_all(back_sum, 'dp', split_axis=0, concat_axis=1, tiled=True)  13.5 us
    all_gather x1, waiting for transfers between devices, on_device(): lax.all_gather(moved_grad, 'expert', axis=0, tiled=True)  10.8 us
  transfers between devices with their start and end apart: 7, of which 5 were waited for; matrix products, arithmetic and copies ran while one was open for 10% of the time, Pallas kernels for 0%

commit v1 on v0

v1 whole, which is shorter than its diff:
```python
import jax
import jax.numpy as jnp
from jax import lax
from jax.sharding import PartitionSpec as P

BF = jnp.bfloat16
F32 = jnp.float32


def gelu_slope(value):
    cdf = 0.5 * (1.0 + jax.scipy.special.erf(value * 0.7071067811865476))
    density = jnp.exp(-0.5 * value * value) * 0.3989422804014327
    return cdf + value * density


def dot(a, b, dims):
    return lax.dot_general(a, b, (dims, ((), ())), preferred_element_type=F32)


def exchange(blocks, axis):
    return lax.all_to_all(blocks, axis, split_axis=0, concat_axis=0, tiled=True)


def side_by_side(parts):
    return jnp.concatenate(parts, axis=1)


def on_device(tokens, grad_out, logits, router, fc1_out, w_in, w_out):
    images, slots, _ = logits.shape
    width = tokens.shape[2]
    dp_count = lax.axis_size("dp")
    ex_count = lax.axis_size("expert")
    group = dp_count * ex_count
    w_in, w_out, pre = w_in[0], w_out[0], fc1_out[0]

    over_slots = jnp.exp(logits - jnp.max(logits, axis=1, keepdims=True))
    comb = over_slots / jnp.sum(over_slots, axis=1, keepdims=True)
    comb_b = comb.astype(BF)
    over_tokens = jnp.exp(logits - jnp.max(logits, axis=2, keepdims=True))
    disp = over_tokens / jnp.sum(over_tokens, axis=2, keepdims=True)
    disp_b = disp.astype(BF)

    slot_grad = side_by_side([dot(comb_b[b], grad_out[b], ((1,), (0,))).astype(BF) for b in range(images)])
    slot_in = side_by_side([dot(disp_b[b], tokens[b], ((1,), (0,))).astype(BF) for b in range(images)])

    hidden = pre.shape[1]
    pre = pre.reshape(dp_count, ex_count, images, hidden).transpose(2, 1, 0, 3).reshape(-1, hidden)
    pre_f = pre.astype(F32)
    act = jax.nn.gelu(pre_f, approximate=False).astype(BF)
    slope = gelu_slope(pre_f)

    def by_image(rows):
        return jnp.concatenate([rows[:, b * width : (b + 1) * width] for b in range(images)], axis=0)

    def by_lane(rows):
        return side_by_side([rows[b * group : (b + 1) * group] for b in range(images)])

    moved_grad = exchange(slot_grad, "dp")
    all_grad = exchange(jnp.broadcast_to(moved_grad[None], (ex_count,) + moved_grad.shape), "expert")
    all_grad = by_image(all_grad.reshape(group, -1))

    out_part = by_lane(dot(act, w_out, ((1,), (0,))).astype(BF))
    out_sum = lax.psum_scatter(out_part, "expert", scatter_dimension=0, tiled=True)

    act_grad = dot(all_grad, w_out, ((1,), (1,)))
    hid_grad = (act_grad * slope).astype(BF)
    back_part = by_lane(dot(hid_grad, w_in, ((1,), (1,))).astype(BF))
    back_parts = exchange(back_part.reshape(ex_count, dp_count, -1), "expert")
    back_sum = jnp.sum(back_parts.astype(F32), axis=0).astype(BF)

    moved_in = exchange(slot_in, "dp")
    all_in = by_image(lax.all_gather(moved_in, "expert", axis=0, tiled=True))
    grad_w_out = dot(act, all_grad, ((0,), (0,))).astype(BF)
    grad_w_in = dot(all_in, hid_grad, ((0,), (0,))).astype(BF)

    slot_out = exchange(out_sum, "dp")
    slot_back = exchange(back_sum, "dp")

    grads, router_part = [], 0.0
    for b in range(images):
        lanes = slice(b * width, (b + 1) * width)
        comb_grad = dot(slot_out[:, lanes], grad_out[b], ((1,), (1,)))
        disp_grad = dot(slot_back[:, lanes], tokens[b], ((1,), (1,)))
        through_comb = comb[b] * (comb_grad - jnp.sum(comb[b] * comb_grad, axis=0, keepdims=True))
        through_disp = disp[b] * (disp_grad - jnp.sum(disp[b] * disp_grad, axis=1, keepdims=True))
        logit_grad = (through_comb + through_disp).astype(BF)
        left = jnp.concatenate([disp_b[b], logit_grad], axis=0)
        right = jnp.concatenate([slot_back[:, lanes], router], axis=0)
        grads.append(dot(left, right, ((0,), (0,))).astype(BF))
        router_part = router_part + dot(logit_grad, tokens[b], ((1,), (0,)))
    grad_x = jnp.stack(grads)

    row = jnp.sum(exchange(router_part, "dp"), axis=0, keepdims=True)
    rows = exchange(jnp.broadcast_to(row[None], (ex_count, 1, width)), "expert")
    row = jnp.sum(rows, axis=0, keepdims=True)
    grad_router = exchange(jnp.broadcast_to(row, (dp_count, 1, width)), "dp").reshape(slots, width)
    return grad_x, grad_router, grad_w_in[None], grad_w_out[None]


def solution(mesh):
    return jax.shard_map(
        on_device,
        mesh=mesh,
        in_specs=(
            P(("dp", "expert"), None, None),
            P(("dp", "expert"), None, None),
            P(("dp", "expert"), None, None),
            P(),
            P("dp", None, "expert"),
            P("dp", None, "expert"),
            P("dp", "expert", None),
        ),
        out_specs=(
            P(("dp", "expert"), None, None),
            P(),
            P("dp", None, "expert"),
            P("dp", "expert", None),
        ),
        check_vma=False,
    )
```

time: 476 us -> 218 us (0.46)
  waiting for transfers between devices: 319 us -> 67.5 us
  blocking collectives: 51.7 us -> 0 us
  starting transfers between devices: 29 us -> 64.9 us
  other arithmetic: 13.4 us -> 23.2 us
  matrix products: 26.8 us -> 18.6 us
  local copies, waits for them, and re-layouts: 22 us -> 27.7 us
    psum x1 -> x0, waiting for transfers between devices: 244 us -> none  [on_device(): grad_router = lax.psum(router_part, ('dp', 'expert'))]
    all_to_all x2 -> x9, waiting for transfers between devices: 0.01 us -> 56.8 us  [exchange(): return lax.all_to_all(blocks, axis, split_axis=0, concat_axis=0, tiled=True)]
    all_to_all x2 -> x0, blocking collectives: 51.7 us -> none  [the longest x1 27.7 us: on_device(): lax.all_to_all(slot_in, 'dp', split_axis=1, concat_axis=0, tiled=True)]
    all_gather x2 -> x1, waiting for transfers between devices: 39.4 us -> 0.02 us  [on_device(): all_in = by_image(lax.all_gather(moved_in, 'expert', axis=0, tiled=True))]
    all_to_all x2 -> x9, starting transfers between devices: 28.8 us -> 64.9 us  [exchange(): return lax.all_to_all(blocks, axis, split_axis=0, concat_axis=0, tiled=True)]
    reduce_scatter x2 -> x1, waiting for transfers between devices: 34.8 us -> 10.6 us  [on_device(): lax.psum_scatter(out_part, 'expert', scatter_dimension=0, tiled=True)]
    dot_general x12 -> x17, matrix products: 26.8 us -> 18.6 us  [dot(): return lax.dot_general(a, b, (dims, ((), ())), preferred_element_type=F32)]
    convert_element_type x1 -> x5, other arithmetic: 4.02 us -> 9.87 us  [the longest x2 9.05 us: on_device(): act = jax.nn.gelu(pre_f, approximate=False).astype(BF)]
  transfers between devices with their start and end apart: 7 -> 11, of which waited for: 5 -> 8; matrix products, arithmetic and copies ran while one was open for 10% -> 26% of each run, Pallas kernels for 0% -> 0%
where the time goes in v1:
time: 218 us; the launch traced here: 216 us
  waiting for transfers between devices  67.5 us (31%)
  starting transfers between devices  64.9 us (30%)
  local copies, waits for them, and re-layouts  27.7 us (13%)
  other arithmetic  23.2 us (11%)
  matrix products  18.6 us (9%)
  between operations  14.6 us (7%)
    all_to_all x9, starting transfers between devices, exchange(): return lax.all_to_all(blocks, axis, split_axis=0, concat_axis=0, tiled=True)  64.9 us
    all_to_all x9, waiting for transfers between devices, exchange(): return lax.all_to_all(blocks, axis, split_axis=0, concat_axis=0, tiled=True)  56.8 us
    dot_general x17, matrix products, dot(): return lax.dot_general(a, b, (dims, ((), ())), preferred_element_type=F32)  18.6 us
    reduce_scatter x1, waiting for transfers between devices, on_device(): lax.psum_scatter(out_part, 'expert', scatter_dimension=0, tiled=True)  10.6 us
    convert_element_type x2, other arithmetic, on_device(): act = jax.nn.gelu(pre_f, approximate=False).astype(BF)  9.05 us
    unnamed x60, local copies, waits for them, and re-layouts  8.66 us
    mul x2, local copies, waits for them, and re-layouts, on_device(): act = jax.nn.gelu(pre_f, approximate=False).astype(BF)  5 us
    convert_element_type x2, local copies, waits for them, and re-layouts, on_device(): pre_f = pre.astype(F32)  4.61 us
  transfers between devices with their start and end apart: 11, of which 8 were waited for; matrix products, arithmetic and copies ran while one was open for 26% of the time, Pallas kernels for 0%

profile of v1, /device:TPU:1, one launch (start us, length us, event | category | flops | bytes accessed | tf_op | source)
XLA Modules:
  0.0 216.5 jit_solution(12504510783441297337)
XLA Ops:
  13.6 12.8 %all-to-all-start.1 = ((bf16[32,2,1280]{2,1,0:T(2,128)(2,1)}), bf16[32,2,1280]{2,1,0:T(2,128)(2,1)S(1)}, u32[]{:S(2)}, u32[]{:S(2)}) async-start(bf16[32,2,1280]{2,1,0:T(2,128)(2,1)} %reshape.63), calls=%async_computation.2 | async-start | bytes 327680 | tf_op jit(solution)/shard_map/all_to_all | solution.py:21
  26.4 1.7 negate_multiply_fusion
  28.0 2.1 mul.79
  30.1 2.9 %reshape.59 = f32[32,8,2,640]{3,2,1,0:T(2,128)} reshape(f32[1,512,640]{2,1,0:T(8,128)} %get-tuple-element.22) | data formatting | bytes 2621440 | tf_op jit(solution)/shard_map/mul | solution.py:49
  33.0 4.0 %fusion.19 = bf16[2,8,32,640]{3,2,1,0:T(8,128)(2,1)S(1)} fusion(f32[32,8,2,640]{3,2,1,0:T(2,128)S(1)} %mul.79, f32[32,8,2,640]{3,2,1,0:T(2,128)} %reshape.59), kind=kLoop, calls=%fused_computation.29 | loop fusion | flops 20316160 | bytes 3276800 | tf_op jit(solution)/shard_map/convert_element_type | solution.py:49
  39.7 4.5 %all-to-all-start.2 = ((bf16[8,32,2560]{2,1,0:T(8,128)(2,1)}), bf16[8,32,2560]{2,1,0:T(8,128)(2,1)}, u32[]{:S(2)}, u32[]{:S(2)}) async-start(bf16[8,32,2560]{2,1,0:T(8,128)(2,1)} %broadcast_in_dim.13), calls=%async_computation.3 | async-start | bytes 2621440 | tf_op jit(solution)/shard_map/all_to_all | solution.py:21
  46.5 1.7 reshape.61
  48.2 2.9 %copy.50 = f32[32,8,2,640]{3,0,1,2:T(8,128)} copy(f32[32,8,2,640]{3,2,1,0:T(2,128)} %reshape.61) | data formatting | bytes 2621440 | tf_op jit(solution)/shard_map/convert_element_type | solution.py:48
  53.5 5.0 %fusion.26 = (bf16[512,640]{1,0:T(8,128)(2,1)}, f32[512,640]{1,0:T(8,128)}) fusion(f32[32,8,2,640]{3,0,1,2:T(8,128)} %copy.50), kind=kLoop, calls=%fused_computation.36 | loop fusion | flops 22282240 | bytes 3276800 | tf_op jit(solution)/shard_map/convert_element_type | solution.py:49
  58.5 3.6 %all-to-all-done.2 = bf16[8,32,2560]{2,1,0:T(8,128)(2,1)} async-done(((bf16[8,32,2560]{2,1,0:T(8,128)(2,1)}), bf16[8,32,2560]{2,1,0:T(8,128)(2,1)}, u32[]{:S(2)}, u32[]{:S(2)}) %all-to-all-start.2) | async-done | bytes 1310752 | tf_op jit(solution)/shard_map/all_to_all | solution.py:21
  62.1 10.2 %all-to-all-start.8 = ((bf16[32,2,1280]{2,1,0:T(2,128)(2,1)}), bf16[32,2,1280]{2,1,0:T(2,128)(2,1)S(1)}, u32[]{:S(2)}, u32[]{:S(2)}) async-start(bf16[32,2,1280]{2,1,0:T(2,128)(2,1)} %reshape.69), calls=%async_computation.9 | async-start | bytes 327680 | tf_op jit(solution)/shard_map/all_to_all | solution.py:21
  72.3 1.5 fusion.109
  78.3 10.6 %reduce-scatter.2.cloned.1.call-done = bf16[32,2560]{1,0:T(8,128)(2,1)} async-done(((bf16[256,2560]{1,0:T(8,128)(2,1)}), bf16[32,2560]{1,0:T(8,128)(2,1)}) %reduce-scatter.2.cloned.1.call-update) | async-done | bytes 163856 | tf_op jit(solution)/shard_map/reduce_scatter | solution.py:63
  88.9 1.6 reduce.5
  91.2 14.7 %all-to-all-start = ((bf16[32,2,1280]{2,1,0:T(2,128)(2,1)}), bf16[32,2,1280]{2,1,0:T(2,128)(2,1)S(1)}, u32[]{:S(2)}, u32[]{:S(2)}) async-start(bf16[32,2,1280]{2,1,0:T(2,128)(2,1)} %reshape.67), calls=%async_computation.1 | async-start | bytes 327680 | tf_op jit(solution)/shard_map/all_to_all | solution.py:21
  106.0 2.4 %pad_maximum_fusion.2 = bf16[256,2560]{1,0:T(8,128)(2,1)} fusion(bf16[256,1280]{1,0:T(8,128)(2,1)} %get-tuple-element.19, bf16[256,1280]{1,0:T(8,128)(2,1)} %get-tuple-element.18), kind=kLoop, calls=%fused_computation.39 | loop fusion | flops 2621440 | bytes 2621440 | tf_op jit(solution)/shard_map/concatenate | solution.py:25
  108.4 8.9 %all-to-all-done = bf16[32,2,1280]{2,1,0:T(2,128)(2,1)S(1)} async-done(((bf16[32,2,1280]{2,1,0:T(2,128)(2,1)}), bf16[32,2,1280]{2,1,0:T(2,128)(2,1)S(1)}, u32[]{:S(2)}, u32[]{:S(2)}) %all-to-all-start) | async-done | bytes 163872 | tf_op jit(solution)/shard_map/all_to_all | solution.py:21
  118.0 4.3 %all-to-all-start.3 = ((bf16[8,32,2560]{2,1,0:T(8,128)(2,1)}), bf16[8,32,2560]{2,1,0:T(8,128)(2,1)}, u32[]{:S(2)}, u32[]{:S(2)}) async-start(bf16[8,32,2560]{2,1,0:T(8,128)(2,1)} %bitcast.222), calls=%async_computation.4 | async-start | bytes 2621440 | tf_op jit(solution)/shard_map/all_to_all | solution.py:21
  123.8 1.4 reshape.68
  125.9 16.4 %all-to-all-done.3 = bf16[8,32,2560]{2,1,0:T(8,128)(2,1)} async-done(((bf16[8,32,2560]{2,1,0:T(8,128)(2,1)}), bf16[8,32,2560]{2,1,0:T(8,128)(2,1)}, u32[]{:S(2)}, u32[]{:S(2)}) %all-to-all-start.3) | async-done | bytes 1310752 | tf_op jit(solution)/shard_map/all_to_all | solution.py:21
  142.3 1.5 reduce_sum.87
  145.3 4.7 %all-to-all-start.4 = ((bf16[32,2,1280]{2,1,0:T(2,128)(2,1)}), bf16[32,2,1280]{2,1,0:T(2,128)(2,1)S(1)}, u32[]{:S(2)}, u32[]{:S(2)}) async-start(bf16[32,2,1280]{2,1,0:T(2,128)(2,1)} %reshape.65), calls=%async_computation.5 | async-start | bytes 327680 | tf_op jit(solution)/shard_map/all_to_all | solution.py:21
  151.5 2.7 %multiply_reduce_fusion.3 = (f32[256]{0:T(256)}, f32[256]{0:T(256)}, f32[32,256]{1,0:T(8,128)}) fusion(f32[2,32,256]{2,1,0:T(8,128)} %get-tuple-element.11, f32[32,256]{1,0:T(8,128)S(1)} %fusion.71, bf16[2,256,1280]{2,1,0:T(8,128)(2,1)} %param.8, bf16[32,2560]{1,0:T(8,128)(2,1)S(1)} %bitcast.231), kind=kOutput, calls=%fused_computation.143 | convolution fusion | flops 21003776 | bytes 870400 | tf_op jit(solution)/shard_map/dot_general | solution.py:17
  154.2 9.0 %all-to-all-done.4 = bf16[32,2,1280]{2,1,0:T(2,128)(2,1)S(1)} async-done(((bf16[32,2,1280]{2,1,0:T(2,128)(2,1)}), bf16[32,2,1280]{2,1,0:T(2,128)(2,1)S(1)}, u32[]{:S(2)}, u32[]{:S(2)}) %all-to-all-start.4) | async-done | bytes 163872 | tf_op jit(solution)/shard_map/all_to_all | solution.py:21
  165.6 4.4 %all-to-all-start.5 = ((f32[32,1,1280]{2,1,0:T(1,128)}), f32[32,1,1280]{2,1,0:T(1,128)S(1)}, u32[]{:S(2)}, u32[]{:S(2)}) async-start(f32[32,1,1280]{2,1,0:T(1,128)} %copy.52), calls=%async_computation.6 | async-start | bytes 327680 | tf_op jit(solution)/shard_map/all_to_all | solution.py:21
  171.5 2.4 %fusion.2 = bf16[1,1280,640]{2,1,0:T(8,128)(2,1)} fusion(bf16[512,640]{1,0:T(8,128)(2,1)S(1)} %copy-done.23, bf16[256,1280]{1,0:T(8,128)(2,1)S(1)} %get-tuple-element.15, bf16[256,1280]{1,0:T(8,128)(2,1)S(1)} %get-tuple-element.14), kind=kOutput, calls=%fused_computation.6 | convolution fusion | flops 842301440 | bytes 3604480 | tf_op jit(solution)/shard_map/dot_general | solution.py:17
  173.9 7.6 %all-to-all-done.5 = f32[32,1,1280]{2,1,0:T(1,128)S(1)} async-done(((f32[32,1,1280]{2,1,0:T(1,128)}), f32[32,1,1280]{2,1,0:T(1,128)S(1)}, u32[]{:S(2)}, u32[]{:S(2)}) %all-to-all-start.5) | async-done | bytes 163872 | tf_op jit(solution)/shard_map/all_to_all | solution.py:21
  182.3 4.5 %all-to-all-start.6 = ((f32[8,1,1280]{2,1,0:T(1,128)}), f32[8,1,1280]{2,1,0:T(1,128)S(1)}, u32[]{:S(2)}, u32[]{:S(2)}) async-start(f32[8,1,1280]{2,1,0:T(1,128)} %broadcast_in_dim.14), calls=%async_computation.7 | async-start | bytes 81920 | tf_op jit(solution)/shard_map/all_to_all | solution.py:21
  186.8 3.3 %fusion.3 = bf16[1,640,1280]{2,1,0:T(8,128)(2,1)} fusion(bf16[512,640]{1,0:T(8,128)(2,1)} %get-tuple-element.12, bf16[256,1280]{1,0:T(8,128)(2,1)S(1)} %copy-done.9, bf16[256,1280]{1,0:T(8,128)(2,1)S(1)} %copy-done.7), kind=kOutput, calls=%fused_computation.7 | convolution fusion | flops 842301440 | bytes 3604480 | tf_op jit(solution)/shard_map/dot_general | solution.py:17
  190.2 1.8 all-to-all-done.6
  192.8 4.9 %all-to-all-start.7 = ((f32[32,1,1280]{2,1,0:T(1,128)}), f32[32,1,1280]{2,1,0:T(1,128)S(1)}, u32[]{:S(2)}, u32[]{:S(2)}) async-start(f32[32,1,1280]{2,1,0:T(1,128)} %broadcast_in_dim.15), calls=%async_computation.8 | async-start | bytes 327680 | tf_op jit(solution)/shard_map/all_to_all | solution.py:21
  199.6 9.4 %all-to-all-done.7 = f32[32,1,1280]{2,1,0:T(1,128)S(1)} async-done(((f32[32,1,1280]{2,1,0:T(1,128)}), f32[32,1,1280]{2,1,0:T(1,128)S(1)}, u32[]{:S(2)}, u32[]{:S(2)}) %all-to-all-start.7) | async-done | bytes 163872 | tf_op jit(solution)/shard_map/all_to_all | solution.py:21
  (105 shorter events, 32.4 us)
Async XLA Ops:
  7.2 29.9 %copy-start = (bf16[1,640,1280]{2,1,0:T(8,128)(2,1)S(1)}, bf16[1,640,1280]{2,1,0:T(8,128)(2,1)}, u32[]{:S(2)}) copy-start(bf16[1,640,1280]{2,1,0:T(8,128)(2,1)} %param.13) | copy-start | bytes 4915204
  8.9 17.5 %copy-start.3 = (bf16[1,512,640]{2,1,0:T(8,128)(2,1)S(1)}, bf16[1,512,640]{2,1,0:T(8,128)(2,1)}, u32[]{:S(2)}) copy-start(bf16[1,512,640]{2,1,0:T(8,128)(2,1)} %param.11) | copy-start | bytes 1966084
  13.6 24.8 %all-to-all-start.1 = ((bf16[32,2,1280]{2,1,0:T(2,128)(2,1)}), bf16[32,2,1280]{2,1,0:T(2,128)(2,1)S(1)}, u32[]{:S(2)}, u32[]{:S(2)}) async-start(bf16[32,2,1280]{2,1,0:T(2,128)(2,1)} %reshape.63), calls=%async_computation.2 | async-start | bytes 327680 | tf_op jit(solution)/shard_map/all_to_all | solution.py:21
  39.7 22.4 %all-to-all-start.2 = ((bf16[8,32,2560]{2,1,0:T(8,128)(2,1)}), bf16[8,32,2560]{2,1,0:T(8,128)(2,1)}, u32[]{:S(2)}, u32[]{:S(2)}) async-start(bf16[8,32,2560]{2,1,0:T(8,128)(2,1)} %broadcast_in_dim.13), calls=%async_computation.3 | async-start | bytes 2621440 | tf_op jit(solution)/shard_map/all_to_all | solution.py:21
  44.2 44.7 %reduce-scatter.2.cloned.1.call-start = ((), (), s32[]{:S(2)}) async-start(), calls=%async_computation.10 | async-start | bytes 1474560 | tf_op jit(solution)/shard_map/reduce_scatter | solution.py:63
  45.4 1.1 copy-start.4
  48.2 2.9 %copy-start.14 = (f32[2,32,256]{2,1,0:T(8,128)S(1)}, f32[2,32,256]{2,1,0:T(8,128)}, u32[]{:S(2)}) copy-start(f32[2,32,256]{2,1,0:T(8,128)} %param.9) | copy-start | bytes 196612
  48.2 3.3 %copy-start.1 = (bf16[2,256,1280]{2,1,0:T(8,128)(2,1)S(1)}, bf16[2,256,1280]{2,1,0:T(8,128)(2,1)}, u32[]{:S(2)}) copy-start(bf16[2,256,1280]{2,1,0:T(8,128)(2,1)} %param.7) | copy-start | bytes 3932164
  62.1 29.2 %all-to-all-start.8 = ((bf16[32,2,1280]{2,1,0:T(2,128)(2,1)}), bf16[32,2,1280]{2,1,0:T(2,128)(2,1)S(1)}, u32[]{:S(2)}, u32[]{:S(2)}) async-start(bf16[32,2,1280]{2,1,0:T(2,128)(2,1)} %reshape.69), calls=%async_computation.9 | async-start | bytes 327680 | tf_op jit(solution)/shard_map/all_to_all | solution.py:21
  72.3 1.7 copy-start.2
  72.3 2.1 copy-start.5
  73.9 1.9 copy-start.6
  73.9 1.9 copy-start.8
  74.4 1.5 copy-start.21
  75.9 1.2 copy-start.22
  91.2 26.1 %all-to-all-start = ((bf16[32,2,1280]{2,1,0:T(2,128)(2,1)}), bf16[32,2,1280]{2,1,0:T(2,128)(2,1)S(1)}, u32[]{:S(2)}, u32[]{:S(2)}) async-start(bf16[32,2,1280]{2,1,0:T(2,128)(2,1)} %reshape.67), calls=%async_computation.1 | async-start | bytes 327680 | tf_op jit(solution)/shard_map/all_to_all | solution.py:21
  118.0 24.4 %all-to-all-start.3 = ((bf16[8,32,2560]{2,1,0:T(8,128)(2,1)}), bf16[8,32,2560]{2,1,0:T(8,128)(2,1)}, u32[]{:S(2)}, u32[]{:S(2)}) async-start(bf16[8,32,2560]{2,1,0:T(8,128)(2,1)} %bitcast.222), calls=%async_computation.4 | async-start | bytes 2621440 | tf_op jit(solution)/shard_map/all_to_all | solution.py:21
  122.3 47.8 %all-gather.3.cloned.1.call-start = ((), (), s32[]{:S(2)}) async-start(), calls=%async_computation.11 | async-start | bytes 1474560 | tf_op jit(solution)/shard_map/all_gather | solution.py:72
  144.6 6.8 %copy-start.12 = (bf16[32,1,2560]{2,0,1:T(8,128)(2,1)S(1)}, bf16[32,1,2560]{2,0,1:T(8,128)(2,1)}, u32[]{:S(2)}) copy-start(bf16[32,1,2560]{2,0,1:T(8,128)(2,1)} %copy.70) | copy-start | bytes 491524
  145.3 17.9 %all-to-all-start.4 = ((bf16[32,2,1280]{2,1,0:T(2,128)(2,1)}), bf16[32,2,1280]{2,1,0:T(2,128)(2,1)S(1)}, u32[]{:S(2)}, u32[]{:S(2)}) async-start(bf16[32,2,1280]{2,1,0:T(2,128)(2,1)} %reshape.65), calls=%async_computation.5 | async-start | bytes 327680 | tf_op jit(solution)/shard_map/all_to_all | solution.py:21
  151.4 2.7 %copy-start.15 = (f32[32,256]{1,0:T(8,128)}, f32[32,256]{1,0:T(8,128)S(1)}, u32[]{:S(2)}) copy-start(f32[32,256]{1,0:T(8,128)S(1)} %fusion.71) | copy-start | bytes 98308
  163.3 0.9 copy-start.11
  163.3 0.9 copy-start.16
  163.3 0.9 copy-start.17
  165.6 15.9 %all-to-all-start.5 = ((f32[32,1,1280]{2,1,0:T(1,128)}), f32[32,1,1280]{2,1,0:T(1,128)S(1)}, u32[]{:S(2)}, u32[]{:S(2)}) async-start(f32[32,1,1280]{2,1,0:T(1,128)} %copy.52), calls=%async_computation.6 | async-start | bytes 327680 | tf_op jit(solution)/shard_map/all_to_all | solution.py:21
  170.0 1.5 copy-start.23
  171.5 15.3 %copy-start.7 = (bf16[256,1280]{1,0:T(8,128)(2,1)S(1)}, bf16[256,1280]{1,0:T(8,128)(2,1)}, u32[]{:S(2)}) copy-start(bf16[256,1280]{1,0:T(8,128)(2,1)} %copy-done.6) | copy-start | bytes 1966084
  171.5 15.3 %copy-start.9 = (bf16[256,1280]{1,0:T(8,128)(2,1)S(1)}, bf16[256,1280]{1,0:T(8,128)(2,1)}, u32[]{:S(2)}) copy-start(bf16[256,1280]{1,0:T(8,128)(2,1)} %copy-done.8) | copy-start | bytes 1966084
  182.3 9.7 %all-to-all-start.6 = ((f32[8,1,1280]{2,1,0:T(1,128)}), f32[8,1,1280]{2,1,0:T(1,128)S(1)}, u32[]{:S(2)}, u32[]{:S(2)}) async-start(f32[8,1,1280]{2,1,0:T(1,128)} %broadcast_in_dim.14), calls=%async_computation.7 | async-start | bytes 81920 | tf_op jit(solution)/shard_map/all_to_all | solution.py:21
  186.8 10.9 %copy-start.13 = (bf16[32,1280]{1,0:T(8,128)(2,1)S(1)}, bf16[32,1280]{1,0:T(8,128)(2,1)}, u32[]{:S(2)}) copy-start(bf16[32,1280]{1,0:T(8,128)(2,1)} %param.10) | copy-start | bytes 245764
  186.8 10.9 %copy-start.18 = (bf16[32,256]{1,0:T(8,128)(2,1)S(1)}, bf16[32,256]{1,0:T(8,128)(2,1)}, u32[]{:S(2)}) copy-start(bf16[32,256]{1,0:T(8,128)(2,1)} %get-tuple-element.28) | copy-start | bytes 49156
  192.8 16.2 %all-to-all-start.7 = ((f32[32,1,1280]{2,1,0:T(1,128)}), f32[32,1,1280]{2,1,0:T(1,128)S(1)}, u32[]{:S(2)}, u32[]{:S(2)}) async-start(f32[32,1,1280]{2,1,0:T(1,128)} %broadcast_in_dim.15), calls=%async_computation.8 | async-start | bytes 327680 | tf_op jit(solution)/shard_map/all_to_all | solution.py:21
  (3 other events, 2.4 us)
Sparse Core Ops, SparseCore 0:
  47.6 41.2 reduce-scatter.1
  125.5 36.5 all-gather.2

commit v2 on v1

v2 whole, which is shorter than its diff:
```python
import functools

import jax
import jax.numpy as jnp
from jax import lax
from jax.experimental import pallas as pl
from jax.experimental.pallas import tpu as pltpu
from jax.sharding import PartitionSpec as P

BF = jnp.bfloat16
F32 = jnp.float32
MIB = 1024 * 1024
MOST = 60 * MIB


def gelu_slope(value):
    cdf = 0.5 * (1.0 + jax.scipy.special.erf(value * 0.7071067811865476))
    density = jnp.exp(-0.5 * value * value) * 0.3989422804014327
    return cdf + value * density


def dot(a, b, dims):
    return lax.dot_general(a, b, (dims, ((), ())), preferred_element_type=F32)


def softmax(scores, axis):
    over = jnp.exp(scores - jnp.max(scores, axis=axis, keepdims=True))
    return over / jnp.sum(over, axis=axis, keepdims=True)


def exchange(blocks, axis):
    return lax.all_to_all(blocks, axis, split_axis=0, concat_axis=0, tiled=True)


def after(value, *others):
    return lax.optimization_barrier((value,) + others)[0]


def kernel_call(kernel, inputs, outputs, flops=0, moved=0, scratch=(), vmem=16 * MIB):
    place = {
        "v": pl.BlockSpec(memory_space=pltpu.VMEM),
        "h": pl.BlockSpec(memory_space=pltpu.HBM),
        "r": pl.BlockSpec(memory_space=pltpu.HBM),
        "s": pl.BlockSpec(memory_space=pltpu.SMEM),
    }

    def run(*operands):
        n_in, n_out = len(operands), len(outputs)
        fetched = [i for i in range(n_in) if inputs[i] == "h"]
        stored = [i for i in range(n_out) if outputs[i][0] == "h"]
        staged = [pltpu.VMEM(operands[i].shape, operands[i].dtype) for i in fetched]
        staged += [pltpu.VMEM(outputs[i][1].shape, outputs[i][1].dtype) for i in stored]
        sems = [pltpu.SemaphoreType.DMA((len(staged),))] if staged else []

        def body(*refs):
            ins, outs = list(refs[:n_in]), list(refs[n_in : n_in + n_out])
            extra = list(refs[n_in + n_out :])
            buffers = extra[: len(staged)]
            sem = extra[len(staged)] if staged else None
            rest = extra[len(staged) + len(sems) :]
            copies = []
            for j, i in enumerate(fetched):
                copies.append(pltpu.make_async_copy(ins[i], buffers[j], sem.at[j]))
                copies[-1].start()
                ins[i] = buffers[j]
            for copy in copies:
                copy.wait()
            targets = [outs[i] for i in stored]
            for j, i in enumerate(stored):
                outs[i] = buffers[len(fetched) + j]
            kernel(*ins, *outs, *rest)
            copies = []
            for j, target in enumerate(targets):
                at = len(fetched) + j
                copies.append(pltpu.make_async_copy(buffers[at], target, sem.at[at]))
                copies[-1].start()
            for copy in copies:
                copy.wait()

        return pl.pallas_call(
            body,
            out_shape=tuple(o[1] for o in outputs),
            in_specs=[place[flag] for flag in inputs],
            out_specs=tuple(place[o[0]] for o in outputs),
            scratch_shapes=staged + sems + list(scratch),
            compiler_params=pltpu.CompilerParams(vmem_limit_bytes=vmem),
            cost_estimate=pl.CostEstimate(flops=flops, bytes_accessed=moved, transcendentals=0),
        )(*operands)

    return run


def shuffle(slots, pieces, back):
    total = slots * pieces
    row = lax.broadcasted_iota(jnp.int32, (total, total), 1 if back else 0)
    col = lax.broadcasted_iota(jnp.int32, (total, total), 0 if back else 1)
    return ((row % pieces) * slots + row // pieces == col).astype(BF)


def pack(rows, width):
    half = width // 2
    stack = jnp.concatenate([r[:, h * half : (h + 1) * half] for r in rows for h in range(2)], axis=0)
    return dot(shuffle(rows[0].shape[0], 2 * len(rows), False), stack, ((1,), (0,))).astype(BF)


def unpack(packed, slots):
    pieces = packed.shape[0] // slots
    stack = dot(shuffle(slots, pieces, True), packed, ((1,), (0,))).astype(BF)
    part = [stack[p * slots : (p + 1) * slots] for p in range(pieces)]
    return [jnp.concatenate(part[p : p + 2], axis=1) for p in range(0, pieces, 2)]


def fetch(pairs, sems):
    copies = [pltpu.make_async_copy(src, dst, sems.at[i]) for i, (src, dst) in enumerate(pairs)]
    for copy in copies:
        copy.start()
    return copies


def halves(src, dst, b):
    rows = src.shape[1] // 2
    return [(src.at[b, pl.ds(h * rows, rows)], dst.at[b, pl.ds(h * rows, rows)]) for h in range(2)]


def slots_kernel(logits_in, dy_in, tokens_in, out_ref, logits, dy, tokens, sems):
    images = dy.shape[0]
    pairs = [(logits_in, logits)]
    for src, dst in ((dy_in, dy), (tokens_in, tokens)):
        for b in range(images):
            pairs += halves(src, dst, b)
    copies = fetch(pairs, sems)
    copies[0].wait()
    rows = []
    for axis, values in ((0, dy), (1, tokens)):
        for b in range(images):
            at = 1 + 2 * (axis * images + b)
            weights = softmax(logits[b], axis).astype(BF)
            copies[at].wait()
            copies[at + 1].wait()
            rows.append(dot(weights, values[b], ((1,), (0,))).astype(BF))
    out_ref[...] = pack(rows, rows[0].shape[1])


def hidden_kernel(dp_count, ex_count, me_ref, fc1_ref, w_ref, act_ref, *refs):
    slope_refs, out_refs = refs[:2], refs[2:]
    total = fc1_ref.shape[0]
    images = total // (dp_count * ex_count)
    group = dp_count * images
    block = 2 * group
    me = me_ref[0]
    for c in range(total // block):
        at = lax.broadcasted_iota(jnp.int32, (block, total), 0) + c * block
        owner = lax.bitwise_xor(at // group, jnp.full(at.shape, me, jnp.int32))
        source = (at % dp_count) * (ex_count * images) + owner * images + (at // dp_count) % images
        pick = (source == lax.broadcasted_iota(jnp.int32, (block, total), 1)).astype(BF)
        pre = dot(pick, fc1_ref[...], ((1,), (0,)))
        cdf = 0.5 * (1.0 + lax.erf(pre * 0.7071067811865476))
        density = jnp.exp(-0.5 * pre * pre) * 0.3989422804014327
        act = (pre * cdf).astype(BF)
        act_ref[c * block : (c + 1) * block, :] = act
        slope_refs[c // 2][(c % 2) * block : (c % 2 + 1) * block, :] = (cdf + pre * density).astype(BF)
        out = dot(act, w_ref[...], ((1,), (0,))).astype(BF)
        out_refs[2 * c][...] = out[:group]
        out_refs[2 * c + 1][...] = out[group:]


def back_kernel(*refs):
    blocks, (slope_ref, w_out_ref, w_in_ref, hid_ref), outs = refs[:4], refs[4:8], refs[8:]
    group = blocks[0].shape[0]
    for c in range(0, 4, 2):
        rows = slice(c * group, (c + 2) * group)
        grad = jnp.concatenate([blocks[c][...], blocks[c + 1][...]], axis=0)
        hid = (dot(grad, w_out_ref[...], ((1,), (1,))) * slope_ref[rows, :].astype(F32)).astype(BF)
        hid_ref[rows, :] = hid
        back = dot(hid, w_in_ref[...], ((1,), (1,))).astype(BF)
        outs[c][...] = back[:group]
        outs[c + 1][...] = back[group:]


def weight_out_kernel(act_ref, *refs):
    grad = jnp.concatenate([r[...] for r in refs[:-1]], axis=0)
    for c in range(0, act_ref.shape[1], 128):
        cols = slice(c, c + 128)
        refs[-1][cols, :] = dot(act_ref[:, cols], grad, ((0,), (0,))).astype(BF)


def weight_in_kernel(me_ref, all_ref, hid_a_ref, hid_b_ref, out_ref):
    me = me_ref[0]
    group = all_ref.shape[1]
    rows = jnp.concatenate([all_ref[lax.bitwise_xor(me, jnp.int32(k))] for k in range(all_ref.shape[0])], axis=0)
    hid = jnp.concatenate([hid_a_ref[...], hid_b_ref[...]], axis=0)
    for c in range(0, rows.shape[1], 256):
        cols = slice(c, c + 256)
        out_ref[cols, :] = dot(rows[:, cols], hid, ((0,), (0,))).astype(BF)


def unpack_kernel(slots, moved_ref, grad_ref, in_ref):
    rows = unpack(moved_ref[...], slots)
    count = len(rows) // 2
    for b in range(count):
        at = slice(b * slots, (b + 1) * slots)
        grad_ref[at, :] = rows[b]
        in_ref[at, :] = rows[count + b]


def sum_kernel(images, *refs):
    out_ref = refs[-1]
    each = (len(refs) - 1) // 2
    slots = refs[0].shape[0] // images
    sums = []
    for first in (0, each):
        total = refs[first][...].astype(F32)
        for ref in refs[first + 1 : first + each]:
            total = total + ref[...].astype(F32)
        total = total.astype(BF)
        sums += [total[b * slots : (b + 1) * slots] for b in range(images)]
    out_ref[...] = pack(sums, refs[0].shape[1])


def logits_kernel(owners, moved_ref, logits_in, tokens_in, dy_in, disp_ref, grad_ref, back_ref, router_ref, logits, tokens, dy, sems):
    images, slots, _ = logits.shape
    pairs = [(logits_in, logits)]
    for src, dst in ((dy_in, dy), (tokens_in, tokens)):
        for b in range(images):
            pairs += halves(src, dst, b)
    copies = fetch(pairs, sems)
    rows = unpack(moved_ref[...], slots)
    copies[0].wait()
    parts = []
    for b in range(images):
        comb = softmax(logits[b], 0)
        disp = softmax(logits[b], 1)
        back_ref[b] = rows[images + b]
        for axis in range(2):
            at = 1 + 2 * (axis * images + b)
            copies[at].wait()
            copies[at + 1].wait()
        comb_grad = dot(rows[b], dy[b], ((1,), (1,)))
        disp_grad = dot(rows[images + b], tokens[b], ((1,), (1,)))
        through_comb = comb * (comb_grad - jnp.sum(comb * comb_grad, axis=0, keepdims=True))
        through_disp = disp * (disp_grad - jnp.sum(disp * disp_grad, axis=1, keepdims=True))
        logit_grad = (through_comb + through_disp).astype(BF)
        disp_ref[b] = disp.astype(BF)
        grad_ref[b] = logit_grad
        parts.append(dot(logit_grad, tokens[b], ((1,), (0,))))
    part = sum(parts[1:], parts[0])
    count, half = slots // owners, part.shape[1] // 2
    for k in range(owners):
        for h in range(2):
            at = (2 * k + h) * count
            router_ref[at : at + count, :] = part[k * count : (k + 1) * count, h * half : (h + 1) * half]


def total_kernel(parts_ref, out_ref):
    total = parts_ref[0].astype(F32)
    for k in range(1, parts_ref.shape[0]):
        total = total + parts_ref[k].astype(F32)
    total = total.astype(out_ref.dtype)
    for k in range(out_ref.shape[0]):
        out_ref[k] = total


def rows_kernel(parts_ref, out_ref):
    owners, count, half = parts_ref.shape
    count = count // 2
    for k in range(owners):
        for h in range(2):
            out_ref[k * count : (k + 1) * count, h * half : (h + 1) * half] = parts_ref[k, h * count : (h + 1) * count, :]


def tokens_kernel(disp_ref, grad_ref, back_ref, router_ref, out_ref):
    for b in range(out_ref.shape[0]):
        rows = dot(disp_ref[b], back_ref[b], ((0,), (0,)))
        out_ref[b] = (rows + dot(grad_ref[b], router_ref[...], ((0,), (0,)))).astype(BF)


def on_device(tokens, grad_out, logits, router, fc1_out, w_in, w_out):
    images, slots, count = logits.shape
    width = tokens.shape[2]
    dp_count = lax.axis_size("dp")
    ex_count = lax.axis_size("expert")
    group = dp_count * images
    total = group * ex_count
    w_in, w_out, fc1 = w_in[0], w_out[0], fc1_out[0]
    small = 2 * images * slots * count * width

    def shape(dtype, *dims):
        return jax.ShapeDtypeStruct(dims, dtype)

    fetched = [
        pltpu.VMEM(logits.shape, F32),
        pltpu.VMEM(tokens.shape, BF),
        pltpu.VMEM(tokens.shape, BF),
        pltpu.SemaphoreType.DMA((1 + 4 * images,)),
    ]
    packed_shape = shape(BF, slots * 4 * images, width // 2)

    def swap(packed):
        return exchange(packed.reshape(dp_count, -1, width // 2), "dp").reshape(packed.shape)

    (packed,) = kernel_call(slots_kernel, "rrr", [("v", packed_shape)], 2 * small, 2 * tokens.nbytes, fetched, MOST)(
        logits, grad_out, tokens
    )
    moved = swap(packed)

    hidden = fc1.shape[1]
    big = 2 * total * width * hidden
    me = lax.axis_index("expert").astype(jnp.int32).reshape(1)
    block = shape(BF, group, width)

    def to_peer(value, k):
        return lax.ppermute(value, "expert", [(i, i ^ k) for i in range(ex_count)])

    act, slope_a, slope_b, *out_part = kernel_call(
        functools.partial(hidden_kernel, dp_count, ex_count),
        "svv",
        [("v", shape(BF, total, hidden))] + [("v", shape(BF, total // 2, hidden))] * 2 + [("v", block)] * ex_count,
        2 * big,
        10 * total * hidden,
        vmem=MOST,
    )(me, after(fc1, packed), w_out)
    own_grad, moved_in = kernel_call(
        functools.partial(unpack_kernel, slots), "v", [("v", block), ("v", block)], small, total * width
    )(after(moved, *out_part))
    grad_blocks = [own_grad] + [to_peer(own_grad, k) for k in range(1, ex_count)]
    out_blocks = [out_part[0]]
    for k in range(1, ex_count):
        out_blocks.append(to_peer(out_part[k], k))

    hid, back_part = [], []
    for h, slope in enumerate((slope_a, slope_b)):
        hid_half, *part = kernel_call(
            back_kernel,
            "v" * 7,
            [("v", shape(BF, total // 2, hidden))] + [("v", block)] * 4,
            big,
            5 * total * hidden,
        )(*grad_blocks[4 * h : 4 * h + 4], slope, w_out, w_in)
        hid.append(hid_half)
        back_part += part
    back_blocks = [back_part[0]] + [to_peer(back_part[k], k) for k in range(1, ex_count)]

    (both,) = kernel_call(
        functools.partial(sum_kernel, images),
        "v" * (2 * ex_count),
        [("v", packed_shape)],
        total * width,
        2 * total * width,
    )(*out_blocks, *back_blocks)
    moved_both = swap(both)
    all_in = lax.all_gather(after(moved_in, both), "expert", axis=0, tiled=False)

    half = width // 2
    count_rows = 2 * slots // ex_count
    disp_b, logit_grad, back_rows, router_part = kernel_call(
        functools.partial(logits_kernel, ex_count),
        "vrrr",
        [
            ("v", shape(BF, images, slots, count)),
            ("v", shape(BF, images, slots, count)),
            ("v", shape(BF, images, slots, width)),
            ("v", shape(F32, 2 * slots, half)),
        ],
        3 * small,
        2 * tokens.nbytes,
        fetched,
        20 * MIB,
    )(moved_both, logits, tokens, grad_out)
    (grad_x,) = kernel_call(tokens_kernel, "vvvv", [("v", shape(BF, *tokens.shape))], 2 * small, tokens.nbytes)(
        disp_b, logit_grad, back_rows, router
    )
    (grad_w_out,) = kernel_call(
        weight_out_kernel, "v" * (ex_count + 1), [("v", shape(BF, hidden, width))], big, 10 * total * hidden
    )(act, *grad_blocks)
    (grad_w_in,) = kernel_call(
        weight_in_kernel, "svvv", [("v", shape(BF, width, hidden))], big, 10 * total * hidden
    )(me, all_in, *hid)

    parts = exchange(router_part.reshape(ex_count, count_rows, half), "expert")
    (spread,) = kernel_call(total_kernel, "v", [("v", shape(BF, dp_count, count_rows, half))], small, tokens.nbytes)(parts)
    parts = after(exchange(spread, "dp"), grad_x, grad_w_out)
    (spread,) = kernel_call(total_kernel, "v", [("v", shape(F32, ex_count, count_rows, half))], small, tokens.nbytes)(parts)
    parts = exchange(spread, "expert")
    (grad_router,) = kernel_call(rows_kernel, "v", [("v", shape(F32, slots, width))], small, tokens.nbytes)(
        after(parts, grad_w_in)
    )
    return grad_x, grad_router, grad_w_in[None], grad_w_out[None]


def solution(mesh):
    return jax.shard_map(
        on_device,
        mesh=mesh,
        in_specs=(
            P(("dp", "expert"), None, None),
            P(("dp", "expert"), None, None),
            P(("dp", "expert"), None, None),
            P(),
            P("dp", None, "expert"),
            P("dp", None, "expert"),
            P("dp", "expert", None),
        ),
        out_specs=(
            P(("dp", "expert"), None, None),
            P(),
            P("dp", None, "expert"),
            P("dp", "expert", None),
        ),
        check_vma=False,
    )
```

time: 218 us -> 173 us (0.79)
  blocking collectives: 0 us -> 34.2 us
  waiting for transfers between devices: 67.5 us -> 37.6 us
  Pallas kernels: 0 us -> 27.3 us
  other arithmetic: 23.2 us -> 0 us
  local copies, waits for them, and re-layouts: 27.7 us -> 6.52 us
  matrix products: 18.6 us -> 0 us
  starting transfers between devices: 64.9 us -> 52 us
    all_to_all x9 -> x3, starting transfers between devices: 64.9 us -> 20.6 us  [exchange(): return lax.all_to_all(blocks, axis, split_axis=0, concat_axis=0, tiled=True)]
    all_to_all x9 -> x3, waiting for transfers between devices: 56.8 us -> 15.3 us  [exchange(): return lax.all_to_all(blocks, axis, split_axis=0, concat_axis=0, tiled=True)]
    all_to_all x0 -> x2, blocking collectives: none -> 34.2 us  [exchange(): return lax.all_to_all(blocks, axis, split_axis=0, concat_axis=0, tiled=True)]
    ppermute x0 -> x21, starting transfers between devices: none -> 31.3 us  [to_peer(): return lax.ppermute(value, 'expert', [(i, i ^ k) for i in range(ex_count)])]
    pallas_call x0 -> x13, Pallas kernels: none -> 27.3 us  [run(): pl.pallas_call(body, out_shape=tuple((o[1] for o in outputs)), in_specs=[...]
    ppermute x0 -> x21, waiting for transfers between devices: none -> 22.3 us  [to_peer(): return lax.ppermute(value, 'expert', [(i, i ^ k) for i in range(ex_count)])]
    dot_general x17 -> x0, matrix products: 18.6 us -> none  [dot(): return lax.dot_general(a, b, (dims, ((), ())), preferred_element_type=F32)]
    reduce_scatter x1 -> x0, waiting for transfers between devices: 10.6 us -> none  [on_device(): lax.psum_scatter(out_part, 'expert', scatter_dimension=0, tiled=True)]
  transfers between devices with their start and end apart: 11 -> 25, of which waited for: 8 -> 11; matrix products, arithmetic and copies ran while one was open for 26% -> 0% of each run, Pallas kernels for 0% -> 13%
where the time goes in v2:
time: 173 us; the launch traced here: 172 us
  starting transfers between devices  52 us (30%)
  waiting for transfers between devices  37.6 us (22%)
  blocking collectives  34.2 us (20%)
  Pallas kernels  27.3 us (16%)
  between operations  14.4 us (8%)
  local copies, waits for them, and re-layouts  6.52 us (4%)
    all_to_all x2, blocking collectives, exchange(): return lax.all_to_all(blocks, axis, split_axis=0, concat_axis=0, tiled=True)  34.2 us
    ppermute x21, starting transfers between devices, to_peer(): return lax.ppermute(value, 'expert', [(i, i ^ k) for i in range(ex_count)])  31.3 us
    pallas_call x13, Pallas kernels, run(): pl.pallas_call(body, out_shape=tuple((o[1] for o in outputs)), in_specs=[...  27.3 us
    ppermute x21, waiting for transfers between devices, to_peer(): return lax.ppermute(value, 'expert', [(i, i ^ k) for i in range(ex_count)])  22.3 us
    all_to_all x3, starting transfers between devices, exchange(): return lax.all_to_all(blocks, axis, split_axis=0, concat_axis=0, tiled=True)  20.6 us
    all_to_all x3, waiting for transfers between devices, exchange(): return lax.all_to_all(blocks, axis, split_axis=0, concat_axis=0, tiled=True)  15.3 us
    unnamed x68, local copies, waits for them, and re-layouts  6.52 us
  transfers between devices with their start and end apart: 25, of which 11 were waited for; matrix products, arithmetic and copies ran while one was open for 0% of the time, Pallas kernels for 13%

profile of v2, /device:TPU:1, one launch (start us, length us, event | category | flops | bytes accessed | tf_op | source)
XLA Modules:
  0.0 172.1 jit_solution(6692979420879699898)
XLA Ops:
  7.2 3.1 %shard_map.102 = bf16[256,640]{1,0:T(8,128)(2,1)} custom-call(f32[2,32,256]{2,1,0:T(8,128)} %refs_1_.3, bf16[2,256,1280]{2,1,0:T(8,128)(2,1)} %refs_3_.2, bf16[2,256,1280]{2,1,0:T(8,128)(2,1)} %refs_2_.3), custom_call_target="tpu_custom_call" | custom-call | flops 83886080 | bytes 2621440 | tf_op jit(solution)/shard_map/pallas_call | solution.py:80
  10.3 12.8 %all-to-all-start = ((bf16[32,8,640]{2,1,0:T(8,128)(2,1)}), bf16[32,8,640]{2,1,0:T(8,128)(2,1)}, u32[]{:S(2)}, u32[]{:S(2)}) async-start(bf16[32,8,640]{2,1,0:T(8,128)(2,1)} %bitcast.23), calls=%async_computation | async-start | bytes 655360 | tf_op jit(solution)/shard_map/all_to_all | solution.py:32
  23.2 4.6 %shard_map.103 = (bf16[512,640]{1,0:T(8,128)(2,1)}, bf16[256,640]{1,0:T(8,128)(2,1)}, bf16[256,640]{1,0:T(8,128)(2,1)}, bf16[64,1280]{1,0:T(8,128)(2,1)}, bf16[6...) custom-call(s32[1]{0:T(128)} %bitcast.refs_0_, ...), custom_call_target="tpu_custom_call" | custom-call | flops 1677721600 | bytes 3276800 | tf_op jit(solution)/shard_map/pallas_call | solution.py:80
  29.0 2.4 %collective-permute-start.1 = (bf16[64,1280]{1,0:T(8,128)(2,1)}, bf16[64,1280]{1,0:T(8,128)(2,1)}, u32[]{:S(2)}, u32[]{:S(2)}) collective-permute-start(bf16[64,1280]{1,0:T(8,128)(2,1)} %get-tuple-element.39), channel_id=1, source_target_pairs={{0,2},{1,3},{2,0},{3,1},{4,6},{5,7},{6,4},{7,5},{8,10},{9,11},{10,... | collective-permute-start | bytes 491528 | tf_op jit(solution)/shard_map/ppermute | solution.py:312
  32.4 5.6 %all-to-all-done = bf16[32,8,640]{2,1,0:T(8,128)(2,1)} async-done(((bf16[32,8,640]{2,1,0:T(8,128)(2,1)}), bf16[32,8,640]{2,1,0:T(8,128)(2,1)}, u32[]{:S(2)}, u32[]{:S(2)}) %all-to-all-start) | async-done | bytes 327712 | tf_op jit(solution)/shard_map/all_to_all | solution.py:32
  37.9 1.9 %shard_map.104 = (bf16[64,1280]{1,0:T(8,128)(2,1)S(1)}, bf16[64,1280]{1,0:T(8,128)(2,1)}) custom-call(bf16[256,640]{1,0:T(8,128)(2,1)} %bitcast.4.refs_0_), custom_call_target="tpu_custom_call" | custom-call | flops 41943040 | bytes 655360 | tf_op jit(solution)/shard_map/pallas_call | solution.py:80
  42.2 3.1 %collective-permute-start.15 = (bf16[64,1280]{1,0:T(8,128)(2,1)S(1)}, bf16[64,1280]{1,0:T(8,128)(2,1)S(1)}, u32[]{:S(2)}, u32[]{:S(2)}) collective-permute-start(bf16[64,1280]{1,0:T(8,128)(2,1)S(1)} %get-tuple-element.46.refs_0_.refs_1_), channel_id=1, source_target_pairs={{0,6},{1,7},{2,4},{3,5},{4,2},{5,3},{6,0},{7,1},{8,14},{9,15},{10,... | collective-permute-start | bytes 491528 | tf_op jit(solution)/shard_map/ppermute | solution.py:312
  45.8 3.7 %collective-permute-start.8 = (bf16[64,1280]{1,0:T(8,128)(2,1)S(1)}, bf16[64,1280]{1,0:T(8,128)(2,1)S(1)}, u32[]{:S(2)}, u32[]{:S(2)}) collective-permute-start(bf16[64,1280]{1,0:T(8,128)(2,1)S(1)} %get-tuple-element.46.refs_0_.refs_1_), channel_id=1, source_target_pairs={{0,2},{1,3},{2,0},{3,1},{4,6},{5,7},{6,4},{7,5},{8,10},{9,11},{10,... | collective-permute-start | bytes 491528 | tf_op jit(solution)/shard_map/ppermute | solution.py:312
  49.6 1.8 %collective-permute-start.9 = (bf16[64,1280]{1,0:T(8,128)(2,1)S(1)}, bf16[64,1280]{1,0:T(8,128)(2,1)S(1)}, u32[]{:S(2)}, u32[]{:S(2)}) collective-permute-start(bf16[64,1280]{1,0:T(8,128)(2,1)S(1)} %get-tuple-element.46.refs_0_.refs_1_), channel_id=1, source_target_pairs={{0,3},{1,2},{2,1},{3,0},{4,7},{5,6},{6,5},{7,4},{8,11},{9,10},{10,... | collective-permute-start | bytes 491528 | tf_op jit(solution)/shard_map/ppermute | solution.py:312
  51.4 3.3 %collective-permute-done.15.refs_2_.refs_7_ = bf16[64,1280]{1,0:T(8,128)(2,1)S(1)} collective-permute-done((bf16[64,1280]{1,0:T(8,128)(2,1)S(1)}, bf16[64,1280]{1,0:T(8,128)(2,1)S(1)}, u32[]{:S(2)}, u32[]{:S(2)}) %collective-permute-start.15) | collective-permute-done | bytes 163872 | tf_op jit(solution)/shard_map/ppermute | solution.py:312
  56.1 2.2 %collective-permute-done.16.refs_3_.refs_8_ = bf16[64,1280]{1,0:T(8,128)(2,1)S(1)} collective-permute-done((bf16[64,1280]{1,0:T(8,128)(2,1)S(1)}, bf16[64,1280]{1,0:T(8,128)(2,1)S(1)}, u32[]{:S(2)}, u32[]{:S(2)}) %collective-permute-start.16) | collective-permute-done | bytes 163872 | tf_op jit(solution)/shard_map/ppermute | solution.py:312
  60.3 2.1 %shard_map.106 = (bf16[256,640]{1,0:T(8,128)(2,1)S(1)}, bf16[64,1280]{1,0:T(8,128)(2,1)S(1)}, bf16[64,1280]{1,0:T(8,128)(2,1)S(1)}, bf16[64,1280]{1,0:T(8,128)(2,1)S(1)}, bf16[64,1280]{1,0:T(8,128)(2,1)S(1)}) custom-call(bf16[64,1280]{1,0:T(8,128)(2,1)S(1)} %collective-permute-done.13.refs_0_.refs_5_, ...), custom_call_target="tpu_custom_call" | custom-call | flops 838860800 | bytes 1638400 | tf_op jit(solution)/shard_map/pallas_call | solution.py:80
  62.5 2.8 %collective-permute-start.6 = (bf16[64,1280]{1,0:T(8,128)(2,1)S(1)}, bf16[64,1280]{1,0:T(8,128)(2,1)S(1)}, u32[]{:S(2)}, u32[]{:S(2)}) collective-permute-start(bf16[64,1280]{1,0:T(8,128)(2,1)S(1)} %copy-done.33), channel_id=1, source_target_pairs={{0,7},{1,6},{2,5},{3,4},{4,3},{5,2},{6,1},{7,0},{8,15},{9,14},{10,... | collective-permute-start | bytes 491528 | tf_op jit(solution)/shard_map/ppermute | solution.py:312
  65.3 5.8 %collective-permute-done.8.refs_2_.refs_3_ = bf16[64,1280]{1,0:T(8,128)(2,1)S(1)} collective-permute-done((bf16[64,1280]{1,0:T(8,128)(2,1)S(1)}, bf16[64,1280]{1,0:T(8,128)(2,1)S(1)}, u32[]{:S(2)}, u32[]{:S(2)}) %collective-permute-start.8) | collective-permute-done | bytes 163872 | tf_op jit(solution)/shard_map/ppermute | solution.py:312
  71.1 1.6 collective-permute-start.17
  72.7 2.1 %shard_map.105 = (bf16[256,640]{1,0:T(8,128)(2,1)S(1)}, bf16[64,1280]{1,0:T(8,128)(2,1)S(1)}, bf16[64,1280]{1,0:T(8,128)(2,1)S(1)}, bf16[64,1280]{1,0:T(8,128)(2,1)S(1)}, bf16[64,1280]{1,0:T(8,128)(2,1)S(1)}) custom-call(bf16[64,1280]{1,0:T(8,128)(2,1)S(1)} %get-tuple-element.46.refs_0_.refs_1_, bf16[64,1280]{1,0:T(8,128)(2,1)S(1)} %collective-permute-done.7.refs_1_.refs_2_, ...), custom_call_target="tpu_custom_call" | custom-call | flops 838860800 | bytes 1638400 | tf_op jit(solution)/shard_map/pallas_call | solution.py:80
  77.1 3.0 %collective-permute-start.20 = (bf16[64,1280]{1,0:T(8,128)(2,1)S(1)}, bf16[64,1280]{1,0:T(8,128)(2,1)S(1)}, u32[]{:S(2)}, u32[]{:S(2)}) collective-permute-start(bf16[64,1280]{1,0:T(8,128)(2,1)S(1)} %get-tuple-element.56), channel_id=1, source_target_pairs={{0,7},{1,6},{2,5},{3,4},{4,3},{5,2},{6,1},{7,0},{8,15},{9,14},{10,... | collective-permute-start | bytes 491528 | tf_op jit(solution)/shard_map/ppermute | solution.py:312
  81.6 2.4 %collective-permute-start.12 = (bf16[64,1280]{1,0:T(8,128)(2,1)S(1)}, bf16[64,1280]{1,0:T(8,128)(2,1)S(1)}, u32[]{:S(2)}, u32[]{:S(2)}) collective-permute-start(bf16[64,1280]{1,0:T(8,128)(2,1)S(1)} %get-tuple-element.51), channel_id=1, source_target_pairs={{0,3},{1,2},{2,1},{3,0},{4,7},{5,6},{6,5},{7,4},{8,11},{9,10},{10,... | collective-permute-start | bytes 491528 | tf_op jit(solution)/shard_map/ppermute | solution.py:312
  84.0 2.3 %collective-permute-done.20.refs_15_ = bf16[64,1280]{1,0:T(8,128)(2,1)S(1)} collective-permute-done((bf16[64,1280]{1,0:T(8,128)(2,1)S(1)}, bf16[64,1280]{1,0:T(8,128)(2,1)S(1)}, u32[]{:S(2)}, u32[]{:S(2)}) %collective-permute-start.20) | collective-permute-done | bytes 163872 | tf_op jit(solution)/shard_map/ppermute | solution.py:312
  86.9 3.8 %collective-permute-done.11.refs_10_ = bf16[64,1280]{1,0:T(8,128)(2,1)S(1)} collective-permute-done((bf16[64,1280]{1,0:T(8,128)(2,1)S(1)}, bf16[64,1280]{1,0:T(8,128)(2,1)S(1)}, u32[]{:S(2)}, u32[]{:S(2)}) %collective-permute-start.11) | collective-permute-done | bytes 163872 | tf_op jit(solution)/shard_map/ppermute | solution.py:312
  90.7 4.1 %collective-permute-done.12.refs_11_ = bf16[64,1280]{1,0:T(8,128)(2,1)S(1)} collective-permute-done((bf16[64,1280]{1,0:T(8,128)(2,1)S(1)}, bf16[64,1280]{1,0:T(8,128)(2,1)S(1)}, u32[]{:S(2)}, u32[]{:S(2)}) %collective-permute-start.12) | collective-permute-done | bytes 163872 | tf_op jit(solution)/shard_map/ppermute | solution.py:312
  94.9 1.9 %shard_map.107 = bf16[256,640]{1,0:T(8,128)(2,1)S(1)} custom-call(bf16[64,1280]{1,0:T(8,128)(2,1)S(1)} %copy-done.27, bf16[64,1280]{1,0:T(8,128)(2,1)} %collective-permute-done.refs_1_, bf16[64,1280]{1,0:T(8,128)(2,1)} %collective-permute-done.1.refs_2_, bf16[64,1280]{1,0:T(8,128)(2,1)} %collective-permute-done.2.refs_3_, ...), custom_call_target="tpu_custom_call" | custom-call | flops 655360 | bytes 1310720 | tf_op jit(solution)/shard_map/pallas_call | solution.py:80
  96.8 22.6 %all_to_all.25 = bf16[32,8,640]{2,1,0:T(8,128)(2,1)S(1)} all-to-all(bf16[32,8,640]{2,1,0:T(8,128)(2,1)S(1)} %bitcast.19), channel_id=1, replica_groups=mesh['dp'=32,'expert'=8] {'dp'}, dimensions={0} | all-to-all | bytes 655360 | tf_op jit(solution)/shard_map/all_to_all | solution.py:32
  119.4 2.9 %shard_map.108 = (bf16[2,32,256]{2,1,0:T(8,128)(2,1)S(1)}, bf16[2,32,256]{2,1,0:T(8,128)(2,1)S(1)}, bf16[2,32,1280]{2,1,0:T(8,128)(2,1)S(1)}, f32[64,640]{1,0:T(8,128)S(1)}) custom-call(bf16[256,640]{1,0:T(8,128)(2,1)S(1)} %bitcast.17, f32[2,32,256]{2,1,0:T(8,128)S(1)} %copy-done.26, bf16[2,256,1280]{2,1,0:T(8,128)(2,1)S(1)} %copy-done.3, ...), custom_call_target="tpu_custom_call" | custom-call | flops 125829120 | bytes 2621440 | tf_op jit(solution)/shard_map/pallas_call | solution.py:80
  123.0 11.7 %all_to_all.26.refs_0_ = f32[8,8,640]{2,1,0:T(8,128)S(1)} all-to-all(f32[8,8,640]{2,1,0:T(8,128)S(1)} %bitcast.20), channel_id=1, replica_groups=mesh['dp'=32,'expert'=8] {'expert'}, dimensions={0} | all-to-all | bytes 327680 | tf_op jit(solution)/shard_map/all_to_all | solution.py:32
  135.4 4.5 %all-to-all-start.3 = ((bf16[32,8,640]{2,1,0:T(8,128)(2,1)}), bf16[32,8,640]{2,1,0:T(8,128)(2,1)S(1)}, u32[]{:S(2)}, u32[]{:S(2)}) async-start(bf16[32,8,640]{2,1,0:T(8,128)(2,1)} %shard_map.110), calls=%async_computation.3 | async-start | bytes 655360 | tf_op jit(solution)/shard_map/all_to_all | solution.py:32
  142.7 2.2 %shard_map.111 = bf16[640,1280]{1,0:T(8,128)(2,1)} custom-call(bf16[512,640]{1,0:T(8,128)(2,1)S(1)} %copy-done.19, bf16[64,1280]{1,0:T(8,128)(2,1)S(1)} %get-tuple-element.46.refs_0_.refs_1_, bf16[64,1280]{1,0:T(8,128)(2,1)S(1)} %copy-done.14, bf16[64,1280]{1,0:T(8,128)(2,1)S(1)} %copy-done.16, bf16[64,1280]{1,0:T(8,128)(2,1)S(1)} %copy-done.18, ...), custom_call_target="tpu_custom_call" | custom-call | flops 838860800 | bytes 3276800 | tf_op jit(solution)/shard_map/pallas_call | solution.py:80
  145.0 1.9 %shard_map.109 = bf16[2,256,1280]{2,1,0:T(8,128)(2,1)} custom-call(bf16[2,32,256]{2,1,0:T(8,128)(2,1)S(1)} %get-tuple-element.57.refs_0_, bf16[2,32,256]{2,1,0:T(8,128)(2,1)S(1)} %copy-done.32, bf16[2,32,1280]{2,1,0:T(8,128)(2,1)S(1)} %copy-done.29, bf16[32,1280]{1,0:T(8,128)(2,1)S(1)} %copy-done.30), custom_call_target="tpu_custom_call" | custom-call | flops 83886080 | bytes 1310720 | tf_op jit(solution)/shard_map/pallas_call | solution.py:80
  146.9 7.9 %all-to-all-done.3.refs_0_ = bf16[32,8,640]{2,1,0:T(8,128)(2,1)S(1)} async-done(((bf16[32,8,640]{2,1,0:T(8,128)(2,1)}), bf16[32,8,640]{2,1,0:T(8,128)(2,1)S(1)}, u32[]{:S(2)}, u32[]{:S(2)}) %all-to-all-start.3) | async-done | bytes 327712 | tf_op jit(solution)/shard_map/all_to_all | solution.py:32
  155.5 3.4 %all-to-all-start.4 = ((f32[8,8,640]{2,1,0:T(8,128)}), f32[8,8,640]{2,1,0:T(8,128)S(1)}, u32[]{:S(2)}, u32[]{:S(2)}) async-start(f32[8,8,640]{2,1,0:T(8,128)} %shard_map.112), calls=%async_computation.4 | async-start | bytes 327680 | tf_op jit(solution)/shard_map/all_to_all | solution.py:32
  160.3 2.4 %shard_map.113 = bf16[1280,640]{1,0:T(8,128)(2,1)} custom-call(s32[1]{0:T(128)} %bitcast.refs_0_, bf16[8,64,1280]{2,1,0:T(8,128)(2,1)S(1)} %bitcast.18, bf16[256,640]{1,0:T(8,128)(2,1)S(1)} %copy-done.25, bf16[256,640]{1,0:T(8,128)(2,1)S(1)} %copy-done.23), custom_call_target="tpu_custom_call" | custom-call | flops 838860800 | bytes 3276800 | tf_op jit(solution)/shard_map/pallas_call | solution.py:80
  162.7 1.9 %all-to-all-done.4.refs_0_ = f32[8,8,640]{2,1,0:T(8,128)S(1)} async-done(((f32[8,8,640]{2,1,0:T(8,128)}), f32[8,8,640]{2,1,0:T(8,128)S(1)}, u32[]{:S(2)}, u32[]{:S(2)}) %all-to-all-start.4) | async-done | bytes 163872 | tf_op jit(solution)/shard_map/all_to_all | solution.py:32
  (102 shorter events, 20.0 us)
Async XLA Ops:
  10.3 27.6 %all-to-all-start = ((bf16[32,8,640]{2,1,0:T(8,128)(2,1)}), bf16[32,8,640]{2,1,0:T(8,128)(2,1)}, u32[]{:S(2)}, u32[]{:S(2)}) async-start(bf16[32,8,640]{2,1,0:T(8,128)(2,1)} %bitcast.23), calls=%async_computation | async-start | bytes 655360 | tf_op jit(solution)/shard_map/all_to_all | solution.py:32
  23.1 135.8 %all-gather.3.cloned.1.call-start = ((), (), s32[]{:S(2)}) async-start(), calls=%async_computation.5 | async-start | bytes 1474560 | tf_op jit(solution)/shard_map/all_gather | solution.py:351
  23.1 36.2 %copy-start = (bf16[1,640,1280]{2,1,0:T(8,128)(2,1)S(1)}, bf16[1,640,1280]{2,1,0:T(8,128)(2,1)}, u32[]{:S(2)}) copy-start(bf16[1,640,1280]{2,1,0:T(8,128)(2,1)} %param.13) | copy-start | bytes 4915204
  23.1 36.2 %copy-start.1 = (bf16[1,1280,640]{2,1,0:T(8,128)(2,1)S(1)}, bf16[1,1280,640]{2,1,0:T(8,128)(2,1)}, u32[]{:S(2)}) copy-start(bf16[1,1280,640]{2,1,0:T(8,128)(2,1)} %param.12) | copy-start | bytes 4915204
  27.7 13.0 %collective-permute-start = (bf16[64,1280]{1,0:T(8,128)(2,1)}, bf16[64,1280]{1,0:T(8,128)(2,1)}, u32[]{:S(2)}, u32[]{:S(2)}) collective-permute-start(bf16[64,1280]{1,0:T(8,128)(2,1)} %get-tuple-element.38), channel_id=1, source_target_pairs={{0,1},{1,0},{2,3},{3,2},{4,5},{5,4},{6,7},{7,6},{8,9},{9,8},{10,11... | collective-permute-start | bytes 491528 | tf_op jit(solution)/shard_map/ppermute | solution.py:312
  29.0 13.3 %collective-permute-start.1 = (bf16[64,1280]{1,0:T(8,128)(2,1)}, bf16[64,1280]{1,0:T(8,128)(2,1)}, u32[]{:S(2)}, u32[]{:S(2)}) collective-permute-start(bf16[64,1280]{1,0:T(8,128)(2,1)} %get-tuple-element.39), channel_id=1, source_target_pairs={{0,2},{1,3},{2,0},{3,1},{4,6},{5,7},{6,4},{7,5},{8,10},{9,11},{10,... | collective-permute-start | bytes 491528 | tf_op jit(solution)/shard_map/ppermute | solution.py:312
  31.4 13.9 %collective-permute-start.2 = (bf16[64,1280]{1,0:T(8,128)(2,1)}, bf16[64,1280]{1,0:T(8,128)(2,1)}, u32[]{:S(2)}, u32[]{:S(2)}) collective-permute-start(bf16[64,1280]{1,0:T(8,128)(2,1)} %get-tuple-element.40), channel_id=1, source_target_pairs={{0,3},{1,2},{2,1},{3,0},{4,7},{5,6},{6,5},{7,4},{8,11},{9,10},{10,... | collective-permute-start | bytes 491528 | tf_op jit(solution)/shard_map/ppermute | solution.py:312
  31.6 14.2 %collective-permute-start.3 = (bf16[64,1280]{1,0:T(8,128)(2,1)}, bf16[64,1280]{1,0:T(8,128)(2,1)}, u32[]{:S(2)}, u32[]{:S(2)}) collective-permute-start(bf16[64,1280]{1,0:T(8,128)(2,1)} %get-tuple-element.41), channel_id=1, source_target_pairs={{0,4},{1,5},{2,6},{3,7},{4,0},{5,1},{6,2},{7,3},{8,12},{9,13},{10,... | collective-permute-start | bytes 491528 | tf_op jit(solution)/shard_map/ppermute | solution.py:312
  39.8 6.0 %collective-permute-start.13 = (bf16[64,1280]{1,0:T(8,128)(2,1)S(1)}, bf16[64,1280]{1,0:T(8,128)(2,1)S(1)}, u32[]{:S(2)}, u32[]{:S(2)}) collective-permute-start(bf16[64,1280]{1,0:T(8,128)(2,1)S(1)} %get-tuple-element.46.refs_0_.refs_1_), channel_id=1, source_target_pairs={{0,4},{1,5},{2,6},{3,7},{4,0},{5,1},{6,2},{7,3},{8,12},{9,13},{10,... | collective-permute-start | bytes 491528 | tf_op jit(solution)/shard_map/ppermute | solution.py:312
  40.8 8.8 %collective-permute-start.14 = (bf16[64,1280]{1,0:T(8,128)(2,1)S(1)}, bf16[64,1280]{1,0:T(8,128)(2,1)S(1)}, u32[]{:S(2)}, u32[]{:S(2)}) collective-permute-start(bf16[64,1280]{1,0:T(8,128)(2,1)S(1)} %get-tuple-element.46.refs_0_.refs_1_), channel_id=1, source_target_pairs={{0,5},{1,4},{2,7},{3,6},{4,1},{5,0},{6,3},{7,2},{8,13},{9,12},{10,... | collective-permute-start | bytes 491528 | tf_op jit(solution)/shard_map/ppermute | solution.py:312
  42.2 12.4 %collective-permute-start.15 = (bf16[64,1280]{1,0:T(8,128)(2,1)S(1)}, bf16[64,1280]{1,0:T(8,128)(2,1)S(1)}, u32[]{:S(2)}, u32[]{:S(2)}) collective-permute-start(bf16[64,1280]{1,0:T(8,128)(2,1)S(1)} %get-tuple-element.46.refs_0_.refs_1_), channel_id=1, source_target_pairs={{0,6},{1,7},{2,4},{3,5},{4,2},{5,3},{6,0},{7,1},{8,14},{9,15},{10,... | collective-permute-start | bytes 491528 | tf_op jit(solution)/shard_map/ppermute | solution.py:312
  45.4 12.9 %collective-permute-start.16 = (bf16[64,1280]{1,0:T(8,128)(2,1)S(1)}, bf16[64,1280]{1,0:T(8,128)(2,1)S(1)}, u32[]{:S(2)}, u32[]{:S(2)}) collective-permute-start(bf16[64,1280]{1,0:T(8,128)(2,1)S(1)} %get-tuple-element.46.refs_0_.refs_1_), channel_id=1, source_target_pairs={{0,7},{1,6},{2,5},{3,4},{4,3},{5,2},{6,1},{7,0},{8,15},{9,14},{10,... | collective-permute-start | bytes 491528 | tf_op jit(solution)/shard_map/ppermute | solution.py:312
  45.8 16.7 %collective-permute-start.7 = (bf16[64,1280]{1,0:T(8,128)(2,1)S(1)}, bf16[64,1280]{1,0:T(8,128)(2,1)S(1)}, u32[]{:S(2)}, u32[]{:S(2)}) collective-permute-start(bf16[64,1280]{1,0:T(8,128)(2,1)S(1)} %get-tuple-element.46.refs_0_.refs_1_), channel_id=1, source_target_pairs={{0,1},{1,0},{2,3},{3,2},{4,5},{5,4},{6,7},{7,6},{8,9},{9,8},{10,11... | collective-permute-start | bytes 491528 | tf_op jit(solution)/shard_map/ppermute | solution.py:312
  45.8 25.3 %collective-permute-start.8 = (bf16[64,1280]{1,0:T(8,128)(2,1)S(1)}, bf16[64,1280]{1,0:T(8,128)(2,1)S(1)}, u32[]{:S(2)}, u32[]{:S(2)}) collective-permute-start(bf16[64,1280]{1,0:T(8,128)(2,1)S(1)} %get-tuple-element.46.refs_0_.refs_1_), channel_id=1, source_target_pairs={{0,2},{1,3},{2,0},{3,1},{4,6},{5,7},{6,4},{7,5},{8,10},{9,11},{10,... | collective-permute-start | bytes 491528 | tf_op jit(solution)/shard_map/ppermute | solution.py:312
  49.6 23.1 %collective-permute-start.9 = (bf16[64,1280]{1,0:T(8,128)(2,1)S(1)}, bf16[64,1280]{1,0:T(8,128)(2,1)S(1)}, u32[]{:S(2)}, u32[]{:S(2)}) collective-permute-start(bf16[64,1280]{1,0:T(8,128)(2,1)S(1)} %get-tuple-element.46.refs_0_.refs_1_), channel_id=1, source_target_pairs={{0,3},{1,2},{2,1},{3,0},{4,7},{5,6},{6,5},{7,4},{8,11},{9,10},{10,... | collective-permute-start | bytes 491528 | tf_op jit(solution)/shard_map/ppermute | solution.py:312
  54.7 21.0 %collective-permute-start.4 = (bf16[64,1280]{1,0:T(8,128)(2,1)}, bf16[64,1280]{1,0:T(8,128)(2,1)S(1)}, u32[]{:S(2)}, u32[]{:S(2)}) collective-permute-start(bf16[64,1280]{1,0:T(8,128)(2,1)} %get-tuple-element.42), channel_id=1, source_target_pairs={{0,5},{1,4},{2,7},{3,6},{4,1},{5,0},{6,3},{7,2},{8,13},{9,12},{10,... | collective-permute-start | bytes 491528 | tf_op jit(solution)/shard_map/ppermute | solution.py:312
  58.3 18.8 %collective-permute-start.5 = (bf16[64,1280]{1,0:T(8,128)(2,1)}, bf16[64,1280]{1,0:T(8,128)(2,1)S(1)}, u32[]{:S(2)}, u32[]{:S(2)}) collective-permute-start(bf16[64,1280]{1,0:T(8,128)(2,1)} %get-tuple-element.43), channel_id=1, source_target_pairs={{0,6},{1,7},{2,4},{3,5},{4,2},{5,3},{6,0},{7,1},{8,14},{9,15},{10,... | collective-permute-start | bytes 491528 | tf_op jit(solution)/shard_map/ppermute | solution.py:312
  62.5 17.6 %collective-permute-start.6 = (bf16[64,1280]{1,0:T(8,128)(2,1)S(1)}, bf16[64,1280]{1,0:T(8,128)(2,1)S(1)}, u32[]{:S(2)}, u32[]{:S(2)}) collective-permute-start(bf16[64,1280]{1,0:T(8,128)(2,1)S(1)} %copy-done.33), channel_id=1, source_target_pairs={{0,7},{1,6},{2,5},{3,4},{4,3},{5,2},{6,1},{7,0},{8,15},{9,14},{10,... | collective-permute-start | bytes 491528 | tf_op jit(solution)/shard_map/ppermute | solution.py:312
  71.1 9.0 %collective-permute-start.17 = (bf16[64,1280]{1,0:T(8,128)(2,1)S(1)}, bf16[64,1280]{1,0:T(8,128)(2,1)S(1)}, u32[]{:S(2)}, u32[]{:S(2)}) collective-permute-start(bf16[64,1280]{1,0:T(8,128)(2,1)S(1)} %get-tuple-element.53), channel_id=1, source_target_pairs={{0,4},{1,5},{2,6},{3,7},{4,0},{5,1},{6,2},{7,3},{8,12},{9,13},{10,... | collective-permute-start | bytes 491528 | tf_op jit(solution)/shard_map/ppermute | solution.py:312
  72.7 8.9 %collective-permute-start.18 = (bf16[64,1280]{1,0:T(8,128)(2,1)S(1)}, bf16[64,1280]{1,0:T(8,128)(2,1)S(1)}, u32[]{:S(2)}, u32[]{:S(2)}) collective-permute-start(bf16[64,1280]{1,0:T(8,128)(2,1)S(1)} %get-tuple-element.54), channel_id=1, source_target_pairs={{0,5},{1,4},{2,7},{3,6},{4,1},{5,0},{6,3},{7,2},{8,13},{9,12},{10,... | collective-permute-start | bytes 491528 | tf_op jit(solution)/shard_map/ppermute | solution.py:312
  72.7 22.1 %copy-start.27 = (bf16[64,1280]{1,0:T(8,128)(2,1)S(1)}, bf16[64,1280]{1,0:T(8,128)(2,1)}, u32[]{:S(2)}) copy-start(bf16[64,1280]{1,0:T(8,128)(2,1)} %get-tuple-element.37.refs_0_) | copy-start | bytes 491524
  75.6 8.4 %collective-permute-start.19 = (bf16[64,1280]{1,0:T(8,128)(2,1)S(1)}, bf16[64,1280]{1,0:T(8,128)(2,1)S(1)}, u32[]{:S(2)}, u32[]{:S(2)}) collective-permute-start(bf16[64,1280]{1,0:T(8,128)(2,1)S(1)} %get-tuple-element.55), channel_id=1, source_target_pairs={{0,6},{1,7},{2,4},{3,5},{4,2},{5,3},{6,0},{7,1},{8,14},{9,15},{10,... | collective-permute-start | bytes 491528 | tf_op jit(solution)/shard_map/ppermute | solution.py:312
  77.1 9.2 %collective-permute-start.20 = (bf16[64,1280]{1,0:T(8,128)(2,1)S(1)}, bf16[64,1280]{1,0:T(8,128)(2,1)S(1)}, u32[]{:S(2)}, u32[]{:S(2)}) collective-permute-start(bf16[64,1280]{1,0:T(8,128)(2,1)S(1)} %get-tuple-element.56), channel_id=1, source_target_pairs={{0,7},{1,6},{2,5},{3,4},{4,3},{5,2},{6,1},{7,0},{8,15},{9,14},{10,... | collective-permute-start | bytes 491528 | tf_op jit(solution)/shard_map/ppermute | solution.py:312
  80.2 6.8 %collective-permute-start.10 = (bf16[64,1280]{1,0:T(8,128)(2,1)S(1)}, bf16[64,1280]{1,0:T(8,128)(2,1)S(1)}, u32[]{:S(2)}, u32[]{:S(2)}) collective-permute-start(bf16[64,1280]{1,0:T(8,128)(2,1)S(1)} %get-tuple-element.49), channel_id=1, source_target_pairs={{0,1},{1,0},{2,3},{3,2},{4,5},{5,4},{6,7},{7,6},{8,9},{9,8},{10,11... | collective-permute-start | bytes 491528 | tf_op jit(solution)/shard_map/ppermute | solution.py:312
  80.2 10.6 %collective-permute-start.11 = (bf16[64,1280]{1,0:T(8,128)(2,1)S(1)}, bf16[64,1280]{1,0:T(8,128)(2,1)S(1)}, u32[]{:S(2)}, u32[]{:S(2)}) collective-permute-start(bf16[64,1280]{1,0:T(8,128)(2,1)S(1)} %get-tuple-element.50), channel_id=1, source_target_pairs={{0,2},{1,3},{2,0},{3,1},{4,6},{5,7},{6,4},{7,5},{8,10},{9,11},{10,... | collective-permute-start | bytes 491528 | tf_op jit(solution)/shard_map/ppermute | solution.py:312
  81.6 13.3 %collective-permute-start.12 = (bf16[64,1280]{1,0:T(8,128)(2,1)S(1)}, bf16[64,1280]{1,0:T(8,128)(2,1)S(1)}, u32[]{:S(2)}, u32[]{:S(2)}) collective-permute-start(bf16[64,1280]{1,0:T(8,128)(2,1)S(1)} %get-tuple-element.51), channel_id=1, source_target_pairs={{0,3},{1,2},{2,1},{3,0},{4,7},{5,6},{6,5},{7,4},{8,11},{9,10},{10,... | collective-permute-start | bytes 491528 | tf_op jit(solution)/shard_map/ppermute | solution.py:312
  94.9 24.5 %copy-start.2 = (bf16[2,256,1280]{2,1,0:T(8,128)(2,1)S(1)}, bf16[2,256,1280]{2,1,0:T(8,128)(2,1)}, u32[]{:S(2)}) copy-start(bf16[2,256,1280]{2,1,0:T(8,128)(2,1)} %refs_3_.2) | copy-start | bytes 3932164
  94.9 24.5 %copy-start.3 = (bf16[2,256,1280]{2,1,0:T(8,128)(2,1)S(1)}, bf16[2,256,1280]{2,1,0:T(8,128)(2,1)}, u32[]{:S(2)}) copy-start(bf16[2,256,1280]{2,1,0:T(8,128)(2,1)} %refs_2_.3) | copy-start | bytes 3932164
  94.9 24.5 %copy-start.26 = (f32[2,32,256]{2,1,0:T(8,128)S(1)}, f32[2,32,256]{2,1,0:T(8,128)}, u32[]{:S(2)}) copy-start(f32[2,32,256]{2,1,0:T(8,128)} %refs_1_.3) | copy-start | bytes 196612
  119.4 20.5 %copy-start.6 = (bf16[64,1280]{1,0:T(8,128)(2,1)S(1)}, bf16[64,1280]{1,0:T(8,128)(2,1)}, u32[]{:S(2)}) copy-start(bf16[64,1280]{1,0:T(8,128)(2,1)} %copy-done.5) | copy-start | bytes 491524
  135.4 19.3 %all-to-all-start.3 = ((bf16[32,8,640]{2,1,0:T(8,128)(2,1)}), bf16[32,8,640]{2,1,0:T(8,128)(2,1)S(1)}, u32[]{:S(2)}, u32[]{:S(2)}) async-start(bf16[32,8,640]{2,1,0:T(8,128)(2,1)} %shard_map.110), calls=%async_computation.3 | async-start | bytes 655360 | tf_op jit(solution)/shard_map/all_to_all | solution.py:32
  155.5 9.0 %all-to-all-start.4 = ((f32[8,8,640]{2,1,0:T(8,128)}), f32[8,8,640]{2,1,0:T(8,128)S(1)}, u32[]{:S(2)}, u32[]{:S(2)}) async-start(f32[8,8,640]{2,1,0:T(8,128)} %shard_map.112), calls=%async_computation.4 | async-start | bytes 327680 | tf_op jit(solution)/shard_map/all_to_all | solution.py:32
  (27 other events, 218.1 us)
Sparse Core Ops, SparseCore 0:
  96.9 38.1 all-gather.2

commit v3 on v2

--- a/solution.py
+++ b/solution.py
@@ -11,6 +11,7 @@
 F32 = jnp.float32
 MIB = 1024 * 1024
 MOST = 60 * MIB
+RING = 4
 
 
 def gelu_slope(value):
@@ -150,7 +151,8 @@
     me = me_ref[0]
     for c in range(total // block):
         at = lax.broadcasted_iota(jnp.int32, (block, total), 0) + c * block
-        owner = lax.bitwise_xor(at // group, jnp.full(at.shape, me, jnp.int32))
+        row = at // group
+        owner = (row + me) % RING + RING * ((row // RING + me // RING) % 2)
         source = (at % dp_count) * (ex_count * images) + owner * images + (at // dp_count) % images
         pick = (source == lax.broadcasted_iota(jnp.int32, (block, total), 1)).astype(BF)
         pre = dot(pick, fc1_ref[...], ((1,), (0,)))
@@ -160,8 +162,9 @@
         act_ref[c * block : (c + 1) * block, :] = act
         slope_refs[c // 2][(c % 2) * block : (c % 2 + 1) * block, :] = (cdf + pre * density).astype(BF)
         out = dot(act, w_ref[...], ((1,), (0,))).astype(BF)
-        out_refs[2 * c][...] = out[:group]
-        out_refs[2 * c + 1][...] = out[group:]
+        for h in range(2):
+            far, step = (2 * c + h) // RING, (2 * c + h) % RING
+            out_refs[step][far * group : (far + 1) * group, :] = out[h * group : (h + 1) * group]
 
 
 def back_kernel(*refs):
@@ -184,11 +187,11 @@
         refs[-1][cols, :] = dot(act_ref[:, cols], grad, ((0,), (0,))).astype(BF)
 
 
-def weight_in_kernel(me_ref, all_ref, hid_a_ref, hid_b_ref, out_ref):
-    me = me_ref[0]
-    group = all_ref.shape[1]
-    rows = jnp.concatenate([all_ref[lax.bitwise_xor(me, jnp.int32(k))] for k in range(all_ref.shape[0])], axis=0)
-    hid = jnp.concatenate([hid_a_ref[...], hid_b_ref[...]], axis=0)
+def weight_in_kernel(*refs):
+    pairs, hid_refs, out_ref = refs[:RING], refs[RING : RING + 2], refs[-1]
+    group = pairs[0].shape[0] // 2
+    rows = jnp.concatenate([r[z * group : (z + 1) * group, :] for z in range(2) for r in pairs], axis=0)
+    hid = jnp.concatenate([r[...] for r in hid_refs], axis=0)
     for c in range(0, rows.shape[1], 256):
         cols = slice(c, c + 256)
         out_ref[cols, :] = dot(rows[:, cols], hid, ((0,), (0,))).astype(BF)
@@ -203,14 +206,28 @@
         in_ref[at, :] = rows[count + b]
 
 
+def plane_kernel(*refs):
+    far_ref, group = refs[4], refs[4].shape[0]
+    both = refs[0].shape[0] > group
+
+    def add(rows):
+        total = refs[0][rows, :].astype(F32)
+        for ref in refs[1:4]:
+            total = total + ref[rows, :].astype(F32)
+        return total
+
+    far_ref[...] = add(slice(group, 2 * group) if both else slice(0, group)).astype(BF)
+    if both:
+        refs[5][...] = add(slice(0, group))
+
+
 def sum_kernel(images, *refs):
     out_ref = refs[-1]
-    each = (len(refs) - 1) // 2
     slots = refs[0].shape[0] // images
     sums = []
-    for first in (0, each):
-        total = refs[first][...].astype(F32)
-        for ref in refs[first + 1 : first + each]:
+    for parts in (refs[:2], refs[2:-1]):
+        total = parts[0][...].astype(F32)
+        for ref in parts[1:]:
             total = total + ref[...].astype(F32)
         total = total.astype(BF)
         sums += [total[b * slots : (b + 1) * slots] for b in range(images)]
@@ -308,13 +325,16 @@
     me = lax.axis_index("expert").astype(jnp.int32).reshape(1)
     block = shape(BF, group, width)
 
-    def to_peer(value, k):
-        return lax.ppermute(value, "expert", [(i, i ^ k) for i in range(ex_count)])
+    def along(value, steps):
+        return lax.ppermute(value, "expert", [(i, i // RING * RING + (i + steps) % RING) for i in range(ex_count)])
+
+    def across(value):
+        return lax.ppermute(value, "expert", [(i, (i + RING) % ex_count) for i in range(ex_count)])
 
     act, slope_a, slope_b, *out_part = kernel_call(
         functools.partial(hidden_kernel, dp_count, ex_count),
         "svv",
-        [("v", shape(BF, total, hidden))] + [("v", shape(BF, total // 2, hidden))] * 2 + [("v", block)] * ex_count,
+        [("v", shape(BF, total, hidden))] + [("v", shape(BF, total // 2, hidden))] * 2 + [("v", shape(BF, 2 * group, width))] * RING,
         2 * big,
         10 * total * hidden,
         vmem=MOST,
@@ -322,33 +342,44 @@
     own_grad, moved_in = kernel_call(
         functools.partial(unpack_kernel, slots), "v", [("v", block), ("v", block)], small, total * width
     )(after(moved, *out_part))
-    grad_blocks = [own_grad] + [to_peer(own_grad, k) for k in range(1, ex_count)]
-    out_blocks = [out_part[0]]
-    for k in range(1, ex_count):
-        out_blocks.append(to_peer(out_part[k], k))
+    out_ring = [out_part[0], along(out_part[1], 1), None, along(out_part[3], 3)]
+    ready = after(own_grad, out_ring[1], out_ring[3])
+    near = [own_grad] + [along(ready, -d) for d in range(1, RING)]
+    other = across(own_grad)
+    far = [other] + [along(after(other, near[1]), -d) for d in range(1, RING)]
+    grad_blocks = near + far
+    out_ring[2] = along(after(out_part[2], *far), 2)
 
     hid, back_part = [], []
-    for h, slope in enumerate((slope_a, slope_b)):
+    for blocks, slope in ((near, slope_a), (far, slope_b)):
         hid_half, *part = kernel_call(
             back_kernel,
             "v" * 7,
-            [("v", shape(BF, total // 2, hidden))] + [("v", block)] * 4,
+            [("v", shape(BF, total // 2, hidden))] + [("v", block)] * RING,
             big,
             5 * total * hidden,
-        )(*grad_blocks[4 * h : 4 * h + 4], slope, w_out, w_in)
+        )(*blocks, slope, w_out, w_in)
         hid.append(hid_half)
-        back_part += part
-    back_blocks = [back_part[0]] + [to_peer(back_part[k], k) for k in range(1, ex_count)]
-
+        back_part.append([part[0]] + [along(part[d], d) for d in range(1, RING)])
+
+    (far_back,) = kernel_call(plane_kernel, "v" * RING, [("v", block)], total * width, total * width)(*back_part[1])
+    far_back = across(far_back)
+    far_out, near_out = kernel_call(
+        plane_kernel, "v" * RING, [("v", block), ("v", shape(F32, group, width))], total * width, 2 * total * width
+    )(*out_ring)
+    far_out = across(far_out)
+
+    other_in = across(after(moved_in, *far))
     (both,) = kernel_call(
         functools.partial(sum_kernel, images),
-        "v" * (2 * ex_count),
+        "v" * (3 + RING),
         [("v", packed_shape)],
         total * width,
         2 * total * width,
-    )(*out_blocks, *back_blocks)
+    )(after(near_out, other_in), far_out, *back_part[0], far_back)
+    in_pair = after(jnp.concatenate([moved_in, other_in], axis=0), both)
+    in_pairs = [in_pair] + [along(in_pair, -d) for d in range(1, RING)]
     moved_both = swap(both)
-    all_in = lax.all_gather(after(moved_in, both), "expert", axis=0, tiled=False)
 
     half = width // 2
     count_rows = 2 * slots // ex_count
@@ -356,9 +387,9 @@
         functools.partial(logits_kernel, ex_count),
         "vrrr",
         [
-            ("v", shape(BF, images, slots, count)),
-            ("v", shape(BF, images, slots, count)),
-            ("v", shape(BF, images, slots, width)),
+            ("h", shape(BF, images, slots, count)),
+            ("h", shape(BF, images, slots, count)),
+            ("h", shape(BF, images, slots, width)),
             ("v", shape(F32, 2 * slots, half)),
         ],
         3 * small,
@@ -373,8 +404,8 @@
         weight_out_kernel, "v" * (ex_count + 1), [("v", shape(BF, hidden, width))], big, 10 * total * hidden
     )(act, *grad_blocks)
     (grad_w_in,) = kernel_call(
-        weight_in_kernel, "svvv", [("v", shape(BF, width, hidden))], big, 10 * total * hidden
-    )(me, all_in, *hid)
+        weight_in_kernel, "v" * (RING + 2), [("v", shape(BF, width, hidden))], big, 10 * total * hidden
+    )(*in_pairs, *hid)
 
     parts = exchange(router_part.reshape(ex_count, count_rows, half), "expert")
     (spread,) = kernel_call(total_kernel, "v", [("v", shape(BF, dp_count, count_rows, half))], small, tokens.nbytes)(parts)

time: 173 us -> 153 us (0.88)
  between operations: 14.4 us -> 1.1 us
  waiting for transfers between devices: 37.6 us -> 32.3 us
  local copies, waits for them, and re-layouts: 6.52 us -> 2.55 us
    ppermute x21 -> x22, waiting for transfers between devices: 22.3 us -> 15.2 us  [the longest x18 9.11 us: along(): lax.ppermute(value, 'expert', [(i, i // RING * RING + (i + steps) % RING)...]
    unnamed x68 -> x64, local copies, waits for them, and re-layouts: 6.52 us -> 2.55 us
    pallas_call x13 -> x15, Pallas kernels: 27.3 us -> 28.1 us  [run(): pl.pallas_call(body, out_shape=tuple((o[1] for o in outputs)), in_specs=[...]
    ppermute x21 -> x22, starting transfers between devices: 31.3 us -> 32 us  [the longest x18 29.3 us: along(): lax.ppermute(value, 'expert', [(i, i // RING * RING + (i + steps) % RING)...]
  transfers between devices with their start and end apart: 25 -> 25, of which waited for: 11 -> 14; matrix products, arithmetic and copies ran while one was open for 0% -> 0% of each run, Pallas kernels for 13% -> 13%
where the time goes in v3:
time: 153 us; the launch traced here: 152 us
  starting transfers between devices  53.2 us (35%)
  blocking collectives  35 us (23%)
  waiting for transfers between devices  32.3 us (21%)
  Pallas kernels  28.1 us (18%)
  local copies, waits for them, and re-layouts  2.55 us (2%)
    all_to_all x2, blocking collectives, exchange(): return lax.all_to_all(blocks, axis, split_axis=0, concat_axis=0, tiled=True)  35 us
    ppermute x18, starting transfers between devices, along(): lax.ppermute(value, 'expert', [(i, i // RING * RING + (i + steps) % RING)...  29.3 us
    pallas_call x15, Pallas kernels, run(): pl.pallas_call(body, out_shape=tuple((o[1] for o in outputs)), in_specs=[...  28.1 us
    all_to_all x3, starting transfers between devices, exchange(): return lax.all_to_all(blocks, axis, split_axis=0, concat_axis=0, tiled=True)  21.2 us
    all_to_all x3, waiting for transfers between devices, exchange(): return lax.all_to_all(blocks, axis, split_axis=0, concat_axis=0, tiled=True)  17 us
    ppermute x18, waiting for transfers between devices, along(): lax.ppermute(value, 'expert', [(i, i // RING * RING + (i + steps) % RING)...  9.11 us
    ppermute x4, waiting for transfers between devices, across(): lax.ppermute(value, 'expert', [(i, (i + RING) % ex_count) for i in range(...  6.13 us
  transfers between devices with their start and end apart: 25, of which 14 were waited for; matrix products, arithmetic and copies ran while one was open for 0% of the time, Pallas kernels for 13%

profile of v3, /device:TPU:1, one launch (start us, length us, event | category | flops | bytes accessed | tf_op | source)
XLA Modules:
  0.0 152.3 jit_solution(16260457147154543630)
XLA Ops:
  0.6 3.1 %shard_map.102 = bf16[256,640]{1,0:T(8,128)(2,1)} custom-call(f32[2,32,256]{2,1,0:T(8,128)} %refs_1_.3, bf16[2,256,1280]{2,1,0:T(8,128)(2,1)} %refs_3_.2, bf16[2,256,1280]{2,1,0:T(8,128)(2,1)} %refs_2_.3), custom_call_target="tpu_custom_call" | custom-call | flops 83886080 | bytes 2621440 | tf_op jit(solution)/shard_map/pallas_call | solution.py:81
  3.7 12.8 %all-to-all-start = ((bf16[32,8,640]{2,1,0:T(8,128)(2,1)}), bf16[32,8,640]{2,1,0:T(8,128)(2,1)}, u32[]{:S(2)}, u32[]{:S(2)}) async-start(bf16[32,8,640]{2,1,0:T(8,128)(2,1)} %bitcast.21), calls=%async_computation | async-start | bytes 655360 | tf_op jit(solution)/shard_map/all_to_all | solution.py:33
  16.6 4.8 %shard_map.103 = (bf16[512,640]{1,0:T(8,128)(2,1)}, bf16[256,640]{1,0:T(8,128)(2,1)}, bf16[256,640]{1,0:T(8,128)(2,1)}, bf16[128,1280]{1,0:T(8,128)(2,1)}, bf16[...) custom-call(s32[1]{0:T(128)} %bitcast.refs_0_, bf16[512,640]{1,0:T(8,128)(2,1)} %bitcast.22, ...), custom_call_target="tpu_custom_call" | custom-call | flops 1677721600 | bytes 3276800 | tf_op jit(solution)/shard_map/pallas_call | solution.py:81
  22.6 1.5 collective-permute-start.2
  24.1 7.3 %all-to-all-done = bf16[32,8,640]{2,1,0:T(8,128)(2,1)} async-done(((bf16[32,8,640]{2,1,0:T(8,128)(2,1)}), bf16[32,8,640]{2,1,0:T(8,128)(2,1)}, u32[]{:S(2)}, u32[]{:S(2)}) %all-to-all-start) | async-done | bytes 327712 | tf_op jit(solution)/shard_map/all_to_all | solution.py:33
  33.7 2.5 %collective-permute-start.3 = (bf16[64,1280]{1,0:T(8,128)(2,1)S(1)}, bf16[64,1280]{1,0:T(8,128)(2,1)S(1)}, u32[]{:S(2)}, u32[]{:S(2)}) collective-permute-start(bf16[64,1280]{1,0:T(8,128)(2,1)S(1)} %get-tuple-element.46.refs_0_.refs_1_), channel_id=1, source_target_pairs={{0,3},{1,0},{2,1},{3,2},{4,7},{5,4},{6,5},{7,6},{8,11},{9,8},{10,9... | collective-permute-start | bytes 491528 | tf_op jit(solution)/shard_map/ppermute | solution.py:329
  36.1 1.9 %collective-permute-done.1.refs_0_.refs_5_ = bf16[64,1280]{1,0:T(8,128)(2,1)S(1)} collective-permute-done((bf16[64,1280]{1,0:T(8,128)(2,1)S(1)}, bf16[64,1280]{1,0:T(8,128)(2,1)S(1)}, u32[]{:S(2)}, u32[]{:S(2)}) %collective-permute-start.1) | collective-permute-done | bytes 163872 | tf_op jit(solution)/shard_map/ppermute | solution.py:332
  40.1 3.7 %collective-permute-start.5 = (bf16[64,1280]{1,0:T(8,128)(2,1)S(1)}, bf16[64,1280]{1,0:T(8,128)(2,1)S(1)}, u32[]{:S(2)}, u32[]{:S(2)}) collective-permute-start(bf16[64,1280]{1,0:T(8,128)(2,1)S(1)} %collective-permute-done.1.refs_0_.refs_5_), channel_id=1, source_target_pairs={{0,2},{1,3},{2,0},{3,1},{4,6},{5,7},{6,4},{7,5},{8,10},{9,11},{10,... | collective-permute-start | bytes 491528 | tf_op jit(solution)/shard_map/ppermute | solution.py:329
  43.7 1.5 collective-permute-start.11
  45.7 4.1 %collective-permute-done.5.refs_2_.refs_7_ = bf16[64,1280]{1,0:T(8,128)(2,1)S(1)} collective-permute-done((bf16[64,1280]{1,0:T(8,128)(2,1)S(1)}, bf16[64,1280]{1,0:T(8,128)(2,1)S(1)}, u32[]{:S(2)}, u32[]{:S(2)}) %collective-permute-start.5) | collective-permute-done | bytes 163872 | tf_op jit(solution)/shard_map/ppermute | solution.py:329
  50.0 1.5 collective-permute-start.7
  51.5 1.5 collective-permute-start.10
  53.9 2.1 %shard_map.107 = (bf16[256,640]{1,0:T(8,128)(2,1)S(1)}, bf16[64,1280]{1,0:T(8,128)(2,1)S(1)}, bf16[64,1280]{1,0:T(8,128)(2,1)S(1)}, bf16[64,1280]{1,0:T(8,128)(2,1)S(1)}, bf16[64,1280]{1,0:T(8,128)(2,1)S(1)}) custom-call(bf16[64,1280]{1,0:T(8,128)(2,1)S(1)} %collective-permute-done.1.refs_0_.refs_5_, ...), custom_call_target="tpu_custom_call" | custom-call | flops 838860800 | bytes 1638400 | tf_op jit(solution)/shard_map/pallas_call | solution.py:81
  56.8 1.9 %collective-permute-start.15 = (bf16[64,1280]{1,0:T(8,128)(2,1)S(1)}, bf16[64,1280]{1,0:T(8,128)(2,1)S(1)}, u32[]{:S(2)}, u32[]{:S(2)}) collective-permute-start(bf16[64,1280]{1,0:T(8,128)(2,1)S(1)} %get-tuple-element.61), channel_id=1, source_target_pairs={{0,1},{1,2},{2,3},{3,0},{4,5},{5,6},{6,7},{7,4},{8,9},{9,10},{10,1... | collective-permute-start | bytes 491528 | tf_op jit(solution)/shard_map/ppermute | solution.py:329
  58.7 2.3 %collective-permute-start.16 = (bf16[64,1280]{1,0:T(8,128)(2,1)S(1)}, bf16[64,1280]{1,0:T(8,128)(2,1)S(1)}, u32[]{:S(2)}, u32[]{:S(2)}) collective-permute-start(bf16[64,1280]{1,0:T(8,128)(2,1)S(1)} %get-tuple-element.62), channel_id=1, source_target_pairs={{0,2},{1,3},{2,0},{3,1},{4,6},{5,7},{6,4},{7,5},{8,10},{9,11},{10,... | collective-permute-start | bytes 491528 | tf_op jit(solution)/shard_map/ppermute | solution.py:329
  62.6 2.1 %shard_map.106 = (bf16[256,640]{1,0:T(8,128)(2,1)S(1)}, bf16[64,1280]{1,0:T(8,128)(2,1)S(1)}, bf16[64,1280]{1,0:T(8,128)(2,1)S(1)}, bf16[64,1280]{1,0:T(8,128)(2,1)S(1)}, bf16[64,1280]{1,0:T(8,128)(2,1)S(1)}) custom-call(bf16[64,1280]{1,0:T(8,128)(2,1)S(1)} %get-tuple-element.46.refs_0_.refs_1_, bf16[64,1280]{1,0:T(8,128)(2,1)S(1)} %collective-permute-done.3.refs_1_.refs_2_, ...), custom_call_target="tpu_custom_call" | custom-call | flops 838860800 | bytes 1638400 | tf_op jit(solution)/shard_map/pallas_call | solution.py:81
  65.9 2.5 %collective-permute-start.12 = (bf16[64,1280]{1,0:T(8,128)(2,1)S(1)}, bf16[64,1280]{1,0:T(8,128)(2,1)S(1)}, u32[]{:S(2)}, u32[]{:S(2)}) collective-permute-start(bf16[64,1280]{1,0:T(8,128)(2,1)S(1)} %get-tuple-element.56), channel_id=1, source_target_pairs={{0,1},{1,2},{2,3},{3,0},{4,5},{5,6},{6,7},{7,4},{8,9},{9,10},{10,1... | collective-permute-start | bytes 491528 | tf_op jit(solution)/shard_map/ppermute | solution.py:329
  69.4 1.6 %collective-permute-start.13 = (bf16[64,1280]{1,0:T(8,128)(2,1)S(1)}, bf16[64,1280]{1,0:T(8,128)(2,1)S(1)}, u32[]{:S(2)}, u32[]{:S(2)}) collective-permute-start(bf16[64,1280]{1,0:T(8,128)(2,1)S(1)} %get-tuple-element.57), channel_id=1, source_target_pairs={{0,2},{1,3},{2,0},{3,1},{4,6},{5,7},{6,4},{7,5},{8,10},{9,11},{10,... | collective-permute-start | bytes 491528 | tf_op jit(solution)/shard_map/ppermute | solution.py:329
  71.5 3.9 %collective-permute-start.14 = (bf16[64,1280]{1,0:T(8,128)(2,1)S(1)}, bf16[64,1280]{1,0:T(8,128)(2,1)S(1)}, u32[]{:S(2)}, u32[]{:S(2)}) collective-permute-start(bf16[64,1280]{1,0:T(8,128)(2,1)S(1)} %get-tuple-element.58), channel_id=1, source_target_pairs={{0,3},{1,0},{2,1},{3,2},{4,7},{5,4},{6,5},{7,6},{8,11},{9,8},{10,9... | collective-permute-start | bytes 491528 | tf_op jit(solution)/shard_map/ppermute | solution.py:329
  78.5 1.6 %collective-permute-done.18.refs_6_ = bf16[64,1280]{1,0:T(8,128)(2,1)S(1)} collective-permute-done((bf16[64,1280]{1,0:T(8,128)(2,1)S(1)}, bf16[64,1280]{1,0:T(8,128)(2,1)S(1)}, u32[]{:S(2)}, u32[]{:S(2)}) %collective-permute-start.18) | collective-permute-done | bytes 163872 | tf_op jit(solution)/shard_map/ppermute | solution.py:332
  80.1 2.6 %collective-permute-done.9.refs_1_ = bf16[64,1280]{1,0:T(8,128)(2,1)S(1)} collective-permute-done((bf16[64,1280]{1,0:T(8,128)(2,1)S(1)}, bf16[64,1280]{1,0:T(8,128)(2,1)S(1)}, u32[]{:S(2)}, u32[]{:S(2)}) %collective-permute-start.9) | collective-permute-done | bytes 163872 | tf_op jit(solution)/shard_map/ppermute | solution.py:332
  83.1 24.8 %all_to_all.25 = bf16[32,8,640]{2,1,0:T(8,128)(2,1)S(1)} all-to-all(bf16[32,8,640]{2,1,0:T(8,128)(2,1)S(1)} %bitcast.17), channel_id=1, replica_groups=mesh['dp'=32,'expert'=8] {'dp'}, dimensions={0} | all-to-all | bytes 655360 | tf_op jit(solution)/shard_map/all_to_all | solution.py:33
  107.9 3.2 %shard_map.110 = (bf16[2,32,256]{2,1,0:T(8,128)(2,1)S(1)}, bf16[2,32,256]{2,1,0:T(8,128)(2,1)S(1)}, bf16[2,32,1280]{2,1,0:T(8,128)(2,1)S(1)}, f32[64,640]{1,0:T(8,128)S(1)}) custom-call(bf16[256,640]{1,0:T(8,128)(2,1)S(1)} %bitcast.16, f32[2,32,256]{2,1,0:T(8,128)S(1)} %copy-done.26, bf16[2,256,1280]{2,1,0:T(8,128)(2,1)S(1)} %copy-done.3, ...), custom_call_target="tpu_custom_call" | custom-call | flops 125829120 | bytes 2621440 | tf_op jit(solution)/shard_map/pallas_call | solution.py:81
  111.2 10.2 %all_to_all.26.refs_0_ = f32[8,8,640]{2,1,0:T(8,128)S(1)} all-to-all(f32[8,8,640]{2,1,0:T(8,128)S(1)} %bitcast.18), channel_id=1, replica_groups=mesh['dp'=32,'expert'=8] {'expert'}, dimensions={0} | all-to-all | bytes 327680 | tf_op jit(solution)/shard_map/all_to_all | solution.py:33
  122.2 5.0 %all-to-all-start.3 = ((bf16[32,8,640]{2,1,0:T(8,128)(2,1)}), bf16[32,8,640]{2,1,0:T(8,128)(2,1)S(1)}, u32[]{:S(2)}, u32[]{:S(2)}) async-start(bf16[32,8,640]{2,1,0:T(8,128)(2,1)} %shard_map.112), calls=%async_computation.3 | async-start | bytes 655360 | tf_op jit(solution)/shard_map/all_to_all | solution.py:33
  127.5 1.8 %collective-permute-start.20 = (bf16[128,1280]{1,0:T(8,128)(2,1)S(1)}, bf16[128,1280]{1,0:T(8,128)(2,1)S(1)}, u32[]{:S(2)}, u32[]{:S(2)}) collective-permute-start(bf16[128,1280]{1,0:T(8,128)(2,1)S(1)} %pad_maximum_fusion.refs_0_), channel_id=1, source_target_pairs={{0,2},{1,3},{2,0},{3,1},{4,6},{5,7},{6,4},{7,5},{8,10},{9,11},{10,... | collective-permute-start | bytes 983048 | tf_op jit(solution)/shard_map/ppermute | solution.py:329
  130.2 2.2 %shard_map.113 = bf16[640,1280]{1,0:T(8,128)(2,1)} custom-call(bf16[512,640]{1,0:T(8,128)(2,1)S(1)} %copy-done.18, bf16[64,1280]{1,0:T(8,128)(2,1)S(1)} %get-tuple-element.46.refs_0_.refs_1_, bf16[64,1280]{1,0:T(8,128)(2,1)S(1)} %copy-done.7, bf16[64,1280]{1,0:T(8,128)(2,1)S(1)} %copy-done.17, bf16[64,1280]{1,0:T(8,128)(2,1)S(1)} %copy-done.15, ...), custom_call_target="tpu_custom_call" | custom-call | flops 838860800 | bytes 3276800 | tf_op jit(solution)/shard_map/pallas_call | solution.py:81
  132.4 1.9 %shard_map.111 = bf16[2,256,1280]{2,1,0:T(8,128)(2,1)} custom-call(bf16[2,32,256]{2,1,0:T(8,128)(2,1)S(1)} %get-tuple-element.64.refs_0_, bf16[2,32,256]{2,1,0:T(8,128)(2,1)S(1)} %get-tuple-element.65.refs_1_, bf16[2,32,1280]{2,1,0:T(8,128)(2,1)S(1)} %get-tuple-element.66.refs_2_, bf16[32,1280]{1,0:T(8,128)(2,1)S(1)} %copy-done.29), custom_call_target="tpu_custom_call" | custom-call | flops 83886080 | bytes 1310720 | tf_op jit(solution)/shard_map/pallas_call | solution.py:81
  134.3 7.5 %all-to-all-done.3.refs_0_ = bf16[32,8,640]{2,1,0:T(8,128)(2,1)S(1)} async-done(((bf16[32,8,640]{2,1,0:T(8,128)(2,1)}), bf16[32,8,640]{2,1,0:T(8,128)(2,1)S(1)}, u32[]{:S(2)}, u32[]{:S(2)}) %all-to-all-start.3) | async-done | bytes 327712 | tf_op jit(solution)/shard_map/all_to_all | solution.py:33
  142.5 3.4 %all-to-all-start.4 = ((f32[8,8,640]{2,1,0:T(8,128)}), f32[8,8,640]{2,1,0:T(8,128)S(1)}, u32[]{:S(2)}, u32[]{:S(2)}) async-start(f32[8,8,640]{2,1,0:T(8,128)} %shard_map.114), calls=%async_computation.4 | async-start | bytes 327680 | tf_op jit(solution)/shard_map/all_to_all | solution.py:33
  146.0 3.4 %shard_map.115 = bf16[1280,640]{1,0:T(8,128)(2,1)} custom-call(bf16[128,1280]{1,0:T(8,128)(2,1)S(1)} %pad_maximum_fusion.refs_0_, bf16[128,1280]{1,0:T(8,128)(2,1)} %collective-permute-done.19.refs_1_, bf16[128,1280]{1,0:T(8,128)(2,1)S(1)} %collective-permute-done.20.refs_2_, bf16[128,1280]{1,0:T(8,128)(2,1)S(1)} %collective-permute-done.21.refs_3_, ...), custom_call_target="tpu_custom_call" | custom-call | flops 838860800 | bytes 3276800 | tf_op jit(solution)/shard_map/pallas_call | solution.py:81
  149.3 2.2 %all-to-all-done.4.refs_0_ = f32[8,8,640]{2,1,0:T(8,128)S(1)} async-done(((f32[8,8,640]{2,1,0:T(8,128)}), f32[8,8,640]{2,1,0:T(8,128)S(1)}, u32[]{:S(2)}, u32[]{:S(2)}) %all-to-all-start.4) | async-done | bytes 163872 | tf_op jit(solution)/shard_map/all_to_all | solution.py:33
  (100 shorter events, 18.7 us)
Async XLA Ops:
  3.7 27.6 %all-to-all-start = ((bf16[32,8,640]{2,1,0:T(8,128)(2,1)}), bf16[32,8,640]{2,1,0:T(8,128)(2,1)}, u32[]{:S(2)}, u32[]{:S(2)}) async-start(bf16[32,8,640]{2,1,0:T(8,128)(2,1)} %bitcast.21), calls=%async_computation | async-start | bytes 655360 | tf_op jit(solution)/shard_map/all_to_all | solution.py:33
  16.5 36.4 %copy-start = (bf16[1,640,1280]{2,1,0:T(8,128)(2,1)S(1)}, bf16[1,640,1280]{2,1,0:T(8,128)(2,1)}, u32[]{:S(2)}) copy-start(bf16[1,640,1280]{2,1,0:T(8,128)(2,1)} %param.13) | copy-start | bytes 4915204
  16.6 36.4 %copy-start.1 = (bf16[1,1280,640]{2,1,0:T(8,128)(2,1)S(1)}, bf16[1,1280,640]{2,1,0:T(8,128)(2,1)}, u32[]{:S(2)}) copy-start(bf16[1,1280,640]{2,1,0:T(8,128)(2,1)} %param.12) | copy-start | bytes 4915204
  21.4 12.3 %collective-permute-start = (bf16[128,1280]{1,0:T(8,128)(2,1)}, bf16[128,1280]{1,0:T(8,128)(2,1)}, u32[]{:S(2)}, u32[]{:S(2)}) collective-permute-start(bf16[128,1280]{1,0:T(8,128)(2,1)} %get-tuple-element.41), channel_id=1, source_target_pairs={{0,1},{1,2},{2,3},{3,0},{4,5},{5,6},{6,7},{7,4},{8,9},{9,10},{10,1... | collective-permute-start | bytes 983048 | tf_op jit(solution)/shard_map/ppermute | solution.py:329
  22.6 11.1 %collective-permute-start.2 = (bf16[128,1280]{1,0:T(8,128)(2,1)}, bf16[128,1280]{1,0:T(8,128)(2,1)}, u32[]{:S(2)}, u32[]{:S(2)}) collective-permute-start(bf16[128,1280]{1,0:T(8,128)(2,1)} %get-tuple-element.43), channel_id=1, source_target_pairs={{0,3},{1,0},{2,1},{3,2},{4,7},{5,4},{6,5},{7,6},{8,11},{9,8},{10,9... | collective-permute-start | bytes 983048 | tf_op jit(solution)/shard_map/ppermute | solution.py:329
  32.6 29.8 %copy-start.27 = (bf16[64,1280]{1,0:T(8,128)(2,1)}, bf16[64,1280]{1,0:T(8,128)(2,1)S(1)}, u32[]{:S(2)}) copy-start(bf16[64,1280]{1,0:T(8,128)(2,1)S(1)} %get-tuple-element.51) | copy-start | bytes 491524
  32.6 5.4 %collective-permute-start.1 = (bf16[64,1280]{1,0:T(8,128)(2,1)S(1)}, bf16[64,1280]{1,0:T(8,128)(2,1)S(1)}, u32[]{:S(2)}, u32[]{:S(2)}) collective-permute-start(bf16[64,1280]{1,0:T(8,128)(2,1)S(1)} %get-tuple-element.46.refs_0_.refs_1_), channel_id=1, source_target_pairs={{0,4},{1,5},{2,6},{3,7},{4,0},{5,1},{6,2},{7,3},{8,12},{9,13},{10,... | collective-permute-start | bytes 491528 | tf_op jit(solution)/shard_map/ppermute | solution.py:332
  33.7 5.5 %collective-permute-start.3 = (bf16[64,1280]{1,0:T(8,128)(2,1)S(1)}, bf16[64,1280]{1,0:T(8,128)(2,1)S(1)}, u32[]{:S(2)}, u32[]{:S(2)}) collective-permute-start(bf16[64,1280]{1,0:T(8,128)(2,1)S(1)} %get-tuple-element.46.refs_0_.refs_1_), channel_id=1, source_target_pairs={{0,3},{1,0},{2,1},{3,2},{4,7},{5,4},{6,5},{7,6},{8,11},{9,8},{10,9... | collective-permute-start | bytes 491528 | tf_op jit(solution)/shard_map/ppermute | solution.py:329
  39.2 6.5 %collective-permute-start.6 = (bf16[64,1280]{1,0:T(8,128)(2,1)S(1)}, bf16[64,1280]{1,0:T(8,128)(2,1)S(1)}, u32[]{:S(2)}, u32[]{:S(2)}) collective-permute-start(bf16[64,1280]{1,0:T(8,128)(2,1)S(1)} %collective-permute-done.1.refs_0_.refs_5_), channel_id=1, source_target_pairs={{0,1},{1,2},{2,3},{3,0},{4,5},{5,6},{6,7},{7,4},{8,9},{9,10},{10,1... | collective-permute-start | bytes 491528 | tf_op jit(solution)/shard_map/ppermute | solution.py:329
  40.1 9.7 %collective-permute-start.5 = (bf16[64,1280]{1,0:T(8,128)(2,1)S(1)}, bf16[64,1280]{1,0:T(8,128)(2,1)S(1)}, u32[]{:S(2)}, u32[]{:S(2)}) collective-permute-start(bf16[64,1280]{1,0:T(8,128)(2,1)S(1)} %collective-permute-done.1.refs_0_.refs_5_), channel_id=1, source_target_pairs={{0,2},{1,3},{2,0},{3,1},{4,6},{5,7},{6,4},{7,5},{8,10},{9,11},{10,... | collective-permute-start | bytes 491528 | tf_op jit(solution)/shard_map/ppermute | solution.py:329
  43.7 6.2 %collective-permute-start.4 = (bf16[64,1280]{1,0:T(8,128)(2,1)S(1)}, bf16[64,1280]{1,0:T(8,128)(2,1)S(1)}, u32[]{:S(2)}, u32[]{:S(2)}) collective-permute-start(bf16[64,1280]{1,0:T(8,128)(2,1)S(1)} %collective-permute-done.1.refs_0_.refs_5_), channel_id=1, source_target_pairs={{0,3},{1,0},{2,1},{3,2},{4,7},{5,4},{6,5},{7,6},{8,11},{9,8},{10,9... | collective-permute-start | bytes 491528 | tf_op jit(solution)/shard_map/ppermute | solution.py:329
  43.7 17.3 %collective-permute-start.11 = (bf16[64,1280]{1,0:T(8,128)(2,1)S(1)}, bf16[64,1280]{1,0:T(8,128)(2,1)S(1)}, u32[]{:S(2)}, u32[]{:S(2)}) collective-permute-start(bf16[64,1280]{1,0:T(8,128)(2,1)S(1)} %get-tuple-element.46.refs_0_.refs_1_), channel_id=1, source_target_pairs={{0,1},{1,2},{2,3},{3,0},{4,5},{5,6},{6,7},{7,4},{8,9},{9,10},{10,1... | collective-permute-start | bytes 491528 | tf_op jit(solution)/shard_map/ppermute | solution.py:329
  50.0 25.6 %collective-permute-start.7 = (bf16[128,1280]{1,0:T(8,128)(2,1)}, bf16[128,1280]{1,0:T(8,128)(2,1)S(1)}, u32[]{:S(2)}, u32[]{:S(2)}) collective-permute-start(bf16[128,1280]{1,0:T(8,128)(2,1)} %get-tuple-element.48), channel_id=1, source_target_pairs={{0,2},{1,3},{2,0},{3,1},{4,6},{5,7},{6,4},{7,5},{8,10},{9,11},{10,... | collective-permute-start | bytes 983048 | tf_op jit(solution)/shard_map/ppermute | solution.py:329
  51.5 10.9 %collective-permute-start.10 = (bf16[64,1280]{1,0:T(8,128)(2,1)S(1)}, bf16[64,1280]{1,0:T(8,128)(2,1)S(1)}, u32[]{:S(2)}, u32[]{:S(2)}) collective-permute-start(bf16[64,1280]{1,0:T(8,128)(2,1)S(1)} %get-tuple-element.46.refs_0_.refs_1_), channel_id=1, source_target_pairs={{0,2},{1,3},{2,0},{3,1},{4,6},{5,7},{6,4},{7,5},{8,10},{9,11},{10,... | collective-permute-start | bytes 491528 | tf_op jit(solution)/shard_map/ppermute | solution.py:329
  56.8 9.1 %collective-permute-start.15 = (bf16[64,1280]{1,0:T(8,128)(2,1)S(1)}, bf16[64,1280]{1,0:T(8,128)(2,1)S(1)}, u32[]{:S(2)}, u32[]{:S(2)}) collective-permute-start(bf16[64,1280]{1,0:T(8,128)(2,1)S(1)} %get-tuple-element.61), channel_id=1, source_target_pairs={{0,1},{1,2},{2,3},{3,0},{4,5},{5,6},{6,7},{7,4},{8,9},{9,10},{10,1... | collective-permute-start | bytes 491528 | tf_op jit(solution)/shard_map/ppermute | solution.py:329
  58.7 10.7 %collective-permute-start.16 = (bf16[64,1280]{1,0:T(8,128)(2,1)S(1)}, bf16[64,1280]{1,0:T(8,128)(2,1)S(1)}, u32[]{:S(2)}, u32[]{:S(2)}) collective-permute-start(bf16[64,1280]{1,0:T(8,128)(2,1)S(1)} %get-tuple-element.62), channel_id=1, source_target_pairs={{0,2},{1,3},{2,0},{3,1},{4,6},{5,7},{6,4},{7,5},{8,10},{9,11},{10,... | collective-permute-start | bytes 491528 | tf_op jit(solution)/shard_map/ppermute | solution.py:329
  61.1 10.5 %collective-permute-start.17 = (bf16[64,1280]{1,0:T(8,128)(2,1)S(1)}, bf16[64,1280]{1,0:T(8,128)(2,1)S(1)}, u32[]{:S(2)}, u32[]{:S(2)}) collective-permute-start(bf16[64,1280]{1,0:T(8,128)(2,1)S(1)} %get-tuple-element.63), channel_id=1, source_target_pairs={{0,3},{1,0},{2,1},{3,2},{4,7},{5,4},{6,5},{7,6},{8,11},{9,8},{10,9... | collective-permute-start | bytes 491528 | tf_op jit(solution)/shard_map/ppermute | solution.py:329
  62.4 14.7 %collective-permute-start.8 = (bf16[64,1280]{1,0:T(8,128)(2,1)S(1)}, bf16[64,1280]{1,0:T(8,128)(2,1)S(1)}, u32[]{:S(2)}, u32[]{:S(2)}) collective-permute-start(bf16[64,1280]{1,0:T(8,128)(2,1)S(1)} %get-tuple-element.51), channel_id=1, source_target_pairs={{0,4},{1,5},{2,6},{3,7},{4,0},{5,1},{6,2},{7,3},{8,12},{9,13},{10,... | collective-permute-start | bytes 491528 | tf_op jit(solution)/shard_map/ppermute | solution.py:332
  65.9 12.6 %collective-permute-start.12 = (bf16[64,1280]{1,0:T(8,128)(2,1)S(1)}, bf16[64,1280]{1,0:T(8,128)(2,1)S(1)}, u32[]{:S(2)}, u32[]{:S(2)}) collective-permute-start(bf16[64,1280]{1,0:T(8,128)(2,1)S(1)} %get-tuple-element.56), channel_id=1, source_target_pairs={{0,1},{1,2},{2,3},{3,0},{4,5},{5,6},{6,7},{7,4},{8,9},{9,10},{10,1... | collective-permute-start | bytes 491528 | tf_op jit(solution)/shard_map/ppermute | solution.py:329
  69.4 9.1 %collective-permute-start.13 = (bf16[64,1280]{1,0:T(8,128)(2,1)S(1)}, bf16[64,1280]{1,0:T(8,128)(2,1)S(1)}, u32[]{:S(2)}, u32[]{:S(2)}) collective-permute-start(bf16[64,1280]{1,0:T(8,128)(2,1)S(1)} %get-tuple-element.57), channel_id=1, source_target_pairs={{0,2},{1,3},{2,0},{3,1},{4,6},{5,7},{6,4},{7,5},{8,10},{9,11},{10,... | collective-permute-start | bytes 491528 | tf_op jit(solution)/shard_map/ppermute | solution.py:329
  71.5 6.9 %collective-permute-start.14 = (bf16[64,1280]{1,0:T(8,128)(2,1)S(1)}, bf16[64,1280]{1,0:T(8,128)(2,1)S(1)}, u32[]{:S(2)}, u32[]{:S(2)}) collective-permute-start(bf16[64,1280]{1,0:T(8,128)(2,1)S(1)} %get-tuple-element.58), channel_id=1, source_target_pairs={{0,3},{1,0},{2,1},{3,2},{4,7},{5,4},{6,5},{7,6},{8,11},{9,8},{10,9... | collective-permute-start | bytes 491528 | tf_op jit(solution)/shard_map/ppermute | solution.py:329
  75.5 32.4 %copy-start.2 = (bf16[2,256,1280]{2,1,0:T(8,128)(2,1)S(1)}, bf16[2,256,1280]{2,1,0:T(8,128)(2,1)}, u32[]{:S(2)}) copy-start(bf16[2,256,1280]{2,1,0:T(8,128)(2,1)} %refs_3_.2) | copy-start | bytes 3932164
  75.5 32.3 %copy-start.3 = (bf16[2,256,1280]{2,1,0:T(8,128)(2,1)S(1)}, bf16[2,256,1280]{2,1,0:T(8,128)(2,1)}, u32[]{:S(2)}) copy-start(bf16[2,256,1280]{2,1,0:T(8,128)(2,1)} %refs_2_.3) | copy-start | bytes 3932164
  75.6 32.3 %copy-start.26 = (f32[2,32,256]{2,1,0:T(8,128)S(1)}, f32[2,32,256]{2,1,0:T(8,128)}, u32[]{:S(2)}) copy-start(f32[2,32,256]{2,1,0:T(8,128)} %refs_1_.3) | copy-start | bytes 196612
  75.6 4.6 %collective-permute-start.18 = (bf16[64,1280]{1,0:T(8,128)(2,1)S(1)}, bf16[64,1280]{1,0:T(8,128)(2,1)S(1)}, u32[]{:S(2)}, u32[]{:S(2)}) collective-permute-start(bf16[64,1280]{1,0:T(8,128)(2,1)S(1)} %shard_map.108), channel_id=1, source_target_pairs={{0,4},{1,5},{2,6},{3,7},{4,0},{5,1},{6,2},{7,3},{8,12},{9,13},{10,... | collective-permute-start | bytes 491528 | tf_op jit(solution)/shard_map/ppermute | solution.py:332
  77.1 30.8 %copy-start.30 = (bf16[64,1280]{1,0:T(8,128)(2,1)}, bf16[64,1280]{1,0:T(8,128)(2,1)S(1)}, u32[]{:S(2)}) copy-start(bf16[64,1280]{1,0:T(8,128)(2,1)S(1)} %collective-permute-done.8) | copy-start | bytes 491524
  77.1 5.7 %collective-permute-start.9 = (bf16[64,1280]{1,0:T(8,128)(2,1)S(1)}, bf16[64,1280]{1,0:T(8,128)(2,1)S(1)}, u32[]{:S(2)}, u32[]{:S(2)}) collective-permute-start(bf16[64,1280]{1,0:T(8,128)(2,1)S(1)} %get-tuple-element.53), channel_id=1, source_target_pairs={{0,4},{1,5},{2,6},{3,7},{4,0},{5,1},{6,2},{7,3},{8,12},{9,13},{10,... | collective-permute-start | bytes 491528 | tf_op jit(solution)/shard_map/ppermute | solution.py:332
  122.2 19.6 %all-to-all-start.3 = ((bf16[32,8,640]{2,1,0:T(8,128)(2,1)}), bf16[32,8,640]{2,1,0:T(8,128)(2,1)S(1)}, u32[]{:S(2)}, u32[]{:S(2)}) async-start(bf16[32,8,640]{2,1,0:T(8,128)(2,1)} %shard_map.112), calls=%async_computation.3 | async-start | bytes 655360 | tf_op jit(solution)/shard_map/all_to_all | solution.py:33
  127.3 18.6 %collective-permute-start.21 = (bf16[128,1280]{1,0:T(8,128)(2,1)S(1)}, bf16[128,1280]{1,0:T(8,128)(2,1)S(1)}, u32[]{:S(2)}, u32[]{:S(2)}) collective-permute-start(bf16[128,1280]{1,0:T(8,128)(2,1)S(1)} %pad_maximum_fusion.refs_0_), channel_id=1, source_target_pairs={{0,1},{1,2},{2,3},{3,0},{4,5},{5,6},{6,7},{7,4},{8,9},{9,10},{10,1... | collective-permute-start | bytes 983048 | tf_op jit(solution)/shard_map/ppermute | solution.py:329
  127.5 18.4 %collective-permute-start.20 = (bf16[128,1280]{1,0:T(8,128)(2,1)S(1)}, bf16[128,1280]{1,0:T(8,128)(2,1)S(1)}, u32[]{:S(2)}, u32[]{:S(2)}) collective-permute-start(bf16[128,1280]{1,0:T(8,128)(2,1)S(1)} %pad_maximum_fusion.refs_0_), channel_id=1, source_target_pairs={{0,2},{1,3},{2,0},{3,1},{4,6},{5,7},{6,4},{7,5},{8,10},{9,11},{10,... | collective-permute-start | bytes 983048 | tf_op jit(solution)/shard_map/ppermute | solution.py:329
  129.3 16.6 %collective-permute-start.19 = (bf16[128,1280]{1,0:T(8,128)(2,1)S(1)}, bf16[128,1280]{1,0:T(8,128)(2,1)}, u32[]{:S(2)}, u32[]{:S(2)}) collective-permute-start(bf16[128,1280]{1,0:T(8,128)(2,1)S(1)} %pad_maximum_fusion.refs_0_), channel_id=1, source_target_pairs={{0,3},{1,0},{2,1},{3,2},{4,7},{5,4},{6,5},{7,6},{8,11},{9,8},{10,9... | collective-permute-start | bytes 983048 | tf_op jit(solution)/shard_map/ppermute | solution.py:329
  142.5 9.0 %all-to-all-start.4 = ((f32[8,8,640]{2,1,0:T(8,128)}), f32[8,8,640]{2,1,0:T(8,128)S(1)}, u32[]{:S(2)}, u32[]{:S(2)}) async-start(f32[8,8,640]{2,1,0:T(8,128)} %shard_map.114), calls=%async_computation.4 | async-start | bytes 327680 | tf_op jit(solution)/shard_map/all_to_all | solution.py:33
  (25 other events, 314.1 us)

commit v4 on v3

--- a/solution.py
+++ b/solution.py
@@ -11,7 +11,9 @@
 F32 = jnp.float32
 MIB = 1024 * 1024
 MOST = 60 * MIB
+LANES = 384
 RING = 4
+ORDER = (0, 1, 3, 2)
 
 
 def gelu_slope(value):
@@ -149,10 +151,9 @@
     group = dp_count * images
     block = 2 * group
     me = me_ref[0]
-    for c in range(total // block):
-        at = lax.broadcasted_iota(jnp.int32, (block, total), 0) + c * block
-        row = at // group
-        owner = (row + me) % RING + RING * ((row // RING + me // RING) % 2)
+    for c, steps in enumerate(ORDER):
+        at = lax.broadcasted_iota(jnp.int32, (block, total), 0)
+        owner = (steps + me) % RING + RING * ((at // group + me // RING) % 2)
         source = (at % dp_count) * (ex_count * images) + owner * images + (at // dp_count) % images
         pick = (source == lax.broadcasted_iota(jnp.int32, (block, total), 1)).astype(BF)
         pre = dot(pick, fc1_ref[...], ((1,), (0,)))
@@ -160,24 +161,30 @@
         density = jnp.exp(-0.5 * pre * pre) * 0.3989422804014327
         act = (pre * cdf).astype(BF)
         act_ref[c * block : (c + 1) * block, :] = act
-        slope_refs[c // 2][(c % 2) * block : (c % 2 + 1) * block, :] = (cdf + pre * density).astype(BF)
-        out = dot(act, w_ref[...], ((1,), (0,))).astype(BF)
-        for h in range(2):
-            far, step = (2 * c + h) // RING, (2 * c + h) % RING
-            out_refs[step][far * group : (far + 1) * group, :] = out[h * group : (h + 1) * group]
+        slope = (cdf + pre * density).astype(BF)
+        if c < RING - 1:
+            slope_refs[0][c * block : (c + 1) * block, :] = slope
+        else:
+            slope_refs[1][...] = slope
+        out_refs[c][...] = dot(act, w_ref[...], ((1,), (0,))).astype(BF)
 
 
 def back_kernel(*refs):
-    blocks, (slope_ref, w_out_ref, w_in_ref, hid_ref), outs = refs[:4], refs[4:8], refs[8:]
-    group = blocks[0].shape[0]
-    for c in range(0, 4, 2):
-        rows = slice(c * group, (c + 2) * group)
-        grad = jnp.concatenate([blocks[c][...], blocks[c + 1][...]], axis=0)
-        hid = (dot(grad, w_out_ref[...], ((1,), (1,))) * slope_ref[rows, :].astype(F32)).astype(BF)
+    count = (len(refs) - 4) // 2
+    blocks, (slope_ref, w_out_ref, w_in_ref, hid_ref), outs = refs[:count], refs[count : count + 4], refs[count + 4 :]
+    block = blocks[0].shape[0]
+    for c in range(count):
+        rows = slice(c * block, (c + 1) * block)
+        grad = dot(blocks[c][...], w_out_ref[...], ((1,), (1,)))
+        hid = (grad * slope_ref[rows, :].astype(F32)).astype(BF)
         hid_ref[rows, :] = hid
-        back = dot(hid, w_in_ref[...], ((1,), (1,))).astype(BF)
-        outs[c][...] = back[:group]
-        outs[c + 1][...] = back[group:]
+        outs[c][...] = dot(hid, w_in_ref[...], ((1,), (1,))).astype(BF)
+
+
+def join_kernel(a_ref, b_ref, out_ref):
+    group = a_ref.shape[0]
+    out_ref[:group, :] = a_ref[...]
+    out_ref[group:, :] = b_ref[...]
 
 
 def weight_out_kernel(act_ref, *refs):
@@ -189,8 +196,7 @@
 
 def weight_in_kernel(*refs):
     pairs, hid_refs, out_ref = refs[:RING], refs[RING : RING + 2], refs[-1]
-    group = pairs[0].shape[0] // 2
-    rows = jnp.concatenate([r[z * group : (z + 1) * group, :] for z in range(2) for r in pairs], axis=0)
+    rows = jnp.concatenate([r[...] for r in pairs], axis=0)
     hid = jnp.concatenate([r[...] for r in hid_refs], axis=0)
     for c in range(0, rows.shape[1], 256):
         cols = slice(c, c + 256)
@@ -207,18 +213,17 @@
 
 
 def plane_kernel(*refs):
-    far_ref, group = refs[4], refs[4].shape[0]
-    both = refs[0].shape[0] > group
+    near_ref, far_ref = refs[RING:]
+    group = far_ref.shape[0]
 
     def add(rows):
         total = refs[0][rows, :].astype(F32)
-        for ref in refs[1:4]:
+        for ref in refs[1:RING]:
             total = total + ref[rows, :].astype(F32)
         return total
 
-    far_ref[...] = add(slice(group, 2 * group) if both else slice(0, group)).astype(BF)
-    if both:
-        refs[5][...] = add(slice(0, group))
+    near_ref[...] = add(slice(0, group))
+    far_ref[...] = add(slice(group, 2 * group)).astype(BF)
 
 
 def sum_kernel(images, *refs):
@@ -261,11 +266,20 @@
         grad_ref[b] = logit_grad
         parts.append(dot(logit_grad, tokens[b], ((1,), (0,))))
     part = sum(parts[1:], parts[0])
-    count, half = slots // owners, part.shape[1] // 2
-    for k in range(owners):
-        for h in range(2):
-            at = (2 * k + h) * count
-            router_ref[at : at + count, :] = part[k * count : (k + 1) * count, h * half : (h + 1) * half]
+    for p in range(owners):
+        for at, slot, lanes in pieces(slots // owners, part.shape[1]):
+            router_ref[p, at : at + 1, : lanes.stop - lanes.start] = part[p * slots // owners + slot][None, lanes]
+            if lanes.stop - lanes.start < router_ref.shape[2]:
+                router_ref[p, at : at + 1, lanes.stop - lanes.start :] = jnp.zeros(
+                    (1, router_ref.shape[2] - lanes.stop + lanes.start), F32
+                )
+
+
+def pieces(count, width):
+    each = -(-width // LANES)
+    return [
+        (slot * each + q, slot, slice(q * LANES, min(width, (q + 1) * LANES))) for slot in range(count) for q in range(each)
+    ]
 
 
 def total_kernel(parts_ref, out_ref):
@@ -278,11 +292,11 @@
 
 
 def rows_kernel(parts_ref, out_ref):
-    owners, count, half = parts_ref.shape
-    count = count // 2
-    for k in range(owners):
-        for h in range(2):
-            out_ref[k * count : (k + 1) * count, h * half : (h + 1) * half] = parts_ref[k, h * count : (h + 1) * count, :]
+    count = out_ref.shape[0] // parts_ref.shape[0]
+    for p in range(parts_ref.shape[0]):
+        for at, slot, lanes in pieces(count, out_ref.shape[1]):
+            row = p * count + slot
+            out_ref[row : row + 1, lanes] = parts_ref[p, at : at + 1, : lanes.stop - lanes.start]
 
 
 def tokens_kernel(disp_ref, grad_ref, back_ref, router_ref, out_ref):
@@ -324,6 +338,7 @@
     big = 2 * total * width * hidden
     me = lax.axis_index("expert").astype(jnp.int32).reshape(1)
     block = shape(BF, group, width)
+    pair = 2 * group
 
     def along(value, steps):
         return lax.ppermute(value, "expert", [(i, i // RING * RING + (i + steps) % RING) for i in range(ex_count)])
@@ -334,7 +349,8 @@
     act, slope_a, slope_b, *out_part = kernel_call(
         functools.partial(hidden_kernel, dp_count, ex_count),
         "svv",
-        [("v", shape(BF, total, hidden))] + [("v", shape(BF, total // 2, hidden))] * 2 + [("v", shape(BF, 2 * group, width))] * RING,
+        [("v", shape(BF, total, hidden)), ("v", shape(BF, total - pair, hidden)), ("v", shape(BF, pair, hidden))]
+        + [("v", shape(BF, pair, width))] * RING,
         2 * big,
         10 * total * hidden,
         vmem=MOST,
@@ -342,55 +358,54 @@
     own_grad, moved_in = kernel_call(
         functools.partial(unpack_kernel, slots), "v", [("v", block), ("v", block)], small, total * width
     )(after(moved, *out_part))
-    out_ring = [out_part[0], along(out_part[1], 1), None, along(out_part[3], 3)]
-    ready = after(own_grad, out_ring[1], out_ring[3])
-    near = [own_grad] + [along(ready, -d) for d in range(1, RING)]
-    other = across(own_grad)
-    far = [other] + [along(after(other, near[1]), -d) for d in range(1, RING)]
-    grad_blocks = near + far
-    out_ring[2] = along(after(out_part[2], *far), 2)
-
-    hid, back_part = [], []
-    for blocks, slope in ((near, slope_a), (far, slope_b)):
-        hid_half, *part = kernel_call(
+    def joined(value, other):
+        return kernel_call(join_kernel, "vv", [("v", shape(BF, pair, width))], pair * width, 4 * pair * width)(value, other)[0]
+
+    def plane_sum(blocks):
+        near, far = kernel_call(
+            plane_kernel, "v" * RING, [("v", shape(F32, group, width)), ("v", block)], total * width, 2 * total * width
+        )(*blocks)
+        return near, across(far)
+
+    out_ring = [out_part[0]] + [along(out_part[c], ORDER[c]) for c in range(1, RING - 1)]
+    mine = joined(after(own_grad, *out_ring), across(own_grad))
+    grads = [mine] + [along(mine, -steps) for steps in ORDER[1:]]
+    out_ring.append(along(after(out_part[RING - 1], *grads), ORDER[RING - 1]))
+
+    hid, back_ring = [], []
+    for first, last, slope in ((0, RING - 1, slope_a), (RING - 1, RING, slope_b)):
+        hid_rows, *part = kernel_call(
             back_kernel,
-            "v" * 7,
-            [("v", shape(BF, total // 2, hidden))] + [("v", block)] * RING,
-            big,
+            "v" * (last - first + 3),
+            [("v", shape(BF, pair * (last - first), hidden))] + [("v", shape(BF, pair, width))] * (last - first),
+            2 * big * (last - first) // RING,
             5 * total * hidden,
-        )(*blocks, slope, w_out, w_in)
-        hid.append(hid_half)
-        back_part.append([part[0]] + [along(part[d], d) for d in range(1, RING)])
-
-    (far_back,) = kernel_call(plane_kernel, "v" * RING, [("v", block)], total * width, total * width)(*back_part[1])
-    far_back = across(far_back)
-    far_out, near_out = kernel_call(
-        plane_kernel, "v" * RING, [("v", block), ("v", shape(F32, group, width))], total * width, 2 * total * width
-    )(*out_ring)
-    far_out = across(far_out)
-
-    other_in = across(after(moved_in, *far))
+        )(*grads[first:last], slope, w_out, w_in)
+        hid.append(hid_rows)
+        back_ring += [along(part[c - first], ORDER[c]) if c else part[c] for c in range(first, last)]
+
+    near_out, far_out = plane_sum(out_ring)
+    near_back, far_back = plane_sum(back_ring)
+    other_in = across(after(moved_in, *grads))
     (both,) = kernel_call(
-        functools.partial(sum_kernel, images),
-        "v" * (3 + RING),
-        [("v", packed_shape)],
-        total * width,
-        2 * total * width,
-    )(after(near_out, other_in), far_out, *back_part[0], far_back)
-    in_pair = after(jnp.concatenate([moved_in, other_in], axis=0), both)
-    in_pairs = [in_pair] + [along(in_pair, -d) for d in range(1, RING)]
+        functools.partial(sum_kernel, images), "vvvv", [("v", packed_shape)], total * width, 2 * total * width
+    )(after(near_out, other_in), far_out, near_back, far_back)
+    in_pair = joined(after(moved_in, both), other_in)
+    in_pairs = [in_pair] + [along(in_pair, -steps) for steps in ORDER[1:]]
     moved_both = swap(both)
 
-    half = width // 2
-    count_rows = 2 * slots // ex_count
+    teams = [[(2 * t + core) * ex_count + i for core in range(2) for i in range(ex_count)] for t in range(dp_count // 2)]
+    peers = [[2 * t + core for t in range(dp_count // 2)] for core in range(2)]
+    team = len(teams[0])
+    rows = (slots // team) * -(-width // LANES)
     disp_b, logit_grad, back_rows, router_part = kernel_call(
-        functools.partial(logits_kernel, ex_count),
+        functools.partial(logits_kernel, team),
         "vrrr",
         [
             ("h", shape(BF, images, slots, count)),
             ("h", shape(BF, images, slots, count)),
             ("h", shape(BF, images, slots, width)),
-            ("v", shape(F32, 2 * slots, half)),
+            ("v", shape(F32, team, rows, LANES)),
         ],
         3 * small,
         2 * tokens.nbytes,
@@ -401,17 +416,21 @@
         disp_b, logit_grad, back_rows, router
     )
     (grad_w_out,) = kernel_call(
-        weight_out_kernel, "v" * (ex_count + 1), [("v", shape(BF, hidden, width))], big, 10 * total * hidden
-    )(act, *grad_blocks)
+        weight_out_kernel, "v" * (RING + 1), [("v", shape(BF, hidden, width))], big, 10 * total * hidden
+    )(act, *grads)
     (grad_w_in,) = kernel_call(
         weight_in_kernel, "v" * (RING + 2), [("v", shape(BF, width, hidden))], big, 10 * total * hidden
     )(*in_pairs, *hid)
 
-    parts = exchange(router_part.reshape(ex_count, count_rows, half), "expert")
-    (spread,) = kernel_call(total_kernel, "v", [("v", shape(BF, dp_count, count_rows, half))], small, tokens.nbytes)(parts)
-    parts = after(exchange(spread, "dp"), grad_x, grad_w_out)
-    (spread,) = kernel_call(total_kernel, "v", [("v", shape(F32, ex_count, count_rows, half))], small, tokens.nbytes)(parts)
-    parts = exchange(spread, "expert")
+    def swap_rows(value, axes, groups):
+        return lax.all_to_all(value, axes, split_axis=0, concat_axis=0, axis_index_groups=groups, tiled=True)
+
+    def spread_sum(parts, dtype, count):
+        return kernel_call(total_kernel, "v", [("v", shape(dtype, count, rows, LANES))], small, tokens.nbytes)(parts)[0]
+
+    parts = after(swap_rows(router_part, ("dp", "expert"), teams), grad_w_out)
+    parts = after(swap_rows(spread_sum(parts, BF, len(teams)), "dp", peers), grad_x)
+    parts = swap_rows(spread_sum(parts, F32, team), ("dp", "expert"), teams)
     (grad_router,) = kernel_call(rows_kernel, "v", [("v", shape(F32, slots, width))], small, tokens.nbytes)(
         after(parts, grad_w_in)
     )

time: 153 us -> 147 us (0.961)
  blocking collectives: 35 us -> 19.5 us
  waiting for transfers between devices: 32.3 us -> 47.8 us
  starting transfers between devices: 53.2 us -> 49.3 us
    all_to_all x2 -> x1, blocking collectives: 35 us -> 19.5 us  [exchange(): return lax.all_to_all(blocks, axis, split_axis=0, concat_axis=0, tiled=True)]
    all_to_all x0 -> x3, starting transfers between devices: none -> 14.2 us  [swap_rows(): lax.all_to_all(value, axes, split_axis=0, concat_axis=0, axis_index_group...]
    ppermute x18 -> x12, waiting for transfers between devices: 9.11 us -> 21.2 us  [along(): lax.ppermute(value, 'expert', [(i, i // RING * RING + (i + steps) % RING)...]
    ppermute x18 -> x12, starting transfers between devices: 29.3 us -> 18.1 us  [along(): lax.ppermute(value, 'expert', [(i, i // RING * RING + (i + steps) % RING)...]
    all_to_all x0 -> x3, waiting for transfers between devices: none -> 10.8 us  [swap_rows(): lax.all_to_all(value, axes, split_axis=0, concat_axis=0, axis_index_group...]
    all_to_all x3 -> x1, waiting for transfers between devices: 17 us -> 7.56 us  [exchange(): return lax.all_to_all(blocks, axis, split_axis=0, concat_axis=0, tiled=True)]
    all_to_all x3 -> x1, starting transfers between devices: 21.2 us -> 12.8 us  [exchange(): return lax.all_to_all(blocks, axis, split_axis=0, concat_axis=0, tiled=True)]
    ppermute x4, waiting for transfers between devices: 6.13 us -> 8.31 us  [across(): lax.ppermute(value, 'expert', [(i, (i + RING) % ex_count) for i in range(...]
  transfers between devices with their start and end apart: 25 -> 20, of which waited for: 14 -> 11; matrix products, arithmetic and copies ran while one was open for 0% -> 0% of each run, Pallas kernels for 13% -> 13%
where the time goes in v4:
time: 147 us
  starting transfers between devices  49.3 us (34%)
  waiting for transfers between devices  47.8 us (33%)
  Pallas kernels  27.4 us (19%)
  blocking collectives  19.5 us (13%)
  local copies, waits for them, and re-layouts  1.89 us (1%)
    pallas_call x17, Pallas kernels, run(): pl.pallas_call(body, out_shape=tuple((o[1] for o in outputs)), in_specs=[...  27.4 us
    ppermute x12, waiting for transfers between devices, along(): lax.ppermute(value, 'expert', [(i, i // RING * RING + (i + steps) % RING)...  21.2 us
    all_to_all x1, blocking collectives, exchange(): return lax.all_to_all(blocks, axis, split_axis=0, concat_axis=0, tiled=True)  19.5 us
    ppermute x12, starting transfers between devices, along(): lax.ppermute(value, 'expert', [(i, i // RING * RING + (i + steps) % RING)...  18.1 us
    all_to_all x3, starting transfers between devices, swap_rows(): lax.all_to_all(value, axes, split_axis=0, concat_axis=0, axis_index_group...  14.2 us
    all_to_all x1, starting transfers between devices, exchange(): return lax.all_to_all(blocks, axis, split_axis=0, concat_axis=0, tiled=True)  12.8 us
    all_to_all x3, waiting for transfers between devices, swap_rows(): lax.all_to_all(value, axes, split_axis=0, concat_axis=0, axis_index_group...  10.8 us
    ppermute x4, waiting for transfers between devices, across(): lax.ppermute(value, 'expert', [(i, (i + RING) % ex_count) for i in range(...  8.31 us
  transfers between devices with their start and end apart: 20, of which 11 were waited for; matrix products, arithmetic and copies ran while one was open for 0% of the time, Pallas kernels for 13%

profile of v4, /device:TPU:1, one launch (start us, length us, event | category | flops | bytes accessed | tf_op | source)
XLA Modules:
  0.0 146.9 jit_solution(14676388111976291474)
XLA Ops:
  0.6 3.1 %shard_map.102 = bf16[256,640]{1,0:T(8,128)(2,1)} custom-call(f32[2,32,256]{2,1,0:T(8,128)} %refs_1_.3, bf16[2,256,1280]{2,1,0:T(8,128)(2,1)} %refs_3_.2, bf16[2,256,1280]{2,1,0:T(8,128)(2,1)} %refs_2_.3), custom_call_target="tpu_custom_call" | custom-call | flops 83886080 | bytes 2621440 | tf_op jit(solution)/shard_map/pallas_call | solution.py:83
  3.7 12.8 %all-to-all-start = ((bf16[32,8,640]{2,1,0:T(8,128)(2,1)}), bf16[32,8,640]{2,1,0:T(8,128)(2,1)}, u32[]{:S(2)}, u32[]{:S(2)}) async-start(bf16[32,8,640]{2,1,0:T(8,128)(2,1)} %bitcast.19), calls=%async_computation | async-start | bytes 655360 | tf_op jit(solution)/shard_map/all_to_all | solution.py:35
  16.6 4.6 %shard_map.103 = (bf16[512,640]{1,0:T(8,128)(2,1)}, bf16[384,640]{1,0:T(8,128)(2,1)}, bf16[128,640]{1,0:T(8,128)(2,1)}, bf16[128,1280]{1,0:T(8,128)(2,1)}, bf16[...) custom-call(s32[1]{0:T(128)} %bitcast.refs_0_, bf16[512,640]{1,0:T(8,128)(2,1)} %bitcast.20, ...), custom_call_target="tpu_custom_call" | custom-call | flops 1677721600 | bytes 3276800 | tf_op jit(solution)/shard_map/pallas_call | solution.py:83
  22.4 1.5 collective-permute-start.1
  23.8 7.6 %all-to-all-done = bf16[32,8,640]{2,1,0:T(8,128)(2,1)} async-done(((bf16[32,8,640]{2,1,0:T(8,128)(2,1)}), bf16[32,8,640]{2,1,0:T(8,128)(2,1)}, u32[]{:S(2)}, u32[]{:S(2)}) %all-to-all-start) | async-done | bytes 327712 | tf_op jit(solution)/shard_map/all_to_all | solution.py:35
  31.4 1.2 shard_map.104
  33.7 4.3 %collective-permute-done.2.refs_1_ = bf16[64,1280]{1,0:T(8,128)(2,1)S(1)} collective-permute-done((bf16[64,1280]{1,0:T(8,128)(2,1)S(1)}, bf16[64,1280]{1,0:T(8,128)(2,1)S(1)}, u32[]{:S(2)}, u32[]{:S(2)}) %collective-permute-start.2) | collective-permute-done | bytes 163872 | tf_op jit(solution)/shard_map/ppermute | solution.py:347
  38.1 2.9 %collective-permute-start.5 = (bf16[128,1280]{1,0:T(8,128)(2,1)S(1)}, bf16[128,1280]{1,0:T(8,128)(2,1)S(1)}, u32[]{:S(2)}, u32[]{:S(2)}) collective-permute-start(bf16[128,1280]{1,0:T(8,128)(2,1)S(1)} %shard_map.105.refs_0_.refs_1_), channel_id=1, source_target_pairs={{0,2},{1,3},{2,0},{3,1},{4,6},{5,7},{6,4},{7,5},{8,10},{9,11},{10,... | collective-permute-start | bytes 983048 | tf_op jit(solution)/shard_map/ppermute | solution.py:344
  41.2 2.4 %collective-permute-start.3 = (bf16[128,1280]{1,0:T(8,128)(2,1)S(1)}, bf16[128,1280]{1,0:T(8,128)(2,1)S(1)}, u32[]{:S(2)}, u32[]{:S(2)}) collective-permute-start(bf16[128,1280]{1,0:T(8,128)(2,1)S(1)} %shard_map.105.refs_0_.refs_1_), channel_id=1, source_target_pairs={{0,3},{1,0},{2,1},{3,2},{4,7},{5,4},{6,5},{7,6},{8,11},{9,8},{10,9... | collective-permute-start | bytes 983048 | tf_op jit(solution)/shard_map/ppermute | solution.py:344
  43.6 4.0 %collective-permute-done.5.refs_0_.refs_4_ = bf16[128,1280]{1,0:T(8,128)(2,1)S(1)} collective-permute-done((bf16[128,1280]{1,0:T(8,128)(2,1)S(1)}, bf16[128,1280]{1,0:T(8,128)(2,1)S(1)}, u32[]{:S(2)}, u32[]{:S(2)}) %collective-permute-start.5) | collective-permute-done | bytes 327712 | tf_op jit(solution)/shard_map/ppermute | solution.py:344
  49.8 2.9 %collective-permute-start.11 = (bf16[128,1280]{1,0:T(8,128)(2,1)S(1)}, bf16[128,1280]{1,0:T(8,128)(2,1)S(1)}, u32[]{:S(2)}, u32[]{:S(2)}) collective-permute-start(bf16[128,1280]{1,0:T(8,128)(2,1)S(1)} %get-tuple-element.56), channel_id=1, source_target_pairs={{0,2},{1,3},{2,0},{3,1},{4,6},{5,7},{6,4},{7,5},{8,10},{9,11},{10,... | collective-permute-start | bytes 983048 | tf_op jit(solution)/shard_map/ppermute | solution.py:344
  52.8 5.2 %collective-permute-done.4.refs_2_.refs_3_ = bf16[128,1280]{1,0:T(8,128)(2,1)S(1)} collective-permute-done((bf16[128,1280]{1,0:T(8,128)(2,1)S(1)}, bf16[128,1280]{1,0:T(8,128)(2,1)S(1)}, u32[]{:S(2)}, u32[]{:S(2)}) %collective-permute-start.4) | collective-permute-done | bytes 327712 | tf_op jit(solution)/shard_map/ppermute | solution.py:344
  58.3 3.0 %shard_map.107 = (bf16[384,640]{1,0:T(8,128)(2,1)S(1)}, bf16[128,1280]{1,0:T(8,128)(2,1)S(1)}, bf16[128,1280]{1,0:T(8,128)(2,1)S(1)}, bf16[128,1280]{1,0:T(8,128)(2,1)S(1)}) custom-call(bf16[128,1280]{1,0:T(8,128)(2,1)S(1)} %shard_map.105.refs_0_.refs_1_, bf16[128,1280]{1,0:T(8,128)(2,1)S(1)} %collective-permute-done.3.refs_1_.refs_2_, ...), custom_call_target="tpu_custom_call" | custom-call | flops 1258291200 | bytes 1638400 | tf_op jit(solution)/shard_map/pallas_call | solution.py:83
  62.1 2.7 %collective-permute-start.9 = (bf16[128,1280]{1,0:T(8,128)(2,1)S(1)}, bf16[128,1280]{1,0:T(8,128)(2,1)S(1)}, u32[]{:S(2)}, u32[]{:S(2)}) collective-permute-start(bf16[128,1280]{1,0:T(8,128)(2,1)S(1)} %get-tuple-element.53), channel_id=1, source_target_pairs={{0,1},{1,2},{2,3},{3,0},{4,5},{5,6},{6,7},{7,4},{8,9},{9,10},{10,1... | collective-permute-start | bytes 983048 | tf_op jit(solution)/shard_map/ppermute | solution.py:344
  66.4 3.0 %collective-permute-done.6.refs_3_ = bf16[128,1280]{1,0:T(8,128)(2,1)S(1)} collective-permute-done((bf16[128,1280]{1,0:T(8,128)(2,1)S(1)}, bf16[128,1280]{1,0:T(8,128)(2,1)S(1)}, u32[]{:S(2)}, u32[]{:S(2)}) %collective-permute-start.6) | collective-permute-done | bytes 327712 | tf_op jit(solution)/shard_map/ppermute | solution.py:344
  69.4 1.2 shard_map.106
  71.7 5.7 %collective-permute-done.9.refs_1_ = bf16[128,1280]{1,0:T(8,128)(2,1)S(1)} collective-permute-done((bf16[128,1280]{1,0:T(8,128)(2,1)S(1)}, bf16[128,1280]{1,0:T(8,128)(2,1)S(1)}, u32[]{:S(2)}, u32[]{:S(2)}) %collective-permute-start.9) | collective-permute-done | bytes 327712 | tf_op jit(solution)/shard_map/ppermute | solution.py:344
  77.6 1.3 collective-permute-start.12
  78.9 4.0 %collective-permute-done.12.refs_3_ = bf16[64,1280]{1,0:T(8,128)(2,1)S(1)} collective-permute-done((bf16[64,1280]{1,0:T(8,128)(2,1)S(1)}, bf16[64,1280]{1,0:T(8,128)(2,1)S(1)}, u32[]{:S(2)}, u32[]{:S(2)}) %collective-permute-start.12) | collective-permute-done | bytes 163872 | tf_op jit(solution)/shard_map/ppermute | solution.py:347
  83.1 19.5 %all_to_all.25 = bf16[32,8,640]{2,1,0:T(8,128)(2,1)S(1)} all-to-all(bf16[32,8,640]{2,1,0:T(8,128)(2,1)S(1)} %bitcast.16), channel_id=1, replica_groups=mesh['dp'=32,'expert'=8] {'dp'}, dimensions={0} | all-to-all | bytes 655360 | tf_op jit(solution)/shard_map/all_to_all | solution.py:35
  102.7 3.9 %shard_map.111 = (bf16[2,32,256]{2,1,0:T(8,128)(2,1)S(1)}, bf16[2,32,256]{2,1,0:T(8,128)(2,1)S(1)}, bf16[2,32,1280]{2,1,0:T(8,128)(2,1)S(1)}, f32[16,8,384]{2,1,0:T(8,128)}) custom-call(bf16[256,640]{1,0:T(8,128)(2,1)S(1)} %bitcast.15, f32[2,32,256]{2,1,0:T(8,128)S(1)} %copy-done.17, bf16[2,256,1280]{2,1,0:T(8,128)(2,1)S(1)} %copy-done.3, ...), custom_call_target="tpu_custom_call" | custom-call | flops 125829120 | bytes 2621440 | tf_op jit(solution)/shard_map/pallas_call | solution.py:83
  106.6 6.0 %all-to-all-start.2 = ((f32[16,8,384]{2,1,0:T(8,128)}), f32[16,8,384]{2,1,0:T(8,128)S(1)}, u32[]{:S(2)}, u32[]{:S(2)}) async-start(f32[16,8,384]{2,1,0:T(8,128)} %get-tuple-element.62), calls=%async_computation.2 | async-start | bytes 393216 | tf_op jit(solution)/shard_map/all_to_all | solution.py:426
  112.7 2.2 %shard_map.113 = bf16[640,1280]{1,0:T(8,128)(2,1)} custom-call(bf16[512,640]{1,0:T(8,128)(2,1)S(1)} %copy-done.12, bf16[128,1280]{1,0:T(8,128)(2,1)S(1)} %copy-done.5, bf16[128,1280]{1,0:T(8,128)(2,1)S(1)} %copy-done.11, bf16[128,1280]{1,0:T(8,128)(2,1)S(1)} %copy-done.9, bf16[128,1280]{1,0:T(8,128)(2,1)S(1)} %copy-done.7), custom_call_target="tpu_custom_call" | custom-call | flops 838860800 | bytes 3276800 | tf_op jit(solution)/shard_map/pallas_call | solution.py:83
  115.0 4.7 %all-to-all-done.2.refs_0_ = f32[16,8,384]{2,1,0:T(8,128)S(1)} async-done(((f32[16,8,384]{2,1,0:T(8,128)}), f32[16,8,384]{2,1,0:T(8,128)S(1)}, u32[]{:S(2)}, u32[]{:S(2)}) %all-to-all-start.2) | async-done | bytes 196640 | tf_op jit(solution)/shard_map/all_to_all | solution.py:426
  120.4 3.6 %all-to-all-start.3 = ((bf16[16,8,384]{2,1,0:T(8,128)(2,1)}), bf16[16,8,384]{2,1,0:T(8,128)(2,1)S(1)}, u32[]{:S(2)}, u32[]{:S(2)}) async-start(bf16[16,8,384]{2,1,0:T(8,128)(2,1)} %shard_map.114), calls=%async_computation.3 | async-start | bytes 196608 | tf_op jit(solution)/shard_map/all_to_all | solution.py:426
  124.9 2.5 %collective-permute-start.13 = (bf16[128,1280]{1,0:T(8,128)(2,1)S(1)}, bf16[128,1280]{1,0:T(8,128)(2,1)S(1)}, u32[]{:S(2)}, u32[]{:S(2)}) collective-permute-start(bf16[128,1280]{1,0:T(8,128)(2,1)S(1)} %shard_map.116.refs_0_), channel_id=1, source_target_pairs={{0,3},{1,0},{2,1},{3,2},{4,7},{5,4},{6,5},{7,6},{8,11},{9,8},{10,9... | collective-permute-start | bytes 983048 | tf_op jit(solution)/shard_map/ppermute | solution.py:344
  127.4 1.9 %shard_map.112 = bf16[2,256,1280]{2,1,0:T(8,128)(2,1)} custom-call(bf16[2,32,256]{2,1,0:T(8,128)(2,1)S(1)} %get-tuple-element.59.refs_0_, bf16[2,32,256]{2,1,0:T(8,128)(2,1)S(1)} %get-tuple-element.60.refs_1_, bf16[2,32,1280]{2,1,0:T(8,128)(2,1)S(1)} %get-tuple-element.61.refs_2_, bf16[32,1280]{1,0:T(8,128)(2,1)S(1)} %copy-done.21), custom_call_target="tpu_custom_call" | custom-call | flops 83886080 | bytes 1310720 | tf_op jit(solution)/shard_map/pallas_call | solution.py:83
  129.3 4.6 %all-to-all-done.3.refs_0_ = bf16[16,8,384]{2,1,0:T(8,128)(2,1)S(1)} async-done(((bf16[16,8,384]{2,1,0:T(8,128)(2,1)}), bf16[16,8,384]{2,1,0:T(8,128)(2,1)S(1)}, u32[]{:S(2)}, u32[]{:S(2)}) %all-to-all-start.3) | async-done | bytes 98336 | tf_op jit(solution)/shard_map/all_to_all | solution.py:426
  134.6 4.5 %all-to-all-start.4 = ((f32[16,8,384]{2,1,0:T(8,128)}), f32[16,8,384]{2,1,0:T(8,128)S(1)}, u32[]{:S(2)}, u32[]{:S(2)}) async-start(f32[16,8,384]{2,1,0:T(8,128)} %shard_map.115), calls=%async_computation.4 | async-start | bytes 393216 | tf_op jit(solution)/shard_map/all_to_all | solution.py:426
  139.1 3.2 %collective-permute-done.14.refs_2_ = bf16[128,1280]{1,0:T(8,128)(2,1)S(1)} collective-permute-done((bf16[128,1280]{1,0:T(8,128)(2,1)S(1)}, bf16[128,1280]{1,0:T(8,128)(2,1)S(1)}, u32[]{:S(2)}, u32[]{:S(2)}) %collective-permute-start.14) | collective-permute-done | bytes 327712 | tf_op jit(solution)/shard_map/ppermute | solution.py:344
  142.3 2.4 %shard_map.117 = bf16[1280,640]{1,0:T(8,128)(2,1)} custom-call(bf16[128,1280]{1,0:T(8,128)(2,1)S(1)} %shard_map.116.refs_0_, bf16[128,1280]{1,0:T(8,128)(2,1)S(1)} %collective-permute-done.13.refs_1_, bf16[128,1280]{1,0:T(8,128)(2,1)S(1)} %collective-permute-done.14.refs_2_, bf16[128,1280]{1,0:T(8,128)(2,1)S(1)} %collective-permute-done.15.refs_3_, ...), custom_call_target="tpu_custom_call" | custom-call | flops 838860800 | bytes 3276800 | tf_op jit(solution)/shard_map/pallas_call | solution.py:83
  144.7 1.5 %all-to-all-done.4.refs_0_ = f32[16,8,384]{2,1,0:T(8,128)S(1)} async-done(((f32[16,8,384]{2,1,0:T(8,128)}), f32[16,8,384]{2,1,0:T(8,128)S(1)}, u32[]{:S(2)}, u32[]{:S(2)}) %all-to-all-start.4) | async-done | bytes 196640 | tf_op jit(solution)/shard_map/all_to_all | solution.py:426
  (72 shorter events, 12.0 us)
Async XLA Ops:
  3.7 27.6 %all-to-all-start = ((bf16[32,8,640]{2,1,0:T(8,128)(2,1)}), bf16[32,8,640]{2,1,0:T(8,128)(2,1)}, u32[]{:S(2)}, u32[]{:S(2)}) async-start(bf16[32,8,640]{2,1,0:T(8,128)(2,1)} %bitcast.19), calls=%async_computation | async-start | bytes 655360 | tf_op jit(solution)/shard_map/all_to_all | solution.py:35
  16.6 31.0 %copy-start = (bf16[1,640,1280]{2,1,0:T(8,128)(2,1)S(1)}, bf16[1,640,1280]{2,1,0:T(8,128)(2,1)}, u32[]{:S(2)}) copy-start(bf16[1,640,1280]{2,1,0:T(8,128)(2,1)} %param.13) | copy-start | bytes 4915204
  16.6 31.0 %copy-start.1 = (bf16[1,1280,640]{2,1,0:T(8,128)(2,1)S(1)}, bf16[1,1280,640]{2,1,0:T(8,128)(2,1)}, u32[]{:S(2)}) copy-start(bf16[1,1280,640]{2,1,0:T(8,128)(2,1)} %param.12) | copy-start | bytes 4915204
  21.1 12.5 %collective-permute-start = (bf16[128,1280]{1,0:T(8,128)(2,1)}, bf16[128,1280]{1,0:T(8,128)(2,1)}, u32[]{:S(2)}, u32[]{:S(2)}) collective-permute-start(bf16[128,1280]{1,0:T(8,128)(2,1)} %get-tuple-element.39), channel_id=1, source_target_pairs={{0,1},{1,2},{2,3},{3,0},{4,5},{5,6},{6,7},{7,4},{8,9},{9,10},{10,1... | collective-permute-start | bytes 983048 | tf_op jit(solution)/shard_map/ppermute | solution.py:344
  22.4 11.3 %collective-permute-start.1 = (bf16[128,1280]{1,0:T(8,128)(2,1)}, bf16[128,1280]{1,0:T(8,128)(2,1)}, u32[]{:S(2)}, u32[]{:S(2)}) collective-permute-start(bf16[128,1280]{1,0:T(8,128)(2,1)} %get-tuple-element.40), channel_id=1, source_target_pairs={{0,3},{1,0},{2,1},{3,2},{4,7},{5,4},{6,5},{7,6},{8,11},{9,8},{10,9... | collective-permute-start | bytes 983048 | tf_op jit(solution)/shard_map/ppermute | solution.py:344
  32.6 32.8 %copy-start.19 = (bf16[64,1280]{1,0:T(8,128)(2,1)}, bf16[64,1280]{1,0:T(8,128)(2,1)S(1)}, u32[]{:S(2)}) copy-start(bf16[64,1280]{1,0:T(8,128)(2,1)S(1)} %get-tuple-element.66.refs_0_) | copy-start | bytes 491524
  32.6 5.4 %collective-permute-start.2 = (bf16[64,1280]{1,0:T(8,128)(2,1)S(1)}, bf16[64,1280]{1,0:T(8,128)(2,1)S(1)}, u32[]{:S(2)}, u32[]{:S(2)}) collective-permute-start(bf16[64,1280]{1,0:T(8,128)(2,1)S(1)} %get-tuple-element.44.refs_0_), channel_id=1, source_target_pairs={{0,4},{1,5},{2,6},{3,7},{4,0},{5,1},{6,2},{7,3},{8,12},{9,13},{10,... | collective-permute-start | bytes 491528 | tf_op jit(solution)/shard_map/ppermute | solution.py:347
  38.0 20.3 %copy-start.4 = (bf16[128,1280]{1,0:T(8,128)(2,1)}, bf16[128,1280]{1,0:T(8,128)(2,1)S(1)}, u32[]{:S(2)}) copy-start(bf16[128,1280]{1,0:T(8,128)(2,1)S(1)} %shard_map.105.refs_0_.refs_1_) | copy-start | bytes 983044
  38.1 9.5 %collective-permute-start.5 = (bf16[128,1280]{1,0:T(8,128)(2,1)S(1)}, bf16[128,1280]{1,0:T(8,128)(2,1)S(1)}, u32[]{:S(2)}, u32[]{:S(2)}) collective-permute-start(bf16[128,1280]{1,0:T(8,128)(2,1)S(1)} %shard_map.105.refs_0_.refs_1_), channel_id=1, source_target_pairs={{0,2},{1,3},{2,0},{3,1},{4,6},{5,7},{6,4},{7,5},{8,10},{9,11},{10,... | collective-permute-start | bytes 983048 | tf_op jit(solution)/shard_map/ppermute | solution.py:344
  40.9 17.1 %collective-permute-start.4 = (bf16[128,1280]{1,0:T(8,128)(2,1)S(1)}, bf16[128,1280]{1,0:T(8,128)(2,1)S(1)}, u32[]{:S(2)}, u32[]{:S(2)}) collective-permute-start(bf16[128,1280]{1,0:T(8,128)(2,1)S(1)} %shard_map.105.refs_0_.refs_1_), channel_id=1, source_target_pairs={{0,1},{1,2},{2,3},{3,0},{4,5},{5,6},{6,7},{7,4},{8,9},{9,10},{10,1... | collective-permute-start | bytes 983048 | tf_op jit(solution)/shard_map/ppermute | solution.py:344
  41.2 16.8 %collective-permute-start.3 = (bf16[128,1280]{1,0:T(8,128)(2,1)S(1)}, bf16[128,1280]{1,0:T(8,128)(2,1)S(1)}, u32[]{:S(2)}, u32[]{:S(2)}) collective-permute-start(bf16[128,1280]{1,0:T(8,128)(2,1)S(1)} %shard_map.105.refs_0_.refs_1_), channel_id=1, source_target_pairs={{0,3},{1,0},{2,1},{3,2},{4,7},{5,4},{6,5},{7,6},{8,11},{9,8},{10,9... | collective-permute-start | bytes 983048 | tf_op jit(solution)/shard_map/ppermute | solution.py:344
  49.8 21.9 %collective-permute-start.11 = (bf16[128,1280]{1,0:T(8,128)(2,1)S(1)}, bf16[128,1280]{1,0:T(8,128)(2,1)S(1)}, u32[]{:S(2)}, u32[]{:S(2)}) collective-permute-start(bf16[128,1280]{1,0:T(8,128)(2,1)S(1)} %get-tuple-element.56), channel_id=1, source_target_pairs={{0,2},{1,3},{2,0},{3,1},{4,6},{5,7},{6,4},{7,5},{8,10},{9,11},{10,... | collective-permute-start | bytes 983048 | tf_op jit(solution)/shard_map/ppermute | solution.py:344
  58.0 11.4 %collective-permute-start.6 = (bf16[128,1280]{1,0:T(8,128)(2,1)S(1)}, bf16[128,1280]{1,0:T(8,128)(2,1)S(1)}, u32[]{:S(2)}, u32[]{:S(2)}) collective-permute-start(bf16[128,1280]{1,0:T(8,128)(2,1)S(1)} %copy-done.22), channel_id=1, source_target_pairs={{0,2},{1,3},{2,0},{3,1},{4,6},{5,7},{6,4},{7,5},{8,10},{9,11},{10,... | collective-permute-start | bytes 983048 | tf_op jit(solution)/shard_map/ppermute | solution.py:344
  58.3 11.1 %copy-start.16 = (bf16[128,1280]{1,0:T(8,128)(2,1)S(1)}, bf16[128,1280]{1,0:T(8,128)(2,1)}, u32[]{:S(2)}) copy-start(bf16[128,1280]{1,0:T(8,128)(2,1)} %get-tuple-element.38.refs_0_) | copy-start | bytes 983044
  62.1 15.3 %collective-permute-start.9 = (bf16[128,1280]{1,0:T(8,128)(2,1)S(1)}, bf16[128,1280]{1,0:T(8,128)(2,1)S(1)}, u32[]{:S(2)}, u32[]{:S(2)}) collective-permute-start(bf16[128,1280]{1,0:T(8,128)(2,1)S(1)} %get-tuple-element.53), channel_id=1, source_target_pairs={{0,1},{1,2},{2,3},{3,0},{4,5},{5,6},{6,7},{7,4},{8,9},{9,10},{10,1... | collective-permute-start | bytes 983048 | tf_op jit(solution)/shard_map/ppermute | solution.py:344
  64.9 12.5 %collective-permute-start.10 = (bf16[128,1280]{1,0:T(8,128)(2,1)S(1)}, bf16[128,1280]{1,0:T(8,128)(2,1)S(1)}, u32[]{:S(2)}, u32[]{:S(2)}) collective-permute-start(bf16[128,1280]{1,0:T(8,128)(2,1)S(1)} %get-tuple-element.54), channel_id=1, source_target_pairs={{0,3},{1,0},{2,1},{3,2},{4,7},{5,4},{6,5},{7,6},{8,11},{9,8},{10,9... | collective-permute-start | bytes 983048 | tf_op jit(solution)/shard_map/ppermute | solution.py:344
  65.4 13.4 %collective-permute-start.7 = (bf16[64,1280]{1,0:T(8,128)(2,1)S(1)}, bf16[64,1280]{1,0:T(8,128)(2,1)S(1)}, u32[]{:S(2)}, u32[]{:S(2)}) collective-permute-start(bf16[64,1280]{1,0:T(8,128)(2,1)S(1)} %get-tuple-element.66.refs_0_), channel_id=1, source_target_pairs={{0,4},{1,5},{2,6},{3,7},{4,0},{5,1},{6,2},{7,3},{8,12},{9,13},{10,... | collective-permute-start | bytes 491528 | tf_op jit(solution)/shard_map/ppermute | solution.py:347
  70.7 8.2 %collective-permute-start.8 = (bf16[64,1280]{1,0:T(8,128)(2,1)S(1)}, bf16[64,1280]{1,0:T(8,128)(2,1)S(1)}, u32[]{:S(2)}, u32[]{:S(2)}) collective-permute-start(bf16[64,1280]{1,0:T(8,128)(2,1)S(1)} %get-tuple-element.50), channel_id=1, source_target_pairs={{0,4},{1,5},{2,6},{3,7},{4,0},{5,1},{6,2},{7,3},{8,12},{9,13},{10,... | collective-permute-start | bytes 491528 | tf_op jit(solution)/shard_map/ppermute | solution.py:347
  77.4 25.3 %copy-start.2 = (bf16[2,256,1280]{2,1,0:T(8,128)(2,1)S(1)}, bf16[2,256,1280]{2,1,0:T(8,128)(2,1)}, u32[]{:S(2)}) copy-start(bf16[2,256,1280]{2,1,0:T(8,128)(2,1)} %refs_3_.2) | copy-start | bytes 3932164
  77.4 25.3 %copy-start.3 = (bf16[2,256,1280]{2,1,0:T(8,128)(2,1)S(1)}, bf16[2,256,1280]{2,1,0:T(8,128)(2,1)}, u32[]{:S(2)}) copy-start(bf16[2,256,1280]{2,1,0:T(8,128)(2,1)} %refs_2_.3) | copy-start | bytes 3932164
  77.4 25.3 %copy-start.17 = (f32[2,32,256]{2,1,0:T(8,128)S(1)}, f32[2,32,256]{2,1,0:T(8,128)}, u32[]{:S(2)}) copy-start(f32[2,32,256]{2,1,0:T(8,128)} %refs_1_.3) | copy-start | bytes 196612
  77.6 5.2 %collective-permute-start.12 = (bf16[64,1280]{1,0:T(8,128)(2,1)S(1)}, bf16[64,1280]{1,0:T(8,128)(2,1)S(1)}, u32[]{:S(2)}, u32[]{:S(2)}) collective-permute-start(bf16[64,1280]{1,0:T(8,128)(2,1)S(1)} %get-tuple-element.58), channel_id=1, source_target_pairs={{0,4},{1,5},{2,6},{3,7},{4,0},{5,1},{6,2},{7,3},{8,12},{9,13},{10,... | collective-permute-start | bytes 491528 | tf_op jit(solution)/shard_map/ppermute | solution.py:347
  102.7 10.0 %copy-start.5 = (bf16[128,1280]{1,0:T(8,128)(2,1)S(1)}, bf16[128,1280]{1,0:T(8,128)(2,1)}, u32[]{:S(2)}) copy-start(bf16[128,1280]{1,0:T(8,128)(2,1)} %copy-done.4) | copy-start | bytes 983044
  106.6 13.1 %all-to-all-start.2 = ((f32[16,8,384]{2,1,0:T(8,128)}), f32[16,8,384]{2,1,0:T(8,128)S(1)}, u32[]{:S(2)}, u32[]{:S(2)}) async-start(f32[16,8,384]{2,1,0:T(8,128)} %get-tuple-element.62), calls=%async_computation.2 | async-start | bytes 393216 | tf_op jit(solution)/shard_map/all_to_all | solution.py:426
  112.7 11.3 %copy-start.20 = (bf16[64,1280]{1,0:T(8,128)(2,1)S(1)}, bf16[64,1280]{1,0:T(8,128)(2,1)}, u32[]{:S(2)}) copy-start(bf16[64,1280]{1,0:T(8,128)(2,1)} %copy-done.19) | copy-start | bytes 491524
  112.7 14.7 %copy-start.21 = (bf16[32,1280]{1,0:T(8,128)(2,1)S(1)}, bf16[32,1280]{1,0:T(8,128)(2,1)}, u32[]{:S(2)}) copy-start(bf16[32,1280]{1,0:T(8,128)(2,1)} %refs_3_.3) | copy-start | bytes 245764
  120.4 21.9 %copy-start.14 = (bf16[384,640]{1,0:T(8,128)(2,1)S(1)}, bf16[384,640]{1,0:T(8,128)(2,1)}, u32[]{:S(2)}) copy-start(bf16[384,640]{1,0:T(8,128)(2,1)} %copy-done.13) | copy-start | bytes 1474564
  120.4 13.5 %all-to-all-start.3 = ((bf16[16,8,384]{2,1,0:T(8,128)(2,1)}), bf16[16,8,384]{2,1,0:T(8,128)(2,1)S(1)}, u32[]{:S(2)}, u32[]{:S(2)}) async-start(bf16[16,8,384]{2,1,0:T(8,128)(2,1)} %shard_map.114), calls=%async_computation.3 | async-start | bytes 196608 | tf_op jit(solution)/shard_map/all_to_all | solution.py:426
  124.1 15.1 %collective-permute-start.15 = (bf16[128,1280]{1,0:T(8,128)(2,1)S(1)}, bf16[128,1280]{1,0:T(8,128)(2,1)S(1)}, u32[]{:S(2)}, u32[]{:S(2)}) collective-permute-start(bf16[128,1280]{1,0:T(8,128)(2,1)S(1)} %shard_map.116.refs_0_), channel_id=1, source_target_pairs={{0,2},{1,3},{2,0},{3,1},{4,6},{5,7},{6,4},{7,5},{8,10},{9,11},{10,... | collective-permute-start | bytes 983048 | tf_op jit(solution)/shard_map/ppermute | solution.py:344
  124.7 17.6 %collective-permute-start.14 = (bf16[128,1280]{1,0:T(8,128)(2,1)S(1)}, bf16[128,1280]{1,0:T(8,128)(2,1)S(1)}, u32[]{:S(2)}, u32[]{:S(2)}) collective-permute-start(bf16[128,1280]{1,0:T(8,128)(2,1)S(1)} %shard_map.116.refs_0_), channel_id=1, source_target_pairs={{0,1},{1,2},{2,3},{3,0},{4,5},{5,6},{6,7},{7,4},{8,9},{9,10},{10,1... | collective-permute-start | bytes 983048 | tf_op jit(solution)/shard_map/ppermute | solution.py:344
  124.9 17.4 %collective-permute-start.13 = (bf16[128,1280]{1,0:T(8,128)(2,1)S(1)}, bf16[128,1280]{1,0:T(8,128)(2,1)S(1)}, u32[]{:S(2)}, u32[]{:S(2)}) collective-permute-start(bf16[128,1280]{1,0:T(8,128)(2,1)S(1)} %shard_map.116.refs_0_), channel_id=1, source_target_pairs={{0,3},{1,0},{2,1},{3,2},{4,7},{5,4},{6,5},{7,6},{8,11},{9,8},{10,9... | collective-permute-start | bytes 983048 | tf_op jit(solution)/shard_map/ppermute | solution.py:344
  134.6 11.6 %all-to-all-start.4 = ((f32[16,8,384]{2,1,0:T(8,128)}), f32[16,8,384]{2,1,0:T(8,128)S(1)}, u32[]{:S(2)}, u32[]{:S(2)}) async-start(f32[16,8,384]{2,1,0:T(8,128)} %shard_map.115), calls=%async_computation.4 | async-start | bytes 393216 | tf_op jit(solution)/shard_map/all_to_all | solution.py:426
  (11 other events, 69.8 us)

commit v5 on v4

--- a/solution.py
+++ b/solution.py
@@ -97,6 +97,9 @@
     total = slots * pieces
     row = lax.broadcasted_iota(jnp.int32, (total, total), 1 if back else 0)
     col = lax.broadcasted_iota(jnp.int32, (total, total), 0 if back else 1)
+    shift = pieces.bit_length() - 1
+    if pieces == 1 << shift:
+        return ((row & (pieces - 1)) * slots + (row >> shift) == col).astype(BF)
     return ((row % pieces) * slots + row // pieces == col).astype(BF)
 
 
@@ -239,24 +242,14 @@
     out_ref[...] = pack(sums, refs[0].shape[1])
 
 
-def logits_kernel(owners, moved_ref, logits_in, tokens_in, dy_in, disp_ref, grad_ref, back_ref, router_ref, logits, tokens, dy, sems):
+def logits_kernel(owners, moved_ref, logits, tokens, dy, disp_ref, grad_ref, back_ref, router_ref):
     images, slots, _ = logits.shape
-    pairs = [(logits_in, logits)]
-    for src, dst in ((dy_in, dy), (tokens_in, tokens)):
-        for b in range(images):
-            pairs += halves(src, dst, b)
-    copies = fetch(pairs, sems)
     rows = unpack(moved_ref[...], slots)
-    copies[0].wait()
     parts = []
     for b in range(images):
         comb = softmax(logits[b], 0)
         disp = softmax(logits[b], 1)
         back_ref[b] = rows[images + b]
-        for axis in range(2):
-            at = 1 + 2 * (axis * images + b)
-            copies[at].wait()
-            copies[at + 1].wait()
         comb_grad = dot(rows[b], dy[b], ((1,), (1,)))
         disp_grad = dot(rows[images + b], tokens[b], ((1,), (1,)))
         through_comb = comb * (comb_grad - jnp.sum(comb * comb_grad, axis=0, keepdims=True))
@@ -266,20 +259,17 @@
         grad_ref[b] = logit_grad
         parts.append(dot(logit_grad, tokens[b], ((1,), (0,))))
     part = sum(parts[1:], parts[0])
-    for p in range(owners):
-        for at, slot, lanes in pieces(slots // owners, part.shape[1]):
-            router_ref[p, at : at + 1, : lanes.stop - lanes.start] = part[p * slots // owners + slot][None, lanes]
-            if lanes.stop - lanes.start < router_ref.shape[2]:
-                router_ref[p, at : at + 1, lanes.stop - lanes.start :] = jnp.zeros(
-                    (1, router_ref.shape[2] - lanes.stop + lanes.start), F32
-                )
-
-
-def pieces(count, width):
-    each = -(-width // LANES)
-    return [
-        (slot * each + q, slot, slice(q * LANES, min(width, (q + 1) * LANES))) for slot in range(count) for q in range(each)
-    ]
+    count, width = slots // owners, part.shape[1]
+    for q, lanes in enumerate(pieces(width)):
+        size = lanes.stop - lanes.start
+        for p in range(owners):
+            router_ref[p, q * count : (q + 1) * count, :size] = part[p * count : (p + 1) * count, lanes]
+            if size < LANES:
+                router_ref[p, q * count : (q + 1) * count, size:] = jnp.zeros((count, LANES - size), F32)
+
+
+def pieces(width):
+    return [slice(at, min(width, at + LANES)) for at in range(0, width, LANES)]
 
 
 def total_kernel(parts_ref, out_ref):
@@ -293,10 +283,10 @@
 
 def rows_kernel(parts_ref, out_ref):
     count = out_ref.shape[0] // parts_ref.shape[0]
-    for p in range(parts_ref.shape[0]):
-        for at, slot, lanes in pieces(count, out_ref.shape[1]):
-            row = p * count + slot
-            out_ref[row : row + 1, lanes] = parts_ref[p, at : at + 1, : lanes.stop - lanes.start]
+    for q, lanes in enumerate(pieces(out_ref.shape[1])):
+        for p in range(parts_ref.shape[0]):
+            rows = parts_ref[p, q * count : (q + 1) * count, : lanes.stop - lanes.start]
+            out_ref[p * count : (p + 1) * count, lanes] = rows
 
 
 def tokens_kernel(disp_ref, grad_ref, back_ref, router_ref, out_ref):
@@ -387,9 +377,12 @@
     near_out, far_out = plane_sum(out_ring)
     near_back, far_back = plane_sum(back_ring)
     other_in = across(after(moved_in, *grads))
+    (grad_w_out,) = kernel_call(
+        weight_out_kernel, "v" * (RING + 1), [("v", shape(BF, hidden, width))], big, 10 * total * hidden
+    )(act, *grads)
     (both,) = kernel_call(
         functools.partial(sum_kernel, images), "vvvv", [("v", packed_shape)], total * width, 2 * total * width
-    )(after(near_out, other_in), far_out, near_back, far_back)
+    )(after(near_out, other_in, grad_w_out), far_out, near_back, far_back)
     in_pair = joined(after(moved_in, both), other_in)
     in_pairs = [in_pair] + [along(in_pair, -steps) for steps in ORDER[1:]]
     moved_both = swap(both)
@@ -400,7 +393,7 @@
     rows = (slots // team) * -(-width // LANES)
     disp_b, logit_grad, back_rows, router_part = kernel_call(
         functools.partial(logits_kernel, team),
-        "vrrr",
+        "vvvv",
         [
             ("h", shape(BF, images, slots, count)),
             ("h", shape(BF, images, slots, count)),
@@ -409,15 +402,11 @@
         ],
         3 * small,
         2 * tokens.nbytes,
-        fetched,
-        20 * MIB,
+        vmem=20 * MIB,
     )(moved_both, logits, tokens, grad_out)
     (grad_x,) = kernel_call(tokens_kernel, "vvvv", [("v", shape(BF, *tokens.shape))], 2 * small, tokens.nbytes)(
         disp_b, logit_grad, back_rows, router
     )
-    (grad_w_out,) = kernel_call(
-        weight_out_kernel, "v" * (RING + 1), [("v", shape(BF, hidden, width))], big, 10 * total * hidden
-    )(act, *grads)
     (grad_w_in,) = kernel_call(
         weight_in_kernel, "v" * (RING + 2), [("v", shape(BF, width, hidden))], big, 10 * total * hidden
     )(*in_pairs, *hid)
@@ -428,8 +417,8 @@
     def spread_sum(parts, dtype, count):
         return kernel_call(total_kernel, "v", [("v", shape(dtype, count, rows, LANES))], small, tokens.nbytes)(parts)[0]
 
-    parts = after(swap_rows(router_part, ("dp", "expert"), teams), grad_w_out)
-    parts = after(swap_rows(spread_sum(parts, BF, len(teams)), "dp", peers), grad_x)
+    parts = after(swap_rows(router_part, ("dp", "expert"), teams), grad_x)
+    parts = after(swap_rows(spread_sum(parts, BF, len(teams)), "dp", peers), grad_w_out)
     parts = swap_rows(spread_sum(parts, F32, team), ("dp", "expert"), teams)
     (grad_router,) = kernel_call(rows_kernel, "v", [("v", shape(F32, slots, width))], small, tokens.nbytes)(
         after(parts, grad_w_in)

time: 147 us -> 146 us (level)
  Pallas kernels: 27.4 us -> 25.9 us
    all_to_all x3, waiting for transfers between devices: 10.8 us -> 13.1 us  [swap_rows(): lax.all_to_all(value, axes, split_axis=0, concat_axis=0, axis_index_group...]
    ppermute x4, waiting for transfers between devices: 8.31 us -> 6.05 us  [across(): lax.ppermute(value, 'expert', [(i, (i + RING) % ex_count) for i in range(...]
    pallas_call x17, Pallas kernels: 27.4 us -> 25.9 us  [run(): pl.pallas_call(body, out_shape=tuple((o[1] for o in outputs)), in_specs=[...]
where the time goes in v5:
time: 146 us; the launch traced here: 145 us
  starting transfers between devices  49.4 us (34%)
  waiting for transfers between devices  48 us (33%)
  Pallas kernels  25.9 us (18%)
  blocking collectives  19.6 us (13%)
  local copies, waits for them, and re-layouts  1.75 us (1%)
    pallas_call x17, Pallas kernels, run(): pl.pallas_call(body, out_shape=tuple((o[1] for o in outputs)), in_specs=[...  25.9 us
    ppermute x12, waiting for transfers between devices, along(): lax.ppermute(value, 'expert', [(i, i // RING * RING + (i + steps) % RING)...  21.3 us
    all_to_all x1, blocking collectives, exchange(): return lax.all_to_all(blocks, axis, split_axis=0, concat_axis=0, tiled=True)  19.6 us
    ppermute x12, starting transfers between devices, along(): lax.ppermute(value, 'expert', [(i, i // RING * RING + (i + steps) % RING)...  18.1 us
    all_to_all x3, starting transfers between devices, swap_rows(): lax.all_to_all(value, axes, split_axis=0, concat_axis=0, axis_index_group...  14.2 us
    all_to_all x3, waiting for transfers between devices, swap_rows(): lax.all_to_all(value, axes, split_axis=0, concat_axis=0, axis_index_group...  13.1 us
    all_to_all x1, starting transfers between devices, exchange(): return lax.all_to_all(blocks, axis, split_axis=0, concat_axis=0, tiled=True)  12.8 us
    all_to_all x1, waiting for transfers between devices, exchange(): return lax.all_to_all(blocks, axis, split_axis=0, concat_axis=0, tiled=True)  7.57 us
  transfers between devices with their start and end apart: 20, of which 11 were waited for; matrix products, arithmetic and copies ran while one was open for 0% of the time, Pallas kernels for 13%

profile of v5, /device:TPU:1, one launch (start us, length us, event | category | flops | bytes accessed | tf_op | source)
XLA Modules:
  0.0 145.4 jit_solution(9319807181862280382)
XLA Ops:
  0.6 3.1 %shard_map.102 = bf16[256,640]{1,0:T(8,128)(2,1)} custom-call(f32[2,32,256]{2,1,0:T(8,128)} %refs_1_.3, bf16[2,256,1280]{2,1,0:T(8,128)(2,1)} %refs_3_.2, bf16[2,256,1280]{2,1,0:T(8,128)(2,1)} %refs_2_.3), custom_call_target="tpu_custom_call" | custom-call | flops 83886080 | bytes 2621440 | tf_op jit(solution)/shard_map/pallas_call | solution.py:83
  3.8 12.8 %all-to-all-start = ((bf16[32,8,640]{2,1,0:T(8,128)(2,1)}), bf16[32,8,640]{2,1,0:T(8,128)(2,1)}, u32[]{:S(2)}, u32[]{:S(2)}) async-start(bf16[32,8,640]{2,1,0:T(8,128)(2,1)} %bitcast.19), calls=%async_computation | async-start | bytes 655360 | tf_op jit(solution)/shard_map/all_to_all | solution.py:35
  16.6 4.6 %shard_map.103 = (bf16[512,640]{1,0:T(8,128)(2,1)}, bf16[384,640]{1,0:T(8,128)(2,1)}, bf16[128,640]{1,0:T(8,128)(2,1)}, bf16[128,1280]{1,0:T(8,128)(2,1)}, bf16[...) custom-call(s32[1]{0:T(128)} %bitcast.refs_0_, bf16[512,640]{1,0:T(8,128)(2,1)} %bitcast.20, ...), custom_call_target="tpu_custom_call" | custom-call | flops 1677721600 | bytes 3276800 | tf_op jit(solution)/shard_map/pallas_call | solution.py:83
  22.4 1.5 %collective-permute-start.1 = (bf16[128,1280]{1,0:T(8,128)(2,1)}, bf16[128,1280]{1,0:T(8,128)(2,1)}, u32[]{:S(2)}, u32[]{:S(2)}) collective-permute-start(bf16[128,1280]{1,0:T(8,128)(2,1)} %get-tuple-element.40), channel_id=1, source_target_pairs={{0,3},{1,0},{2,1},{3,2},{4,7},{5,4},{6,5},{7,6},{8,11},{9,8},{10,9... | collective-permute-start | bytes 983048 | tf_op jit(solution)/shard_map/ppermute | solution.py:334
  23.8 7.6 %all-to-all-done = bf16[32,8,640]{2,1,0:T(8,128)(2,1)} async-done(((bf16[32,8,640]{2,1,0:T(8,128)(2,1)}), bf16[32,8,640]{2,1,0:T(8,128)(2,1)}, u32[]{:S(2)}, u32[]{:S(2)}) %all-to-all-start) | async-done | bytes 327712 | tf_op jit(solution)/shard_map/all_to_all | solution.py:35
  31.4 1.2 shard_map.104
  33.7 4.3 %collective-permute-done.2.refs_1_ = bf16[64,1280]{1,0:T(8,128)(2,1)S(1)} collective-permute-done((bf16[64,1280]{1,0:T(8,128)(2,1)S(1)}, bf16[64,1280]{1,0:T(8,128)(2,1)S(1)}, u32[]{:S(2)}, u32[]{:S(2)}) %collective-permute-start.2) | collective-permute-done | bytes 163872 | tf_op jit(solution)/shard_map/ppermute | solution.py:337
  38.1 2.9 %collective-permute-start.5 = (bf16[128,1280]{1,0:T(8,128)(2,1)S(1)}, bf16[128,1280]{1,0:T(8,128)(2,1)S(1)}, u32[]{:S(2)}, u32[]{:S(2)}) collective-permute-start(bf16[128,1280]{1,0:T(8,128)(2,1)S(1)} %shard_map.105.refs_1_.refs_0_), channel_id=1, source_target_pairs={{0,2},{1,3},{2,0},{3,1},{4,6},{5,7},{6,4},{7,5},{8,10},{9,11},{10,... | collective-permute-start | bytes 983048 | tf_op jit(solution)/shard_map/ppermute | solution.py:334
  41.2 2.4 %collective-permute-start.3 = (bf16[128,1280]{1,0:T(8,128)(2,1)S(1)}, bf16[128,1280]{1,0:T(8,128)(2,1)S(1)}, u32[]{:S(2)}, u32[]{:S(2)}) collective-permute-start(bf16[128,1280]{1,0:T(8,128)(2,1)S(1)} %shard_map.105.refs_1_.refs_0_), channel_id=1, source_target_pairs={{0,3},{1,0},{2,1},{3,2},{4,7},{5,4},{6,5},{7,6},{8,11},{9,8},{10,9... | collective-permute-start | bytes 983048 | tf_op jit(solution)/shard_map/ppermute | solution.py:334
  43.6 4.0 %collective-permute-done.5.refs_4_.refs_0_ = bf16[128,1280]{1,0:T(8,128)(2,1)S(1)} collective-permute-done((bf16[128,1280]{1,0:T(8,128)(2,1)S(1)}, bf16[128,1280]{1,0:T(8,128)(2,1)S(1)}, u32[]{:S(2)}, u32[]{:S(2)}) %collective-permute-start.5) | collective-permute-done | bytes 327712 | tf_op jit(solution)/shard_map/ppermute | solution.py:334
  49.7 2.9 %collective-permute-start.11 = (bf16[128,1280]{1,0:T(8,128)(2,1)S(1)}, bf16[128,1280]{1,0:T(8,128)(2,1)S(1)}, u32[]{:S(2)}, u32[]{:S(2)}) collective-permute-start(bf16[128,1280]{1,0:T(8,128)(2,1)S(1)} %get-tuple-element.57), channel_id=1, source_target_pairs={{0,2},{1,3},{2,0},{3,1},{4,6},{5,7},{6,4},{7,5},{8,10},{9,11},{10,... | collective-permute-start | bytes 983048 | tf_op jit(solution)/shard_map/ppermute | solution.py:334
  52.6 5.4 %collective-permute-done.4.refs_3_.refs_2_ = bf16[128,1280]{1,0:T(8,128)(2,1)S(1)} collective-permute-done((bf16[128,1280]{1,0:T(8,128)(2,1)S(1)}, bf16[128,1280]{1,0:T(8,128)(2,1)S(1)}, u32[]{:S(2)}, u32[]{:S(2)}) %collective-permute-start.4) | collective-permute-done | bytes 327712 | tf_op jit(solution)/shard_map/ppermute | solution.py:334
  58.3 3.0 %shard_map.108 = (bf16[384,640]{1,0:T(8,128)(2,1)S(1)}, bf16[128,1280]{1,0:T(8,128)(2,1)S(1)}, bf16[128,1280]{1,0:T(8,128)(2,1)S(1)}, bf16[128,1280]{1,0:T(8,128)(2,1)S(1)}) custom-call(bf16[128,1280]{1,0:T(8,128)(2,1)S(1)} %shard_map.105.refs_1_.refs_0_, bf16[128,1280]{1,0:T(8,128)(2,1)S(1)} %collective-permute-done.3.refs_2_.refs_1_, ...), custom_call_target="tpu_custom_call" | custom-call | flops 1258291200 | bytes 1638400 | tf_op jit(solution)/shard_map/pallas_call | solution.py:83
  62.1 2.8 %collective-permute-start.9 = (bf16[128,1280]{1,0:T(8,128)(2,1)S(1)}, bf16[128,1280]{1,0:T(8,128)(2,1)S(1)}, u32[]{:S(2)}, u32[]{:S(2)}) collective-permute-start(bf16[128,1280]{1,0:T(8,128)(2,1)S(1)} %get-tuple-element.54), channel_id=1, source_target_pairs={{0,1},{1,2},{2,3},{3,0},{4,5},{5,6},{6,7},{7,4},{8,9},{9,10},{10,1... | collective-permute-start | bytes 983048 | tf_op jit(solution)/shard_map/ppermute | solution.py:334
  66.4 3.0 %collective-permute-done.6.refs_3_ = bf16[128,1280]{1,0:T(8,128)(2,1)S(1)} collective-permute-done((bf16[128,1280]{1,0:T(8,128)(2,1)S(1)}, bf16[128,1280]{1,0:T(8,128)(2,1)S(1)}, u32[]{:S(2)}, u32[]{:S(2)}) %collective-permute-start.6) | collective-permute-done | bytes 327712 | tf_op jit(solution)/shard_map/ppermute | solution.py:334
  69.4 1.2 shard_map.106
  71.6 5.8 %collective-permute-done.9.refs_1_ = bf16[128,1280]{1,0:T(8,128)(2,1)S(1)} collective-permute-done((bf16[128,1280]{1,0:T(8,128)(2,1)S(1)}, bf16[128,1280]{1,0:T(8,128)(2,1)S(1)}, u32[]{:S(2)}, u32[]{:S(2)}) %collective-permute-start.9) | collective-permute-done | bytes 327712 | tf_op jit(solution)/shard_map/ppermute | solution.py:334
  77.6 1.3 collective-permute-start.12
  78.8 2.2 %shard_map.107 = bf16[640,1280]{1,0:T(8,128)(2,1)} custom-call(bf16[512,640]{1,0:T(8,128)(2,1)S(1)} %copy-done.4, bf16[128,1280]{1,0:T(8,128)(2,1)S(1)} %shard_map.105.refs_1_.refs_0_, bf16[128,1280]{1,0:T(8,128)(2,1)S(1)} %collective-permute-done.3.refs_2_.refs_1_, bf16[128,1280]{1,0:T(8,128)(2,1)S(1)} %collective-permute-done.4.refs_3_.refs_2_, ...), custom_call_target="tpu_custom_call" | custom-call | flops 838860800 | bytes 3276800 | tf_op jit(solution)/shard_map/pallas_call | solution.py:83
  81.1 1.7 %collective-permute-done.12.refs_3_ = bf16[64,1280]{1,0:T(8,128)(2,1)S(1)} collective-permute-done((bf16[64,1280]{1,0:T(8,128)(2,1)S(1)}, bf16[64,1280]{1,0:T(8,128)(2,1)S(1)}, u32[]{:S(2)}, u32[]{:S(2)}) %collective-permute-start.12) | collective-permute-done | bytes 163872 | tf_op jit(solution)/shard_map/ppermute | solution.py:337
  83.1 19.6 %all_to_all.25 = bf16[32,8,640]{2,1,0:T(8,128)(2,1)S(1)} all-to-all(bf16[32,8,640]{2,1,0:T(8,128)(2,1)S(1)} %bitcast.16), channel_id=1, replica_groups=mesh['dp'=32,'expert'=8] {'dp'}, dimensions={0} | all-to-all | bytes 655360 | tf_op jit(solution)/shard_map/all_to_all | solution.py:35
  102.7 2.4 %shard_map.112 = (bf16[2,32,256]{2,1,0:T(8,128)(2,1)S(1)}, bf16[2,32,256]{2,1,0:T(8,128)(2,1)S(1)}, bf16[2,32,1280]{2,1,0:T(8,128)(2,1)S(1)}, f32[16,8,384]{2,1,0:T(8,128)}) custom-call(bf16[256,640]{1,0:T(8,128)(2,1)S(1)} %bitcast.15, f32[2,32,256]{2,1,0:T(8,128)S(1)} %copy-done.9, bf16[2,256,1280]{2,1,0:T(8,128)(2,1)S(1)} %copy-done.3, ...), custom_call_target="tpu_custom_call" | custom-call | flops 125829120 | bytes 2621440 | tf_op jit(solution)/shard_map/pallas_call | solution.py:83
  105.1 6.2 %all-to-all-start.2 = ((f32[16,8,384]{2,1,0:T(8,128)}), f32[16,8,384]{2,1,0:T(8,128)S(1)}, u32[]{:S(2)}, u32[]{:S(2)}) async-start(f32[16,8,384]{2,1,0:T(8,128)} %get-tuple-element.63), calls=%async_computation.2 | async-start | bytes 393216 | tf_op jit(solution)/shard_map/all_to_all | solution.py:415
  111.3 1.9 %shard_map.113 = bf16[2,256,1280]{2,1,0:T(8,128)(2,1)} custom-call(bf16[2,32,256]{2,1,0:T(8,128)(2,1)S(1)} %get-tuple-element.60.refs_0_, bf16[2,32,256]{2,1,0:T(8,128)(2,1)S(1)} %get-tuple-element.61.refs_1_, bf16[2,32,1280]{2,1,0:T(8,128)(2,1)S(1)} %get-tuple-element.62.refs_2_, bf16[32,1280]{1,0:T(8,128)(2,1)S(1)} %copy-done.13), custom_call_target="tpu_custom_call" | custom-call | flops 83886080 | bytes 1310720 | tf_op jit(solution)/shard_map/pallas_call | solution.py:83
  113.2 5.1 %all-to-all-done.2.refs_0_ = f32[16,8,384]{2,1,0:T(8,128)S(1)} async-done(((f32[16,8,384]{2,1,0:T(8,128)}), f32[16,8,384]{2,1,0:T(8,128)S(1)}, u32[]{:S(2)}, u32[]{:S(2)}) %all-to-all-start.2) | async-done | bytes 196640 | tf_op jit(solution)/shard_map/all_to_all | solution.py:415
  119.0 3.5 %all-to-all-start.3 = ((bf16[16,8,384]{2,1,0:T(8,128)(2,1)}), bf16[16,8,384]{2,1,0:T(8,128)(2,1)S(1)}, u32[]{:S(2)}, u32[]{:S(2)}) async-start(bf16[16,8,384]{2,1,0:T(8,128)(2,1)} %shard_map.114), calls=%async_computation.3 | async-start | bytes 196608 | tf_op jit(solution)/shard_map/all_to_all | solution.py:415
  123.4 2.5 %collective-permute-start.13 = (bf16[128,1280]{1,0:T(8,128)(2,1)S(1)}, bf16[128,1280]{1,0:T(8,128)(2,1)S(1)}, u32[]{:S(2)}, u32[]{:S(2)}) collective-permute-start(bf16[128,1280]{1,0:T(8,128)(2,1)S(1)} %shard_map.116.refs_0_), channel_id=1, source_target_pairs={{0,3},{1,0},{2,1},{3,2},{4,7},{5,4},{6,5},{7,6},{8,11},{9,8},{10,9... | collective-permute-start | bytes 983048 | tf_op jit(solution)/shard_map/ppermute | solution.py:334
  125.9 6.5 %all-to-all-done.3.refs_0_ = bf16[16,8,384]{2,1,0:T(8,128)(2,1)S(1)} async-done(((bf16[16,8,384]{2,1,0:T(8,128)(2,1)}), bf16[16,8,384]{2,1,0:T(8,128)(2,1)S(1)}, u32[]{:S(2)}, u32[]{:S(2)}) %all-to-all-start.3) | async-done | bytes 98336 | tf_op jit(solution)/shard_map/all_to_all | solution.py:415
  133.1 4.5 %all-to-all-start.4 = ((f32[16,8,384]{2,1,0:T(8,128)}), f32[16,8,384]{2,1,0:T(8,128)S(1)}, u32[]{:S(2)}, u32[]{:S(2)}) async-start(f32[16,8,384]{2,1,0:T(8,128)} %shard_map.115), calls=%async_computation.4 | async-start | bytes 393216 | tf_op jit(solution)/shard_map/all_to_all | solution.py:415
  137.6 3.2 %collective-permute-done.14.refs_2_ = bf16[128,1280]{1,0:T(8,128)(2,1)S(1)} collective-permute-done((bf16[128,1280]{1,0:T(8,128)(2,1)S(1)}, bf16[128,1280]{1,0:T(8,128)(2,1)S(1)}, u32[]{:S(2)}, u32[]{:S(2)}) %collective-permute-start.14) | collective-permute-done | bytes 327712 | tf_op jit(solution)/shard_map/ppermute | solution.py:334
  140.8 2.4 %shard_map.117 = bf16[1280,640]{1,0:T(8,128)(2,1)} custom-call(bf16[128,1280]{1,0:T(8,128)(2,1)S(1)} %shard_map.116.refs_0_, bf16[128,1280]{1,0:T(8,128)(2,1)S(1)} %collective-permute-done.13.refs_1_, bf16[128,1280]{1,0:T(8,128)(2,1)S(1)} %collective-permute-done.14.refs_2_, bf16[128,1280]{1,0:T(8,128)(2,1)S(1)} %collective-permute-done.15.refs_3_, ...), custom_call_target="tpu_custom_call" | custom-call | flops 838860800 | bytes 3276800 | tf_op jit(solution)/shard_map/pallas_call | solution.py:83
  143.2 1.5 %all-to-all-done.4.refs_0_ = f32[16,8,384]{2,1,0:T(8,128)S(1)} async-done(((f32[16,8,384]{2,1,0:T(8,128)}), f32[16,8,384]{2,1,0:T(8,128)S(1)}, u32[]{:S(2)}, u32[]{:S(2)}) %all-to-all-start.4) | async-done | bytes 196640 | tf_op jit(solution)/shard_map/all_to_all | solution.py:415
  (56 shorter events, 11.8 us)
Async XLA Ops:
  3.8 27.6 %all-to-all-start = ((bf16[32,8,640]{2,1,0:T(8,128)(2,1)}), bf16[32,8,640]{2,1,0:T(8,128)(2,1)}, u32[]{:S(2)}, u32[]{:S(2)}) async-start(bf16[32,8,640]{2,1,0:T(8,128)(2,1)} %bitcast.19), calls=%async_computation | async-start | bytes 655360 | tf_op jit(solution)/shard_map/all_to_all | solution.py:35
  16.6 31.0 %copy-start = (bf16[1,640,1280]{2,1,0:T(8,128)(2,1)S(1)}, bf16[1,640,1280]{2,1,0:T(8,128)(2,1)}, u32[]{:S(2)}) copy-start(bf16[1,640,1280]{2,1,0:T(8,128)(2,1)} %param.13) | copy-start | bytes 4915204
  16.6 31.0 %copy-start.1 = (bf16[1,1280,640]{2,1,0:T(8,128)(2,1)S(1)}, bf16[1,1280,640]{2,1,0:T(8,128)(2,1)}, u32[]{:S(2)}) copy-start(bf16[1,1280,640]{2,1,0:T(8,128)(2,1)} %param.12) | copy-start | bytes 4915204
  21.2 12.5 %collective-permute-start = (bf16[128,1280]{1,0:T(8,128)(2,1)}, bf16[128,1280]{1,0:T(8,128)(2,1)}, u32[]{:S(2)}, u32[]{:S(2)}) collective-permute-start(bf16[128,1280]{1,0:T(8,128)(2,1)} %get-tuple-element.39), channel_id=1, source_target_pairs={{0,1},{1,2},{2,3},{3,0},{4,5},{5,6},{6,7},{7,4},{8,9},{9,10},{10,1... | collective-permute-start | bytes 983048 | tf_op jit(solution)/shard_map/ppermute | solution.py:334
  22.4 11.3 %collective-permute-start.1 = (bf16[128,1280]{1,0:T(8,128)(2,1)}, bf16[128,1280]{1,0:T(8,128)(2,1)}, u32[]{:S(2)}, u32[]{:S(2)}) collective-permute-start(bf16[128,1280]{1,0:T(8,128)(2,1)} %get-tuple-element.40), channel_id=1, source_target_pairs={{0,3},{1,0},{2,1},{3,2},{4,7},{5,4},{6,5},{7,6},{8,11},{9,8},{10,9... | collective-permute-start | bytes 983048 | tf_op jit(solution)/shard_map/ppermute | solution.py:334
  32.6 32.8 %copy-start.11 = (bf16[64,1280]{1,0:T(8,128)(2,1)}, bf16[64,1280]{1,0:T(8,128)(2,1)S(1)}, u32[]{:S(2)}) copy-start(bf16[64,1280]{1,0:T(8,128)(2,1)S(1)} %get-tuple-element.66.refs_0_) | copy-start | bytes 491524
  32.7 5.4 %collective-permute-start.2 = (bf16[64,1280]{1,0:T(8,128)(2,1)S(1)}, bf16[64,1280]{1,0:T(8,128)(2,1)S(1)}, u32[]{:S(2)}, u32[]{:S(2)}) collective-permute-start(bf16[64,1280]{1,0:T(8,128)(2,1)S(1)} %get-tuple-element.44.refs_0_), channel_id=1, source_target_pairs={{0,4},{1,5},{2,6},{3,7},{4,0},{5,1},{6,2},{7,3},{8,12},{9,13},{10,... | collective-permute-start | bytes 491528 | tf_op jit(solution)/shard_map/ppermute | solution.py:337
  38.1 9.5 %collective-permute-start.5 = (bf16[128,1280]{1,0:T(8,128)(2,1)S(1)}, bf16[128,1280]{1,0:T(8,128)(2,1)S(1)}, u32[]{:S(2)}, u32[]{:S(2)}) collective-permute-start(bf16[128,1280]{1,0:T(8,128)(2,1)S(1)} %shard_map.105.refs_1_.refs_0_), channel_id=1, source_target_pairs={{0,2},{1,3},{2,0},{3,1},{4,6},{5,7},{6,4},{7,5},{8,10},{9,11},{10,... | collective-permute-start | bytes 983048 | tf_op jit(solution)/shard_map/ppermute | solution.py:334
  40.9 17.1 %collective-permute-start.4 = (bf16[128,1280]{1,0:T(8,128)(2,1)S(1)}, bf16[128,1280]{1,0:T(8,128)(2,1)S(1)}, u32[]{:S(2)}, u32[]{:S(2)}) collective-permute-start(bf16[128,1280]{1,0:T(8,128)(2,1)S(1)} %shard_map.105.refs_1_.refs_0_), channel_id=1, source_target_pairs={{0,1},{1,2},{2,3},{3,0},{4,5},{5,6},{6,7},{7,4},{8,9},{9,10},{10,1... | collective-permute-start | bytes 983048 | tf_op jit(solution)/shard_map/ppermute | solution.py:334
  41.2 16.8 %collective-permute-start.3 = (bf16[128,1280]{1,0:T(8,128)(2,1)S(1)}, bf16[128,1280]{1,0:T(8,128)(2,1)S(1)}, u32[]{:S(2)}, u32[]{:S(2)}) collective-permute-start(bf16[128,1280]{1,0:T(8,128)(2,1)S(1)} %shard_map.105.refs_1_.refs_0_), channel_id=1, source_target_pairs={{0,3},{1,0},{2,1},{3,2},{4,7},{5,4},{6,5},{7,6},{8,11},{9,8},{10,9... | collective-permute-start | bytes 983048 | tf_op jit(solution)/shard_map/ppermute | solution.py:334
  48.5 9.5 %copy-start.14 = (bf16[128,1280]{1,0:T(8,128)(2,1)S(1)}, bf16[128,1280]{1,0:T(8,128)(2,1)}, u32[]{:S(2)}) copy-start(bf16[128,1280]{1,0:T(8,128)(2,1)} %get-tuple-element.45) | copy-start | bytes 983044
  48.5 9.8 %copy-start.7 = (bf16[384,640]{1,0:T(8,128)(2,1)S(1)}, bf16[384,640]{1,0:T(8,128)(2,1)}, u32[]{:S(2)}) copy-start(bf16[384,640]{1,0:T(8,128)(2,1)} %get-tuple-element.52.refs_3_) | copy-start | bytes 1474564
  49.7 21.9 %collective-permute-start.11 = (bf16[128,1280]{1,0:T(8,128)(2,1)S(1)}, bf16[128,1280]{1,0:T(8,128)(2,1)S(1)}, u32[]{:S(2)}, u32[]{:S(2)}) collective-permute-start(bf16[128,1280]{1,0:T(8,128)(2,1)S(1)} %get-tuple-element.57), channel_id=1, source_target_pairs={{0,2},{1,3},{2,0},{3,1},{4,6},{5,7},{6,4},{7,5},{8,10},{9,11},{10,... | collective-permute-start | bytes 983048 | tf_op jit(solution)/shard_map/ppermute | solution.py:334
  58.0 11.3 %collective-permute-start.6 = (bf16[128,1280]{1,0:T(8,128)(2,1)S(1)}, bf16[128,1280]{1,0:T(8,128)(2,1)S(1)}, u32[]{:S(2)}, u32[]{:S(2)}) collective-permute-start(bf16[128,1280]{1,0:T(8,128)(2,1)S(1)} %copy-done.14), channel_id=1, source_target_pairs={{0,2},{1,3},{2,0},{3,1},{4,6},{5,7},{6,4},{7,5},{8,10},{9,11},{10,... | collective-permute-start | bytes 983048 | tf_op jit(solution)/shard_map/ppermute | solution.py:334
  58.3 11.0 %copy-start.8 = (bf16[128,1280]{1,0:T(8,128)(2,1)S(1)}, bf16[128,1280]{1,0:T(8,128)(2,1)}, u32[]{:S(2)}) copy-start(bf16[128,1280]{1,0:T(8,128)(2,1)} %get-tuple-element.38.refs_0_) | copy-start | bytes 983044
  62.1 16.8 %copy-start.4 = (bf16[512,640]{1,0:T(8,128)(2,1)S(1)}, bf16[512,640]{1,0:T(8,128)(2,1)}, u32[]{:S(2)}) copy-start(bf16[512,640]{1,0:T(8,128)(2,1)} %get-tuple-element.49.refs_0_) | copy-start | bytes 1966084
  62.1 15.3 %collective-permute-start.9 = (bf16[128,1280]{1,0:T(8,128)(2,1)S(1)}, bf16[128,1280]{1,0:T(8,128)(2,1)S(1)}, u32[]{:S(2)}, u32[]{:S(2)}) collective-permute-start(bf16[128,1280]{1,0:T(8,128)(2,1)S(1)} %get-tuple-element.54), channel_id=1, source_target_pairs={{0,1},{1,2},{2,3},{3,0},{4,5},{5,6},{6,7},{7,4},{8,9},{9,10},{10,1... | collective-permute-start | bytes 983048 | tf_op jit(solution)/shard_map/ppermute | solution.py:334
  64.8 12.6 %collective-permute-start.10 = (bf16[128,1280]{1,0:T(8,128)(2,1)S(1)}, bf16[128,1280]{1,0:T(8,128)(2,1)S(1)}, u32[]{:S(2)}, u32[]{:S(2)}) collective-permute-start(bf16[128,1280]{1,0:T(8,128)(2,1)S(1)} %get-tuple-element.55), channel_id=1, source_target_pairs={{0,3},{1,0},{2,1},{3,2},{4,7},{5,4},{6,5},{7,6},{8,11},{9,8},{10,9... | collective-permute-start | bytes 983048 | tf_op jit(solution)/shard_map/ppermute | solution.py:334
  65.4 15.7 %collective-permute-start.7 = (bf16[64,1280]{1,0:T(8,128)(2,1)S(1)}, bf16[64,1280]{1,0:T(8,128)(2,1)S(1)}, u32[]{:S(2)}, u32[]{:S(2)}) collective-permute-start(bf16[64,1280]{1,0:T(8,128)(2,1)S(1)} %get-tuple-element.66.refs_0_), channel_id=1, source_target_pairs={{0,4},{1,5},{2,6},{3,7},{4,0},{5,1},{6,2},{7,3},{8,12},{9,13},{10,... | collective-permute-start | bytes 491528 | tf_op jit(solution)/shard_map/ppermute | solution.py:337
  70.6 10.5 %collective-permute-start.8 = (bf16[64,1280]{1,0:T(8,128)(2,1)S(1)}, bf16[64,1280]{1,0:T(8,128)(2,1)S(1)}, u32[]{:S(2)}, u32[]{:S(2)}) collective-permute-start(bf16[64,1280]{1,0:T(8,128)(2,1)S(1)} %get-tuple-element.51), channel_id=1, source_target_pairs={{0,4},{1,5},{2,6},{3,7},{4,0},{5,1},{6,2},{7,3},{8,12},{9,13},{10,... | collective-permute-start | bytes 491528 | tf_op jit(solution)/shard_map/ppermute | solution.py:337
  77.6 5.2 %collective-permute-start.12 = (bf16[64,1280]{1,0:T(8,128)(2,1)S(1)}, bf16[64,1280]{1,0:T(8,128)(2,1)S(1)}, u32[]{:S(2)}, u32[]{:S(2)}) collective-permute-start(bf16[64,1280]{1,0:T(8,128)(2,1)S(1)} %get-tuple-element.59), channel_id=1, source_target_pairs={{0,4},{1,5},{2,6},{3,7},{4,0},{5,1},{6,2},{7,3},{8,12},{9,13},{10,... | collective-permute-start | bytes 491528 | tf_op jit(solution)/shard_map/ppermute | solution.py:337
  78.8 23.8 %copy-start.3 = (bf16[2,256,1280]{2,1,0:T(8,128)(2,1)S(1)}, bf16[2,256,1280]{2,1,0:T(8,128)(2,1)}, u32[]{:S(2)}) copy-start(bf16[2,256,1280]{2,1,0:T(8,128)(2,1)} %refs_2_.3) | copy-start | bytes 3932164
  81.1 21.6 %copy-start.2 = (bf16[2,256,1280]{2,1,0:T(8,128)(2,1)S(1)}, bf16[2,256,1280]{2,1,0:T(8,128)(2,1)}, u32[]{:S(2)}) copy-start(bf16[2,256,1280]{2,1,0:T(8,128)(2,1)} %refs_3_.2) | copy-start | bytes 3932164
  81.1 21.6 %copy-start.9 = (f32[2,32,256]{2,1,0:T(8,128)S(1)}, f32[2,32,256]{2,1,0:T(8,128)}, u32[]{:S(2)}) copy-start(f32[2,32,256]{2,1,0:T(8,128)} %refs_1_.3) | copy-start | bytes 196612
  105.1 17.4 %copy-start.12 = (bf16[64,1280]{1,0:T(8,128)(2,1)S(1)}, bf16[64,1280]{1,0:T(8,128)(2,1)}, u32[]{:S(2)}) copy-start(bf16[64,1280]{1,0:T(8,128)(2,1)} %copy-done.11) | copy-start | bytes 491524
  105.1 13.2 %all-to-all-start.2 = ((f32[16,8,384]{2,1,0:T(8,128)}), f32[16,8,384]{2,1,0:T(8,128)S(1)}, u32[]{:S(2)}, u32[]{:S(2)}) async-start(f32[16,8,384]{2,1,0:T(8,128)} %get-tuple-element.63), calls=%async_computation.2 | async-start | bytes 393216 | tf_op jit(solution)/shard_map/all_to_all | solution.py:415
  111.3 29.5 %copy-start.6 = (bf16[384,640]{1,0:T(8,128)(2,1)S(1)}, bf16[384,640]{1,0:T(8,128)(2,1)}, u32[]{:S(2)}) copy-start(bf16[384,640]{1,0:T(8,128)(2,1)} %copy-done.5) | copy-start | bytes 1474564
  119.0 13.4 %all-to-all-start.3 = ((bf16[16,8,384]{2,1,0:T(8,128)(2,1)}), bf16[16,8,384]{2,1,0:T(8,128)(2,1)S(1)}, u32[]{:S(2)}, u32[]{:S(2)}) async-start(bf16[16,8,384]{2,1,0:T(8,128)(2,1)} %shard_map.114), calls=%async_computation.3 | async-start | bytes 196608 | tf_op jit(solution)/shard_map/all_to_all | solution.py:415
  122.5 15.1 %collective-permute-start.15 = (bf16[128,1280]{1,0:T(8,128)(2,1)S(1)}, bf16[128,1280]{1,0:T(8,128)(2,1)S(1)}, u32[]{:S(2)}, u32[]{:S(2)}) collective-permute-start(bf16[128,1280]{1,0:T(8,128)(2,1)S(1)} %shard_map.116.refs_0_), channel_id=1, source_target_pairs={{0,2},{1,3},{2,0},{3,1},{4,6},{5,7},{6,4},{7,5},{8,10},{9,11},{10,... | collective-permute-start | bytes 983048 | tf_op jit(solution)/shard_map/ppermute | solution.py:334
  123.2 17.6 %collective-permute-start.14 = (bf16[128,1280]{1,0:T(8,128)(2,1)S(1)}, bf16[128,1280]{1,0:T(8,128)(2,1)S(1)}, u32[]{:S(2)}, u32[]{:S(2)}) collective-permute-start(bf16[128,1280]{1,0:T(8,128)(2,1)S(1)} %shard_map.116.refs_0_), channel_id=1, source_target_pairs={{0,1},{1,2},{2,3},{3,0},{4,5},{5,6},{6,7},{7,4},{8,9},{9,10},{10,1... | collective-permute-start | bytes 983048 | tf_op jit(solution)/shard_map/ppermute | solution.py:334
  123.4 17.4 %collective-permute-start.13 = (bf16[128,1280]{1,0:T(8,128)(2,1)S(1)}, bf16[128,1280]{1,0:T(8,128)(2,1)S(1)}, u32[]{:S(2)}, u32[]{:S(2)}) collective-permute-start(bf16[128,1280]{1,0:T(8,128)(2,1)S(1)} %shard_map.116.refs_0_), channel_id=1, source_target_pairs={{0,3},{1,0},{2,1},{3,2},{4,7},{5,4},{6,5},{7,6},{8,11},{9,8},{10,9... | collective-permute-start | bytes 983048 | tf_op jit(solution)/shard_map/ppermute | solution.py:334
  133.1 11.6 %all-to-all-start.4 = ((f32[16,8,384]{2,1,0:T(8,128)}), f32[16,8,384]{2,1,0:T(8,128)S(1)}, u32[]{:S(2)}, u32[]{:S(2)}) async-start(f32[16,8,384]{2,1,0:T(8,128)} %shard_map.115), calls=%async_computation.4 | async-start | bytes 393216 | tf_op jit(solution)/shard_map/all_to_all | solution.py:415
  (3 other events, 10.3 us)

commit v6 on v5

--- a/solution.py
+++ b/solution.py
@@ -417,8 +417,8 @@
     def spread_sum(parts, dtype, count):
         return kernel_call(total_kernel, "v", [("v", shape(dtype, count, rows, LANES))], small, tokens.nbytes)(parts)[0]
 
-    parts = after(swap_rows(router_part, ("dp", "expert"), teams), grad_x)
-    parts = after(swap_rows(spread_sum(parts, BF, len(teams)), "dp", peers), grad_w_out)
+    parts = swap_rows(router_part, ("dp", "expert"), teams)
+    parts = after(swap_rows(spread_sum(parts, BF, len(teams)), "dp", peers), grad_x)
     parts = swap_rows(spread_sum(parts, F32, team), ("dp", "expert"), teams)
     (grad_router,) = kernel_call(rows_kernel, "v", [("v", shape(F32, slots, width))], small, tokens.nbytes)(
         after(parts, grad_w_in)

time: 146 us -> 145 us (level)
  blocking collectives: 19.6 us -> 32.4 us
  waiting for transfers between devices: 48 us -> 41 us
  starting transfers between devices: 49.4 us -> 43.3 us
    all_to_all x0 -> x1, blocking collectives: none -> 12.8 us  [swap_rows(): lax.all_to_all(value, axes, split_axis=0, concat_axis=0, axis_index_group...]
    all_to_all x3 -> x2, waiting for transfers between devices: 13.1 us -> 6.06 us  [swap_rows(): lax.all_to_all(value, axes, split_axis=0, concat_axis=0, axis_index_group...]
    all_to_all x3 -> x2, starting transfers between devices: 14.2 us -> 8.14 us  [swap_rows(): lax.all_to_all(value, axes, split_axis=0, concat_axis=0, axis_index_group...]
  transfers between devices with their start and end apart: 20 -> 19, of which waited for: 11 -> 10; matrix products, arithmetic and copies ran while one was open for 0% -> 0% of each run, Pallas kernels for 13% -> 13%
where the time goes in v6:
time: 145 us; the launch traced here: 144 us
  starting transfers between devices  43.3 us (30%)
  waiting for transfers between devices  41 us (28%)
  blocking collectives  32.4 us (22%)
  Pallas kernels  25.2 us (17%)
  local copies, waits for them, and re-layouts  1.75 us (1%)
    pallas_call x17, Pallas kernels, run(): pl.pallas_call(body, out_shape=tuple((o[1] for o in outputs)), in_specs=[...  25.2 us
    ppermute x12, waiting for transfers between devices, along(): lax.ppermute(value, 'expert', [(i, i // RING * RING + (i + steps) % RING)...  21.3 us
    all_to_all x1, blocking collectives, exchange(): return lax.all_to_all(blocks, axis, split_axis=0, concat_axis=0, tiled=True)  19.6 us
    ppermute x12, starting transfers between devices, along(): lax.ppermute(value, 'expert', [(i, i // RING * RING + (i + steps) % RING)...  18.1 us
    all_to_all x1, blocking collectives, swap_rows(): lax.all_to_all(value, axes, split_axis=0, concat_axis=0, axis_index_group...  12.8 us
    all_to_all x1, starting transfers between devices, exchange(): return lax.all_to_all(blocks, axis, split_axis=0, concat_axis=0, tiled=True)  12.8 us
    all_to_all x2, starting transfers between devices, swap_rows(): lax.all_to_all(value, axes, split_axis=0, concat_axis=0, axis_index_group...  8.14 us
    all_to_all x1, waiting for transfers between devices, exchange(): return lax.all_to_all(blocks, axis, split_axis=0, concat_axis=0, tiled=True)  7.58 us
  transfers between devices with their start and end apart: 19, of which 10 were waited for; matrix products, arithmetic and copies ran while one was open for 0% of the time, Pallas kernels for 13%

profile of v6, /device:TPU:1, one launch (start us, length us, event | category | flops | bytes accessed | tf_op | source)
XLA Modules:
  0.0 144.5 jit_solution(15730143161089244970)
XLA Ops:
  0.6 3.1 %shard_map.102 = bf16[256,640]{1,0:T(8,128)(2,1)} custom-call(f32[2,32,256]{2,1,0:T(8,128)} %refs_1_.3, bf16[2,256,1280]{2,1,0:T(8,128)(2,1)} %refs_3_.2, bf16[2,256,1280]{2,1,0:T(8,128)(2,1)} %refs_2_.3), custom_call_target="tpu_custom_call" | custom-call | flops 83886080 | bytes 2621440 | tf_op jit(solution)/shard_map/pallas_call | solution.py:83
  3.8 12.8 %all-to-all-start = ((bf16[32,8,640]{2,1,0:T(8,128)(2,1)}), bf16[32,8,640]{2,1,0:T(8,128)(2,1)}, u32[]{:S(2)}, u32[]{:S(2)}) async-start(bf16[32,8,640]{2,1,0:T(8,128)(2,1)} %bitcast.19), calls=%async_computation | async-start | bytes 655360 | tf_op jit(solution)/shard_map/all_to_all | solution.py:35
  16.6 4.5 %shard_map.103 = (bf16[512,640]{1,0:T(8,128)(2,1)}, bf16[384,640]{1,0:T(8,128)(2,1)}, bf16[128,640]{1,0:T(8,128)(2,1)}, bf16[128,1280]{1,0:T(8,128)(2,1)}, bf16[...) custom-call(s32[1]{0:T(128)} %bitcast.refs_0_, bf16[512,640]{1,0:T(8,128)(2,1)} %bitcast.20, ...), custom_call_target="tpu_custom_call" | custom-call | flops 1677721600 | bytes 3276800 | tf_op jit(solution)/shard_map/pallas_call | solution.py:83
  21.1 1.2 collective-permute-start
  22.4 1.5 %collective-permute-start.1 = (bf16[128,1280]{1,0:T(8,128)(2,1)}, bf16[128,1280]{1,0:T(8,128)(2,1)}, u32[]{:S(2)}, u32[]{:S(2)}) collective-permute-start(bf16[128,1280]{1,0:T(8,128)(2,1)} %get-tuple-element.39), channel_id=1, source_target_pairs={{0,3},{1,0},{2,1},{3,2},{4,7},{5,4},{6,5},{7,6},{8,11},{9,8},{10,9... | collective-permute-start | bytes 983048 | tf_op jit(solution)/shard_map/ppermute | solution.py:334
  23.8 7.6 %all-to-all-done = bf16[32,8,640]{2,1,0:T(8,128)(2,1)} async-done(((bf16[32,8,640]{2,1,0:T(8,128)(2,1)}), bf16[32,8,640]{2,1,0:T(8,128)(2,1)}, u32[]{:S(2)}, u32[]{:S(2)}) %all-to-all-start) | async-done | bytes 327712 | tf_op jit(solution)/shard_map/all_to_all | solution.py:35
  31.4 1.2 shard_map.104
  33.7 4.3 %collective-permute-done.2.refs_1_ = bf16[64,1280]{1,0:T(8,128)(2,1)S(1)} collective-permute-done((bf16[64,1280]{1,0:T(8,128)(2,1)S(1)}, bf16[64,1280]{1,0:T(8,128)(2,1)S(1)}, u32[]{:S(2)}, u32[]{:S(2)}) %collective-permute-start.2) | collective-permute-done | bytes 163872 | tf_op jit(solution)/shard_map/ppermute | solution.py:337
  38.1 2.9 %collective-permute-start.5 = (bf16[128,1280]{1,0:T(8,128)(2,1)S(1)}, bf16[128,1280]{1,0:T(8,128)(2,1)S(1)}, u32[]{:S(2)}, u32[]{:S(2)}) collective-permute-start(bf16[128,1280]{1,0:T(8,128)(2,1)S(1)} %shard_map.105.refs_1_.refs_0_), channel_id=1, source_target_pairs={{0,2},{1,3},{2,0},{3,1},{4,6},{5,7},{6,4},{7,5},{8,10},{9,11},{10,... | collective-permute-start | bytes 983048 | tf_op jit(solution)/shard_map/ppermute | solution.py:334
  41.2 2.4 %collective-permute-start.3 = (bf16[128,1280]{1,0:T(8,128)(2,1)S(1)}, bf16[128,1280]{1,0:T(8,128)(2,1)S(1)}, u32[]{:S(2)}, u32[]{:S(2)}) collective-permute-start(bf16[128,1280]{1,0:T(8,128)(2,1)S(1)} %shard_map.105.refs_1_.refs_0_), channel_id=1, source_target_pairs={{0,3},{1,0},{2,1},{3,2},{4,7},{5,4},{6,5},{7,6},{8,11},{9,8},{10,9... | collective-permute-start | bytes 983048 | tf_op jit(solution)/shard_map/ppermute | solution.py:334
  43.6 4.0 %collective-permute-done.5.refs_4_.refs_0_ = bf16[128,1280]{1,0:T(8,128)(2,1)S(1)} collective-permute-done((bf16[128,1280]{1,0:T(8,128)(2,1)S(1)}, bf16[128,1280]{1,0:T(8,128)(2,1)S(1)}, u32[]{:S(2)}, u32[]{:S(2)}) %collective-permute-start.5) | collective-permute-done | bytes 327712 | tf_op jit(solution)/shard_map/ppermute | solution.py:334
  49.7 2.9 %collective-permute-start.11 = (bf16[128,1280]{1,0:T(8,128)(2,1)S(1)}, bf16[128,1280]{1,0:T(8,128)(2,1)S(1)}, u32[]{:S(2)}, u32[]{:S(2)}) collective-permute-start(bf16[128,1280]{1,0:T(8,128)(2,1)S(1)} %get-tuple-element.56), channel_id=1, source_target_pairs={{0,2},{1,3},{2,0},{3,1},{4,6},{5,7},{6,4},{7,5},{8,10},{9,11},{10,... | collective-permute-start | bytes 983048 | tf_op jit(solution)/shard_map/ppermute | solution.py:334
  52.6 5.4 %collective-permute-done.4.refs_3_.refs_2_ = bf16[128,1280]{1,0:T(8,128)(2,1)S(1)} collective-permute-done((bf16[128,1280]{1,0:T(8,128)(2,1)S(1)}, bf16[128,1280]{1,0:T(8,128)(2,1)S(1)}, u32[]{:S(2)}, u32[]{:S(2)}) %collective-permute-start.4) | collective-permute-done | bytes 327712 | tf_op jit(solution)/shard_map/ppermute | solution.py:334
  58.3 3.0 %shard_map.108 = (bf16[384,640]{1,0:T(8,128)(2,1)S(1)}, bf16[128,1280]{1,0:T(8,128)(2,1)S(1)}, bf16[128,1280]{1,0:T(8,128)(2,1)S(1)}, bf16[128,1280]{1,0:T(8,128)(2,1)S(1)}) custom-call(bf16[128,1280]{1,0:T(8,128)(2,1)S(1)} %shard_map.105.refs_1_.refs_0_, bf16[128,1280]{1,0:T(8,128)(2,1)S(1)} %collective-permute-done.3.refs_2_.refs_1_, ...), custom_call_target="tpu_custom_call" | custom-call | flops 1258291200 | bytes 1638400 | tf_op jit(solution)/shard_map/pallas_call | solution.py:83
  62.1 2.8 %collective-permute-start.9 = (bf16[128,1280]{1,0:T(8,128)(2,1)S(1)}, bf16[128,1280]{1,0:T(8,128)(2,1)S(1)}, u32[]{:S(2)}, u32[]{:S(2)}) collective-permute-start(bf16[128,1280]{1,0:T(8,128)(2,1)S(1)} %get-tuple-element.53), channel_id=1, source_target_pairs={{0,1},{1,2},{2,3},{3,0},{4,5},{5,6},{6,7},{7,4},{8,9},{9,10},{10,1... | collective-permute-start | bytes 983048 | tf_op jit(solution)/shard_map/ppermute | solution.py:334
  66.4 3.0 %collective-permute-done.6.refs_3_ = bf16[128,1280]{1,0:T(8,128)(2,1)S(1)} collective-permute-done((bf16[128,1280]{1,0:T(8,128)(2,1)S(1)}, bf16[128,1280]{1,0:T(8,128)(2,1)S(1)}, u32[]{:S(2)}, u32[]{:S(2)}) %collective-permute-start.6) | collective-permute-done | bytes 327712 | tf_op jit(solution)/shard_map/ppermute | solution.py:334
  69.3 1.2 shard_map.106
  71.6 5.8 %collective-permute-done.9.refs_1_ = bf16[128,1280]{1,0:T(8,128)(2,1)S(1)} collective-permute-done((bf16[128,1280]{1,0:T(8,128)(2,1)S(1)}, bf16[128,1280]{1,0:T(8,128)(2,1)S(1)}, u32[]{:S(2)}, u32[]{:S(2)}) %collective-permute-start.9) | collective-permute-done | bytes 327712 | tf_op jit(solution)/shard_map/ppermute | solution.py:334
  77.6 1.3 collective-permute-start.12
  78.8 2.2 %shard_map.107 = bf16[640,1280]{1,0:T(8,128)(2,1)} custom-call(bf16[512,640]{1,0:T(8,128)(2,1)S(1)} %copy-done.4, bf16[128,1280]{1,0:T(8,128)(2,1)S(1)} %shard_map.105.refs_1_.refs_0_, bf16[128,1280]{1,0:T(8,128)(2,1)S(1)} %collective-permute-done.3.refs_2_.refs_1_, bf16[128,1280]{1,0:T(8,128)(2,1)S(1)} %collective-permute-done.4.refs_3_.refs_2_, ...), custom_call_target="tpu_custom_call" | custom-call | flops 838860800 | bytes 3276800 | tf_op jit(solution)/shard_map/pallas_call | solution.py:83
  81.1 1.7 %collective-permute-done.12.refs_3_ = bf16[64,1280]{1,0:T(8,128)(2,1)S(1)} collective-permute-done((bf16[64,1280]{1,0:T(8,128)(2,1)S(1)}, bf16[64,1280]{1,0:T(8,128)(2,1)S(1)}, u32[]{:S(2)}, u32[]{:S(2)}) %collective-permute-start.12) | collective-permute-done | bytes 163872 | tf_op jit(solution)/shard_map/ppermute | solution.py:337
  83.1 19.6 %all_to_all.25 = bf16[32,8,640]{2,1,0:T(8,128)(2,1)S(1)} all-to-all(bf16[32,8,640]{2,1,0:T(8,128)(2,1)S(1)} %bitcast.16), channel_id=1, replica_groups=mesh['dp'=32,'expert'=8] {'dp'}, dimensions={0} | all-to-all | bytes 655360 | tf_op jit(solution)/shard_map/all_to_all | solution.py:35
  102.7 1.7 %shard_map.112 = (bf16[2,32,256]{2,1,0:T(8,128)(2,1)S(1)}, bf16[2,32,256]{2,1,0:T(8,128)(2,1)S(1)}, bf16[2,32,1280]{2,1,0:T(8,128)(2,1)S(1)}, f32[16,8,384]{2,1,0:T(8,128)S(1)}) custom-call(bf16[256,640]{1,0:T(8,128)(2,1)S(1)} %bitcast.15, f32[2,32,256]{2,1,0:T(8,128)S(1)} %copy-done.9, bf16[2,256,1280]{2,1,0:T(8,128)(2,1)S(1)} %copy-done.3, ...), custom_call_target="tpu_custom_call" | custom-call | flops 125829120 | bytes 2621440 | tf_op jit(solution)/shard_map/pallas_call | solution.py:83
  104.4 12.8 %all_to_all.26.refs_0_ = f32[16,8,384]{2,1,0:T(8,128)S(1)} all-to-all(f32[16,8,384]{2,1,0:T(8,128)S(1)} %get-tuple-element.62), channel_id=1, replica_groups={{0,1,2,3,4,5,6,7,8,9,10,11,12,13,14,15},{16,17,18,19,20,21,22,23,24,25,..., dimensions={0} | all-to-all | bytes 393216 | tf_op jit(solution)/shard_map/all_to_all | solution.py:415
  117.9 3.6 %all-to-all-start.3 = ((bf16[16,8,384]{2,1,0:T(8,128)(2,1)}), bf16[16,8,384]{2,1,0:T(8,128)(2,1)S(1)}, u32[]{:S(2)}, u32[]{:S(2)}) async-start(bf16[16,8,384]{2,1,0:T(8,128)(2,1)} %shard_map.114), calls=%async_computation.3 | async-start | bytes 196608 | tf_op jit(solution)/shard_map/all_to_all | solution.py:415
  122.5 2.5 %collective-permute-start.13 = (bf16[128,1280]{1,0:T(8,128)(2,1)S(1)}, bf16[128,1280]{1,0:T(8,128)(2,1)S(1)}, u32[]{:S(2)}, u32[]{:S(2)}) collective-permute-start(bf16[128,1280]{1,0:T(8,128)(2,1)S(1)} %shard_map.116.refs_0_), channel_id=1, source_target_pairs={{0,3},{1,0},{2,1},{3,2},{4,7},{5,4},{6,5},{7,6},{8,11},{9,8},{10,9... | collective-permute-start | bytes 983048 | tf_op jit(solution)/shard_map/ppermute | solution.py:334
  125.0 1.9 %shard_map.113 = bf16[2,256,1280]{2,1,0:T(8,128)(2,1)} custom-call(bf16[2,32,256]{2,1,0:T(8,128)(2,1)S(1)} %get-tuple-element.59.refs_0_, bf16[2,32,256]{2,1,0:T(8,128)(2,1)S(1)} %get-tuple-element.60.refs_1_, bf16[2,32,1280]{2,1,0:T(8,128)(2,1)S(1)} %get-tuple-element.61.refs_2_, bf16[32,1280]{1,0:T(8,128)(2,1)S(1)} %copy-done.13), custom_call_target="tpu_custom_call" | custom-call | flops 83886080 | bytes 1310720 | tf_op jit(solution)/shard_map/pallas_call | solution.py:83
  126.9 4.6 %all-to-all-done.3.refs_0_ = bf16[16,8,384]{2,1,0:T(8,128)(2,1)S(1)} async-done(((bf16[16,8,384]{2,1,0:T(8,128)(2,1)}), bf16[16,8,384]{2,1,0:T(8,128)(2,1)S(1)}, u32[]{:S(2)}, u32[]{:S(2)}) %all-to-all-start.3) | async-done | bytes 98336 | tf_op jit(solution)/shard_map/all_to_all | solution.py:415
  132.2 4.5 %all-to-all-start.4 = ((f32[16,8,384]{2,1,0:T(8,128)}), f32[16,8,384]{2,1,0:T(8,128)S(1)}, u32[]{:S(2)}, u32[]{:S(2)}) async-start(f32[16,8,384]{2,1,0:T(8,128)} %shard_map.115), calls=%async_computation.4 | async-start | bytes 393216 | tf_op jit(solution)/shard_map/all_to_all | solution.py:415
  136.7 3.2 %collective-permute-done.14.refs_2_ = bf16[128,1280]{1,0:T(8,128)(2,1)S(1)} collective-permute-done((bf16[128,1280]{1,0:T(8,128)(2,1)S(1)}, bf16[128,1280]{1,0:T(8,128)(2,1)S(1)}, u32[]{:S(2)}, u32[]{:S(2)}) %collective-permute-start.14) | collective-permute-done | bytes 327712 | tf_op jit(solution)/shard_map/ppermute | solution.py:334
  139.9 2.4 %shard_map.117 = bf16[1280,640]{1,0:T(8,128)(2,1)} custom-call(bf16[128,1280]{1,0:T(8,128)(2,1)S(1)} %shard_map.116.refs_0_, bf16[128,1280]{1,0:T(8,128)(2,1)S(1)} %collective-permute-done.13.refs_1_, bf16[128,1280]{1,0:T(8,128)(2,1)S(1)} %collective-permute-done.14.refs_2_, bf16[128,1280]{1,0:T(8,128)(2,1)S(1)} %collective-permute-done.15.refs_3_, ...), custom_call_target="tpu_custom_call" | custom-call | flops 838860800 | bytes 3276800 | tf_op jit(solution)/shard_map/pallas_call | solution.py:83
  142.3 1.5 %all-to-all-done.4.refs_0_ = f32[16,8,384]{2,1,0:T(8,128)S(1)} async-done(((f32[16,8,384]{2,1,0:T(8,128)}), f32[16,8,384]{2,1,0:T(8,128)S(1)}, u32[]{:S(2)}, u32[]{:S(2)}) %all-to-all-start.4) | async-done | bytes 196640 | tf_op jit(solution)/shard_map/all_to_all | solution.py:415
  (55 shorter events, 10.6 us)
Async XLA Ops:
  3.8 27.6 %all-to-all-start = ((bf16[32,8,640]{2,1,0:T(8,128)(2,1)}), bf16[32,8,640]{2,1,0:T(8,128)(2,1)}, u32[]{:S(2)}, u32[]{:S(2)}) async-start(bf16[32,8,640]{2,1,0:T(8,128)(2,1)} %bitcast.19), calls=%async_computation | async-start | bytes 655360 | tf_op jit(solution)/shard_map/all_to_all | solution.py:35
  16.6 31.0 %copy-start = (bf16[1,640,1280]{2,1,0:T(8,128)(2,1)S(1)}, bf16[1,640,1280]{2,1,0:T(8,128)(2,1)}, u32[]{:S(2)}) copy-start(bf16[1,640,1280]{2,1,0:T(8,128)(2,1)} %param.13) | copy-start | bytes 4915204
  16.6 31.0 %copy-start.1 = (bf16[1,1280,640]{2,1,0:T(8,128)(2,1)S(1)}, bf16[1,1280,640]{2,1,0:T(8,128)(2,1)}, u32[]{:S(2)}) copy-start(bf16[1,1280,640]{2,1,0:T(8,128)(2,1)} %param.12) | copy-start | bytes 4915204
  21.1 12.5 %collective-permute-start = (bf16[128,1280]{1,0:T(8,128)(2,1)}, bf16[128,1280]{1,0:T(8,128)(2,1)}, u32[]{:S(2)}, u32[]{:S(2)}) collective-permute-start(bf16[128,1280]{1,0:T(8,128)(2,1)} %get-tuple-element.38), channel_id=1, source_target_pairs={{0,1},{1,2},{2,3},{3,0},{4,5},{5,6},{6,7},{7,4},{8,9},{9,10},{10,1... | collective-permute-start | bytes 983048 | tf_op jit(solution)/shard_map/ppermute | solution.py:334
  22.4 11.3 %collective-permute-start.1 = (bf16[128,1280]{1,0:T(8,128)(2,1)}, bf16[128,1280]{1,0:T(8,128)(2,1)}, u32[]{:S(2)}, u32[]{:S(2)}) collective-permute-start(bf16[128,1280]{1,0:T(8,128)(2,1)} %get-tuple-element.39), channel_id=1, source_target_pairs={{0,3},{1,0},{2,1},{3,2},{4,7},{5,4},{6,5},{7,6},{8,11},{9,8},{10,9... | collective-permute-start | bytes 983048 | tf_op jit(solution)/shard_map/ppermute | solution.py:334
  32.6 32.8 %copy-start.11 = (bf16[64,1280]{1,0:T(8,128)(2,1)}, bf16[64,1280]{1,0:T(8,128)(2,1)S(1)}, u32[]{:S(2)}) copy-start(bf16[64,1280]{1,0:T(8,128)(2,1)S(1)} %get-tuple-element.64.refs_0_) | copy-start | bytes 491524
  32.6 5.4 %collective-permute-start.2 = (bf16[64,1280]{1,0:T(8,128)(2,1)S(1)}, bf16[64,1280]{1,0:T(8,128)(2,1)S(1)}, u32[]{:S(2)}, u32[]{:S(2)}) collective-permute-start(bf16[64,1280]{1,0:T(8,128)(2,1)S(1)} %get-tuple-element.43.refs_0_), channel_id=1, source_target_pairs={{0,4},{1,5},{2,6},{3,7},{4,0},{5,1},{6,2},{7,3},{8,12},{9,13},{10,... | collective-permute-start | bytes 491528 | tf_op jit(solution)/shard_map/ppermute | solution.py:337
  38.1 9.5 %collective-permute-start.5 = (bf16[128,1280]{1,0:T(8,128)(2,1)S(1)}, bf16[128,1280]{1,0:T(8,128)(2,1)S(1)}, u32[]{:S(2)}, u32[]{:S(2)}) collective-permute-start(bf16[128,1280]{1,0:T(8,128)(2,1)S(1)} %shard_map.105.refs_1_.refs_0_), channel_id=1, source_target_pairs={{0,2},{1,3},{2,0},{3,1},{4,6},{5,7},{6,4},{7,5},{8,10},{9,11},{10,... | collective-permute-start | bytes 983048 | tf_op jit(solution)/shard_map/ppermute | solution.py:334
  40.9 17.1 %collective-permute-start.4 = (bf16[128,1280]{1,0:T(8,128)(2,1)S(1)}, bf16[128,1280]{1,0:T(8,128)(2,1)S(1)}, u32[]{:S(2)}, u32[]{:S(2)}) collective-permute-start(bf16[128,1280]{1,0:T(8,128)(2,1)S(1)} %shard_map.105.refs_1_.refs_0_), channel_id=1, source_target_pairs={{0,1},{1,2},{2,3},{3,0},{4,5},{5,6},{6,7},{7,4},{8,9},{9,10},{10,1... | collective-permute-start | bytes 983048 | tf_op jit(solution)/shard_map/ppermute | solution.py:334
  41.2 16.8 %collective-permute-start.3 = (bf16[128,1280]{1,0:T(8,128)(2,1)S(1)}, bf16[128,1280]{1,0:T(8,128)(2,1)S(1)}, u32[]{:S(2)}, u32[]{:S(2)}) collective-permute-start(bf16[128,1280]{1,0:T(8,128)(2,1)S(1)} %shard_map.105.refs_1_.refs_0_), channel_id=1, source_target_pairs={{0,3},{1,0},{2,1},{3,2},{4,7},{5,4},{6,5},{7,6},{8,11},{9,8},{10,9... | collective-permute-start | bytes 983048 | tf_op jit(solution)/shard_map/ppermute | solution.py:334
  48.5 9.5 %copy-start.14 = (bf16[128,1280]{1,0:T(8,128)(2,1)S(1)}, bf16[128,1280]{1,0:T(8,128)(2,1)}, u32[]{:S(2)}) copy-start(bf16[128,1280]{1,0:T(8,128)(2,1)} %get-tuple-element.44) | copy-start | bytes 983044
  48.5 9.8 %copy-start.7 = (bf16[384,640]{1,0:T(8,128)(2,1)S(1)}, bf16[384,640]{1,0:T(8,128)(2,1)}, u32[]{:S(2)}) copy-start(bf16[384,640]{1,0:T(8,128)(2,1)} %get-tuple-element.51.refs_3_) | copy-start | bytes 1474564
  49.7 21.9 %collective-permute-start.11 = (bf16[128,1280]{1,0:T(8,128)(2,1)S(1)}, bf16[128,1280]{1,0:T(8,128)(2,1)S(1)}, u32[]{:S(2)}, u32[]{:S(2)}) collective-permute-start(bf16[128,1280]{1,0:T(8,128)(2,1)S(1)} %get-tuple-element.56), channel_id=1, source_target_pairs={{0,2},{1,3},{2,0},{3,1},{4,6},{5,7},{6,4},{7,5},{8,10},{9,11},{10,... | collective-permute-start | bytes 983048 | tf_op jit(solution)/shard_map/ppermute | solution.py:334
  58.0 11.3 %collective-permute-start.6 = (bf16[128,1280]{1,0:T(8,128)(2,1)S(1)}, bf16[128,1280]{1,0:T(8,128)(2,1)S(1)}, u32[]{:S(2)}, u32[]{:S(2)}) collective-permute-start(bf16[128,1280]{1,0:T(8,128)(2,1)S(1)} %copy-done.14), channel_id=1, source_target_pairs={{0,2},{1,3},{2,0},{3,1},{4,6},{5,7},{6,4},{7,5},{8,10},{9,11},{10,... | collective-permute-start | bytes 983048 | tf_op jit(solution)/shard_map/ppermute | solution.py:334
  58.3 11.0 %copy-start.8 = (bf16[128,1280]{1,0:T(8,128)(2,1)S(1)}, bf16[128,1280]{1,0:T(8,128)(2,1)}, u32[]{:S(2)}) copy-start(bf16[128,1280]{1,0:T(8,128)(2,1)} %get-tuple-element.37.refs_0_) | copy-start | bytes 983044
  62.1 16.8 %copy-start.4 = (bf16[512,640]{1,0:T(8,128)(2,1)S(1)}, bf16[512,640]{1,0:T(8,128)(2,1)}, u32[]{:S(2)}) copy-start(bf16[512,640]{1,0:T(8,128)(2,1)} %get-tuple-element.48.refs_0_) | copy-start | bytes 1966084
  62.1 15.3 %collective-permute-start.9 = (bf16[128,1280]{1,0:T(8,128)(2,1)S(1)}, bf16[128,1280]{1,0:T(8,128)(2,1)S(1)}, u32[]{:S(2)}, u32[]{:S(2)}) collective-permute-start(bf16[128,1280]{1,0:T(8,128)(2,1)S(1)} %get-tuple-element.53), channel_id=1, source_target_pairs={{0,1},{1,2},{2,3},{3,0},{4,5},{5,6},{6,7},{7,4},{8,9},{9,10},{10,1... | collective-permute-start | bytes 983048 | tf_op jit(solution)/shard_map/ppermute | solution.py:334
  64.8 12.6 %collective-permute-start.10 = (bf16[128,1280]{1,0:T(8,128)(2,1)S(1)}, bf16[128,1280]{1,0:T(8,128)(2,1)S(1)}, u32[]{:S(2)}, u32[]{:S(2)}) collective-permute-start(bf16[128,1280]{1,0:T(8,128)(2,1)S(1)} %get-tuple-element.54), channel_id=1, source_target_pairs={{0,3},{1,0},{2,1},{3,2},{4,7},{5,4},{6,5},{7,6},{8,11},{9,8},{10,9... | collective-permute-start | bytes 983048 | tf_op jit(solution)/shard_map/ppermute | solution.py:334
  65.4 15.7 %collective-permute-start.7 = (bf16[64,1280]{1,0:T(8,128)(2,1)S(1)}, bf16[64,1280]{1,0:T(8,128)(2,1)S(1)}, u32[]{:S(2)}, u32[]{:S(2)}) collective-permute-start(bf16[64,1280]{1,0:T(8,128)(2,1)S(1)} %get-tuple-element.64.refs_0_), channel_id=1, source_target_pairs={{0,4},{1,5},{2,6},{3,7},{4,0},{5,1},{6,2},{7,3},{8,12},{9,13},{10,... | collective-permute-start | bytes 491528 | tf_op jit(solution)/shard_map/ppermute | solution.py:337
  70.6 10.5 %collective-permute-start.8 = (bf16[64,1280]{1,0:T(8,128)(2,1)S(1)}, bf16[64,1280]{1,0:T(8,128)(2,1)S(1)}, u32[]{:S(2)}, u32[]{:S(2)}) collective-permute-start(bf16[64,1280]{1,0:T(8,128)(2,1)S(1)} %get-tuple-element.50), channel_id=1, source_target_pairs={{0,4},{1,5},{2,6},{3,7},{4,0},{5,1},{6,2},{7,3},{8,12},{9,13},{10,... | collective-permute-start | bytes 491528 | tf_op jit(solution)/shard_map/ppermute | solution.py:337
  77.6 5.2 %collective-permute-start.12 = (bf16[64,1280]{1,0:T(8,128)(2,1)S(1)}, bf16[64,1280]{1,0:T(8,128)(2,1)S(1)}, u32[]{:S(2)}, u32[]{:S(2)}) collective-permute-start(bf16[64,1280]{1,0:T(8,128)(2,1)S(1)} %get-tuple-element.58), channel_id=1, source_target_pairs={{0,4},{1,5},{2,6},{3,7},{4,0},{5,1},{6,2},{7,3},{8,12},{9,13},{10,... | collective-permute-start | bytes 491528 | tf_op jit(solution)/shard_map/ppermute | solution.py:337
  78.8 23.8 %copy-start.3 = (bf16[2,256,1280]{2,1,0:T(8,128)(2,1)S(1)}, bf16[2,256,1280]{2,1,0:T(8,128)(2,1)}, u32[]{:S(2)}) copy-start(bf16[2,256,1280]{2,1,0:T(8,128)(2,1)} %refs_2_.3) | copy-start | bytes 3932164
  81.1 21.6 %copy-start.2 = (bf16[2,256,1280]{2,1,0:T(8,128)(2,1)S(1)}, bf16[2,256,1280]{2,1,0:T(8,128)(2,1)}, u32[]{:S(2)}) copy-start(bf16[2,256,1280]{2,1,0:T(8,128)(2,1)} %refs_3_.2) | copy-start | bytes 3932164
  81.1 21.6 %copy-start.9 = (f32[2,32,256]{2,1,0:T(8,128)S(1)}, f32[2,32,256]{2,1,0:T(8,128)}, u32[]{:S(2)}) copy-start(f32[2,32,256]{2,1,0:T(8,128)} %refs_1_.3) | copy-start | bytes 196612
  102.7 18.9 %copy-start.12 = (bf16[64,1280]{1,0:T(8,128)(2,1)S(1)}, bf16[64,1280]{1,0:T(8,128)(2,1)}, u32[]{:S(2)}) copy-start(bf16[64,1280]{1,0:T(8,128)(2,1)} %copy-done.11) | copy-start | bytes 491524
  102.7 22.3 %copy-start.13 = (bf16[32,1280]{1,0:T(8,128)(2,1)S(1)}, bf16[32,1280]{1,0:T(8,128)(2,1)}, u32[]{:S(2)}) copy-start(bf16[32,1280]{1,0:T(8,128)(2,1)} %refs_3_.3) | copy-start | bytes 245764
  117.9 21.9 %copy-start.6 = (bf16[384,640]{1,0:T(8,128)(2,1)S(1)}, bf16[384,640]{1,0:T(8,128)(2,1)}, u32[]{:S(2)}) copy-start(bf16[384,640]{1,0:T(8,128)(2,1)} %copy-done.5) | copy-start | bytes 1474564
  117.9 13.5 %all-to-all-start.3 = ((bf16[16,8,384]{2,1,0:T(8,128)(2,1)}), bf16[16,8,384]{2,1,0:T(8,128)(2,1)S(1)}, u32[]{:S(2)}, u32[]{:S(2)}) async-start(bf16[16,8,384]{2,1,0:T(8,128)(2,1)} %shard_map.114), calls=%async_computation.3 | async-start | bytes 196608 | tf_op jit(solution)/shard_map/all_to_all | solution.py:415
  121.6 15.1 %collective-permute-start.15 = (bf16[128,1280]{1,0:T(8,128)(2,1)S(1)}, bf16[128,1280]{1,0:T(8,128)(2,1)S(1)}, u32[]{:S(2)}, u32[]{:S(2)}) collective-permute-start(bf16[128,1280]{1,0:T(8,128)(2,1)S(1)} %shard_map.116.refs_0_), channel_id=1, source_target_pairs={{0,2},{1,3},{2,0},{3,1},{4,6},{5,7},{6,4},{7,5},{8,10},{9,11},{10,... | collective-permute-start | bytes 983048 | tf_op jit(solution)/shard_map/ppermute | solution.py:334
  122.3 17.6 %collective-permute-start.14 = (bf16[128,1280]{1,0:T(8,128)(2,1)S(1)}, bf16[128,1280]{1,0:T(8,128)(2,1)S(1)}, u32[]{:S(2)}, u32[]{:S(2)}) collective-permute-start(bf16[128,1280]{1,0:T(8,128)(2,1)S(1)} %shard_map.116.refs_0_), channel_id=1, source_target_pairs={{0,1},{1,2},{2,3},{3,0},{4,5},{5,6},{6,7},{7,4},{8,9},{9,10},{10,1... | collective-permute-start | bytes 983048 | tf_op jit(solution)/shard_map/ppermute | solution.py:334
  122.5 17.4 %collective-permute-start.13 = (bf16[128,1280]{1,0:T(8,128)(2,1)S(1)}, bf16[128,1280]{1,0:T(8,128)(2,1)S(1)}, u32[]{:S(2)}, u32[]{:S(2)}) collective-permute-start(bf16[128,1280]{1,0:T(8,128)(2,1)S(1)} %shard_map.116.refs_0_), channel_id=1, source_target_pairs={{0,3},{1,0},{2,1},{3,2},{4,7},{5,4},{6,5},{7,6},{8,11},{9,8},{10,9... | collective-permute-start | bytes 983048 | tf_op jit(solution)/shard_map/ppermute | solution.py:334
  132.2 11.6 %all-to-all-start.4 = ((f32[16,8,384]{2,1,0:T(8,128)}), f32[16,8,384]{2,1,0:T(8,128)S(1)}, u32[]{:S(2)}, u32[]{:S(2)}) async-start(f32[16,8,384]{2,1,0:T(8,128)} %shard_map.115), calls=%async_computation.4 | async-start | bytes 393216 | tf_op jit(solution)/shard_map/all_to_all | solution.py:415
  (2 other events, 1.7 us)

commit v7 on v6

--- a/solution.py
+++ b/solution.py
@@ -360,7 +360,6 @@
     out_ring = [out_part[0]] + [along(out_part[c], ORDER[c]) for c in range(1, RING - 1)]
     mine = joined(after(own_grad, *out_ring), across(own_grad))
     grads = [mine] + [along(mine, -steps) for steps in ORDER[1:]]
-    out_ring.append(along(after(out_part[RING - 1], *grads), ORDER[RING - 1]))
 
     hid, back_ring = [], []
     for first, last, slope in ((0, RING - 1, slope_a), (RING - 1, RING, slope_b)):
@@ -374,6 +373,7 @@
         hid.append(hid_rows)
         back_ring += [along(part[c - first], ORDER[c]) if c else part[c] for c in range(first, last)]
 
+    out_ring.append(along(after(out_part[RING - 1], hid[1]), ORDER[RING - 1]))
     near_out, far_out = plane_sum(out_ring)
     near_back, far_back = plane_sum(back_ring)
     other_in = across(after(moved_in, *grads))

time: 145 us -> 145 us (level)
  no operation moved by 1% of the time
where the time goes in v7:
time: 145 us; the launch traced here: 144 us
  waiting for transfers between devices  42.2 us (29%)
  starting transfers between devices  42.1 us (29%)
  blocking collectives  32.4 us (22%)
  Pallas kernels  25.2 us (17%)
  local copies, waits for them, and re-layouts  1.75 us (1%)
    pallas_call x17, Pallas kernels, run(): pl.pallas_call(body, out_shape=tuple((o[1] for o in outputs)), in_specs=[...  25.2 us
    ppermute x12, waiting for transfers between devices, along(): lax.ppermute(value, 'expert', [(i, i // RING * RING + (i + steps) % RING)...  22.5 us
    all_to_all x1, blocking collectives, exchange(): return lax.all_to_all(blocks, axis, split_axis=0, concat_axis=0, tiled=True)  19.6 us
    ppermute x12, starting transfers between devices, along(): lax.ppermute(value, 'expert', [(i, i // RING * RING + (i + steps) % RING)...  17.3 us
    all_to_all x1, blocking collectives, swap_rows(): lax.all_to_all(value, axes, split_axis=0, concat_axis=0, axis_index_group...  12.8 us
    all_to_all x1, starting transfers between devices, exchange(): return lax.all_to_all(blocks, axis, split_axis=0, concat_axis=0, tiled=True)  12.8 us
    all_to_all x2, starting transfers between devices, swap_rows(): lax.all_to_all(value, axes, split_axis=0, concat_axis=0, axis_index_group...  8.14 us
    all_to_all x1, waiting for transfers between devices, exchange(): return lax.all_to_all(blocks, axis, split_axis=0, concat_axis=0, tiled=True)  7.58 us
  transfers between devices with their start and end apart: 19, of which 10 were waited for; matrix products, arithmetic and copies ran while one was open for 0% of the time, Pallas kernels for 13%

profile of v7, /device:TPU:1, one launch (start us, length us, event | category | flops | bytes accessed | tf_op | source)
XLA Modules:
  0.0 144.5 jit_solution(5497228309175906205)
XLA Ops:
  0.6 3.1 %shard_map.102 = bf16[256,640]{1,0:T(8,128)(2,1)} custom-call(f32[2,32,256]{2,1,0:T(8,128)} %refs_1_.3, bf16[2,256,1280]{2,1,0:T(8,128)(2,1)} %refs_3_.2, bf16[2,256,1280]{2,1,0:T(8,128)(2,1)} %refs_2_.3), custom_call_target="tpu_custom_call" | custom-call | flops 83886080 | bytes 2621440 | tf_op jit(solution)/shard_map/pallas_call | solution.py:83
  3.8 12.8 %all-to-all-start = ((bf16[32,8,640]{2,1,0:T(8,128)(2,1)}), bf16[32,8,640]{2,1,0:T(8,128)(2,1)}, u32[]{:S(2)}, u32[]{:S(2)}) async-start(bf16[32,8,640]{2,1,0:T(8,128)(2,1)} %bitcast.19), calls=%async_computation | async-start | bytes 655360 | tf_op jit(solution)/shard_map/all_to_all | solution.py:35
  16.6 4.5 %shard_map.103 = (bf16[512,640]{1,0:T(8,128)(2,1)}, bf16[384,640]{1,0:T(8,128)(2,1)}, bf16[128,640]{1,0:T(8,128)(2,1)}, bf16[128,1280]{1,0:T(8,128)(2,1)}, bf16[...) custom-call(s32[1]{0:T(128)} %bitcast.refs_0_, bf16[512,640]{1,0:T(8,128)(2,1)} %bitcast.20, ...), custom_call_target="tpu_custom_call" | custom-call | flops 1677721600 | bytes 3276800 | tf_op jit(solution)/shard_map/pallas_call | solution.py:83
  21.1 1.2 collective-permute-start
  22.4 1.5 %collective-permute-start.1 = (bf16[128,1280]{1,0:T(8,128)(2,1)}, bf16[128,1280]{1,0:T(8,128)(2,1)}, u32[]{:S(2)}, u32[]{:S(2)}) collective-permute-start(bf16[128,1280]{1,0:T(8,128)(2,1)} %get-tuple-element.39), channel_id=1, source_target_pairs={{0,3},{1,0},{2,1},{3,2},{4,7},{5,4},{6,5},{7,6},{8,11},{9,8},{10,9... | collective-permute-start | bytes 983048 | tf_op jit(solution)/shard_map/ppermute | solution.py:334
  23.8 7.6 %all-to-all-done = bf16[32,8,640]{2,1,0:T(8,128)(2,1)} async-done(((bf16[32,8,640]{2,1,0:T(8,128)(2,1)}), bf16[32,8,640]{2,1,0:T(8,128)(2,1)}, u32[]{:S(2)}, u32[]{:S(2)}) %all-to-all-start) | async-done | bytes 327712 | tf_op jit(solution)/shard_map/all_to_all | solution.py:35
  31.4 1.2 shard_map.104
  33.7 4.3 %collective-permute-done.2.refs_1_ = bf16[64,1280]{1,0:T(8,128)(2,1)S(1)} collective-permute-done((bf16[64,1280]{1,0:T(8,128)(2,1)S(1)}, bf16[64,1280]{1,0:T(8,128)(2,1)S(1)}, u32[]{:S(2)}, u32[]{:S(2)}) %collective-permute-start.2) | collective-permute-done | bytes 163872 | tf_op jit(solution)/shard_map/ppermute | solution.py:337
  38.1 2.9 %collective-permute-start.3 = (bf16[128,1280]{1,0:T(8,128)(2,1)S(1)}, bf16[128,1280]{1,0:T(8,128)(2,1)S(1)}, u32[]{:S(2)}, u32[]{:S(2)}) collective-permute-start(bf16[128,1280]{1,0:T(8,128)(2,1)S(1)} %shard_map.105.refs_1_.refs_0_), channel_id=1, source_target_pairs={{0,2},{1,3},{2,0},{3,1},{4,6},{5,7},{6,4},{7,5},{8,10},{9,11},{10,... | collective-permute-start | bytes 983048 | tf_op jit(solution)/shard_map/ppermute | solution.py:334
  41.2 2.4 %collective-permute-start.5 = (bf16[128,1280]{1,0:T(8,128)(2,1)S(1)}, bf16[128,1280]{1,0:T(8,128)(2,1)S(1)}, u32[]{:S(2)}, u32[]{:S(2)}) collective-permute-start(bf16[128,1280]{1,0:T(8,128)(2,1)S(1)} %shard_map.105.refs_1_.refs_0_), channel_id=1, source_target_pairs={{0,3},{1,0},{2,1},{3,2},{4,7},{5,4},{6,5},{7,6},{8,11},{9,8},{10,9... | collective-permute-start | bytes 983048 | tf_op jit(solution)/shard_map/ppermute | solution.py:334
  43.6 4.0 %collective-permute-done.3.refs_0_.refs_4_ = bf16[128,1280]{1,0:T(8,128)(2,1)S(1)} collective-permute-done((bf16[128,1280]{1,0:T(8,128)(2,1)S(1)}, bf16[128,1280]{1,0:T(8,128)(2,1)S(1)}, u32[]{:S(2)}, u32[]{:S(2)}) %collective-permute-start.3) | collective-permute-done | bytes 327712 | tf_op jit(solution)/shard_map/ppermute | solution.py:334
  49.7 2.9 %collective-permute-start.4 = (bf16[128,1280]{1,0:T(8,128)(2,1)S(1)}, bf16[128,1280]{1,0:T(8,128)(2,1)S(1)}, u32[]{:S(2)}, u32[]{:S(2)}) collective-permute-start(bf16[128,1280]{1,0:T(8,128)(2,1)S(1)} %copy-done.14), channel_id=1, source_target_pairs={{0,2},{1,3},{2,0},{3,1},{4,6},{5,7},{6,4},{7,5},{8,10},{9,11},{10,... | collective-permute-start | bytes 983048 | tf_op jit(solution)/shard_map/ppermute | solution.py:334
  52.8 5.2 %collective-permute-done.6.refs_3_.refs_2_ = bf16[128,1280]{1,0:T(8,128)(2,1)S(1)} collective-permute-done((bf16[128,1280]{1,0:T(8,128)(2,1)S(1)}, bf16[128,1280]{1,0:T(8,128)(2,1)S(1)}, u32[]{:S(2)}, u32[]{:S(2)}) %collective-permute-start.6) | collective-permute-done | bytes 327712 | tf_op jit(solution)/shard_map/ppermute | solution.py:334
  58.0 3.0 %shard_map.109 = (bf16[384,640]{1,0:T(8,128)(2,1)S(1)}, bf16[128,1280]{1,0:T(8,128)(2,1)S(1)}, bf16[128,1280]{1,0:T(8,128)(2,1)S(1)}, bf16[128,1280]{1,0:T(8,128)(2,1)S(1)}) custom-call(bf16[128,1280]{1,0:T(8,128)(2,1)S(1)} %shard_map.105.refs_1_.refs_0_, bf16[128,1280]{1,0:T(8,128)(2,1)S(1)} %collective-permute-done.5.refs_2_.refs_1_, ...), custom_call_target="tpu_custom_call" | custom-call | flops 1258291200 | bytes 1638400 | tf_op jit(solution)/shard_map/pallas_call | solution.py:83
  61.8 1.2 collective-permute-start.9
  63.0 1.5 %collective-permute-start.10 = (bf16[128,1280]{1,0:T(8,128)(2,1)S(1)}, bf16[128,1280]{1,0:T(8,128)(2,1)S(1)}, u32[]{:S(2)}, u32[]{:S(2)}) collective-permute-start(bf16[128,1280]{1,0:T(8,128)(2,1)S(1)} %get-tuple-element.56), channel_id=1, source_target_pairs={{0,3},{1,0},{2,1},{3,2},{4,7},{5,4},{6,5},{7,6},{8,11},{9,8},{10,9... | collective-permute-start | bytes 983048 | tf_op jit(solution)/shard_map/ppermute | solution.py:334
  65.4 1.2 shard_map.107
  68.3 9.1 %collective-permute-done.9.refs_1_ = bf16[128,1280]{1,0:T(8,128)(2,1)S(1)} collective-permute-done((bf16[128,1280]{1,0:T(8,128)(2,1)S(1)}, bf16[128,1280]{1,0:T(8,128)(2,1)S(1)}, u32[]{:S(2)}, u32[]{:S(2)}) %collective-permute-start.9) | collective-permute-done | bytes 327712 | tf_op jit(solution)/shard_map/ppermute | solution.py:334
  77.6 1.3 collective-permute-start.12
  78.8 2.2 %shard_map.108 = bf16[640,1280]{1,0:T(8,128)(2,1)} custom-call(bf16[512,640]{1,0:T(8,128)(2,1)S(1)} %copy-done.4, bf16[128,1280]{1,0:T(8,128)(2,1)S(1)} %shard_map.105.refs_1_.refs_0_, bf16[128,1280]{1,0:T(8,128)(2,1)S(1)} %collective-permute-done.5.refs_2_.refs_1_, bf16[128,1280]{1,0:T(8,128)(2,1)S(1)} %collective-permute-done.6.refs_3_.refs_2_, ...), custom_call_target="tpu_custom_call" | custom-call | flops 838860800 | bytes 3276800 | tf_op jit(solution)/shard_map/pallas_call | solution.py:83
  81.1 1.7 %collective-permute-done.12.refs_3_ = bf16[64,1280]{1,0:T(8,128)(2,1)S(1)} collective-permute-done((bf16[64,1280]{1,0:T(8,128)(2,1)S(1)}, bf16[64,1280]{1,0:T(8,128)(2,1)S(1)}, u32[]{:S(2)}, u32[]{:S(2)}) %collective-permute-start.12) | collective-permute-done | bytes 163872 | tf_op jit(solution)/shard_map/ppermute | solution.py:337
  83.1 19.6 %all_to_all.25 = bf16[32,8,640]{2,1,0:T(8,128)(2,1)S(1)} all-to-all(bf16[32,8,640]{2,1,0:T(8,128)(2,1)S(1)} %bitcast.16), channel_id=1, replica_groups=mesh['dp'=32,'expert'=8] {'dp'}, dimensions={0} | all-to-all | bytes 655360 | tf_op jit(solution)/shard_map/all_to_all | solution.py:35
  102.7 1.7 %shard_map.112 = (bf16[2,32,256]{2,1,0:T(8,128)(2,1)S(1)}, bf16[2,32,256]{2,1,0:T(8,128)(2,1)S(1)}, bf16[2,32,1280]{2,1,0:T(8,128)(2,1)S(1)}, f32[16,8,384]{2,1,0:T(8,128)S(1)}) custom-call(bf16[256,640]{1,0:T(8,128)(2,1)S(1)} %bitcast.15, f32[2,32,256]{2,1,0:T(8,128)S(1)} %copy-done.9, bf16[2,256,1280]{2,1,0:T(8,128)(2,1)S(1)} %copy-done.3, ...), custom_call_target="tpu_custom_call" | custom-call | flops 125829120 | bytes 2621440 | tf_op jit(solution)/shard_map/pallas_call | solution.py:83
  104.4 12.8 %all_to_all.26.refs_0_ = f32[16,8,384]{2,1,0:T(8,128)S(1)} all-to-all(f32[16,8,384]{2,1,0:T(8,128)S(1)} %get-tuple-element.63), channel_id=1, replica_groups={{0,1,2,3,4,5,6,7,8,9,10,11,12,13,14,15},{16,17,18,19,20,21,22,23,24,25,..., dimensions={0} | all-to-all | bytes 393216 | tf_op jit(solution)/shard_map/all_to_all | solution.py:415
  117.9 3.6 %all-to-all-start.3 = ((bf16[16,8,384]{2,1,0:T(8,128)(2,1)}), bf16[16,8,384]{2,1,0:T(8,128)(2,1)S(1)}, u32[]{:S(2)}, u32[]{:S(2)}) async-start(bf16[16,8,384]{2,1,0:T(8,128)(2,1)} %shard_map.114), calls=%async_computation.3 | async-start | bytes 196608 | tf_op jit(solution)/shard_map/all_to_all | solution.py:415
  122.5 2.5 %collective-permute-start.13 = (bf16[128,1280]{1,0:T(8,128)(2,1)S(1)}, bf16[128,1280]{1,0:T(8,128)(2,1)S(1)}, u32[]{:S(2)}, u32[]{:S(2)}) collective-permute-start(bf16[128,1280]{1,0:T(8,128)(2,1)S(1)} %shard_map.116.refs_0_), channel_id=1, source_target_pairs={{0,3},{1,0},{2,1},{3,2},{4,7},{5,4},{6,5},{7,6},{8,11},{9,8},{10,9... | collective-permute-start | bytes 983048 | tf_op jit(solution)/shard_map/ppermute | solution.py:334
  125.0 1.9 %shard_map.113 = bf16[2,256,1280]{2,1,0:T(8,128)(2,1)} custom-call(bf16[2,32,256]{2,1,0:T(8,128)(2,1)S(1)} %get-tuple-element.60.refs_0_, bf16[2,32,256]{2,1,0:T(8,128)(2,1)S(1)} %get-tuple-element.61.refs_1_, bf16[2,32,1280]{2,1,0:T(8,128)(2,1)S(1)} %get-tuple-element.62.refs_2_, bf16[32,1280]{1,0:T(8,128)(2,1)S(1)} %copy-done.13), custom_call_target="tpu_custom_call" | custom-call | flops 83886080 | bytes 1310720 | tf_op jit(solution)/shard_map/pallas_call | solution.py:83
  126.9 4.6 %all-to-all-done.3.refs_0_ = bf16[16,8,384]{2,1,0:T(8,128)(2,1)S(1)} async-done(((bf16[16,8,384]{2,1,0:T(8,128)(2,1)}), bf16[16,8,384]{2,1,0:T(8,128)(2,1)S(1)}, u32[]{:S(2)}, u32[]{:S(2)}) %all-to-all-start.3) | async-done | bytes 98336 | tf_op jit(solution)/shard_map/all_to_all | solution.py:415
  132.2 4.5 %all-to-all-start.4 = ((f32[16,8,384]{2,1,0:T(8,128)}), f32[16,8,384]{2,1,0:T(8,128)S(1)}, u32[]{:S(2)}, u32[]{:S(2)}) async-start(f32[16,8,384]{2,1,0:T(8,128)} %shard_map.115), calls=%async_computation.4 | async-start | bytes 393216 | tf_op jit(solution)/shard_map/all_to_all | solution.py:415
  136.7 3.2 %collective-permute-done.14.refs_2_ = bf16[128,1280]{1,0:T(8,128)(2,1)S(1)} collective-permute-done((bf16[128,1280]{1,0:T(8,128)(2,1)S(1)}, bf16[128,1280]{1,0:T(8,128)(2,1)S(1)}, u32[]{:S(2)}, u32[]{:S(2)}) %collective-permute-start.14) | collective-permute-done | bytes 327712 | tf_op jit(solution)/shard_map/ppermute | solution.py:334
  139.9 2.4 %shard_map.117 = bf16[1280,640]{1,0:T(8,128)(2,1)} custom-call(bf16[128,1280]{1,0:T(8,128)(2,1)S(1)} %shard_map.116.refs_0_, bf16[128,1280]{1,0:T(8,128)(2,1)S(1)} %collective-permute-done.13.refs_1_, bf16[128,1280]{1,0:T(8,128)(2,1)S(1)} %collective-permute-done.14.refs_2_, bf16[128,1280]{1,0:T(8,128)(2,1)S(1)} %collective-permute-done.15.refs_3_, ...), custom_call_target="tpu_custom_call" | custom-call | flops 838860800 | bytes 3276800 | tf_op jit(solution)/shard_map/pallas_call | solution.py:83
  142.3 1.5 %all-to-all-done.4.refs_0_ = f32[16,8,384]{2,1,0:T(8,128)S(1)} async-done(((f32[16,8,384]{2,1,0:T(8,128)}), f32[16,8,384]{2,1,0:T(8,128)S(1)}, u32[]{:S(2)}, u32[]{:S(2)}) %all-to-all-start.4) | async-done | bytes 196640 | tf_op jit(solution)/shard_map/all_to_all | solution.py:415
  (55 shorter events, 10.5 us)
Async XLA Ops:
  3.8 27.6 %all-to-all-start = ((bf16[32,8,640]{2,1,0:T(8,128)(2,1)}), bf16[32,8,640]{2,1,0:T(8,128)(2,1)}, u32[]{:S(2)}, u32[]{:S(2)}) async-start(bf16[32,8,640]{2,1,0:T(8,128)(2,1)} %bitcast.19), calls=%async_computation | async-start | bytes 655360 | tf_op jit(solution)/shard_map/all_to_all | solution.py:35
  16.6 31.0 %copy-start = (bf16[1,640,1280]{2,1,0:T(8,128)(2,1)S(1)}, bf16[1,640,1280]{2,1,0:T(8,128)(2,1)}, u32[]{:S(2)}) copy-start(bf16[1,640,1280]{2,1,0:T(8,128)(2,1)} %param.13) | copy-start | bytes 4915204
  16.6 31.0 %copy-start.1 = (bf16[1,1280,640]{2,1,0:T(8,128)(2,1)S(1)}, bf16[1,1280,640]{2,1,0:T(8,128)(2,1)}, u32[]{:S(2)}) copy-start(bf16[1,1280,640]{2,1,0:T(8,128)(2,1)} %param.12) | copy-start | bytes 4915204
  21.1 12.5 %collective-permute-start = (bf16[128,1280]{1,0:T(8,128)(2,1)}, bf16[128,1280]{1,0:T(8,128)(2,1)}, u32[]{:S(2)}, u32[]{:S(2)}) collective-permute-start(bf16[128,1280]{1,0:T(8,128)(2,1)} %get-tuple-element.38), channel_id=1, source_target_pairs={{0,1},{1,2},{2,3},{3,0},{4,5},{5,6},{6,7},{7,4},{8,9},{9,10},{10,1... | collective-permute-start | bytes 983048 | tf_op jit(solution)/shard_map/ppermute | solution.py:334
  22.4 11.3 %collective-permute-start.1 = (bf16[128,1280]{1,0:T(8,128)(2,1)}, bf16[128,1280]{1,0:T(8,128)(2,1)}, u32[]{:S(2)}, u32[]{:S(2)}) collective-permute-start(bf16[128,1280]{1,0:T(8,128)(2,1)} %get-tuple-element.39), channel_id=1, source_target_pairs={{0,3},{1,0},{2,1},{3,2},{4,7},{5,4},{6,5},{7,6},{8,11},{9,8},{10,9... | collective-permute-start | bytes 983048 | tf_op jit(solution)/shard_map/ppermute | solution.py:334
  32.6 31.8 %copy-start.11 = (bf16[64,1280]{1,0:T(8,128)(2,1)}, bf16[64,1280]{1,0:T(8,128)(2,1)S(1)}, u32[]{:S(2)}) copy-start(bf16[64,1280]{1,0:T(8,128)(2,1)S(1)} %get-tuple-element.65.refs_0_) | copy-start | bytes 491524
  32.6 5.4 %collective-permute-start.2 = (bf16[64,1280]{1,0:T(8,128)(2,1)S(1)}, bf16[64,1280]{1,0:T(8,128)(2,1)S(1)}, u32[]{:S(2)}, u32[]{:S(2)}) collective-permute-start(bf16[64,1280]{1,0:T(8,128)(2,1)S(1)} %get-tuple-element.43.refs_0_), channel_id=1, source_target_pairs={{0,4},{1,5},{2,6},{3,7},{4,0},{5,1},{6,2},{7,3},{8,12},{9,13},{10,... | collective-permute-start | bytes 491528 | tf_op jit(solution)/shard_map/ppermute | solution.py:337
  38.1 9.5 %collective-permute-start.3 = (bf16[128,1280]{1,0:T(8,128)(2,1)S(1)}, bf16[128,1280]{1,0:T(8,128)(2,1)S(1)}, u32[]{:S(2)}, u32[]{:S(2)}) collective-permute-start(bf16[128,1280]{1,0:T(8,128)(2,1)S(1)} %shard_map.105.refs_1_.refs_0_), channel_id=1, source_target_pairs={{0,2},{1,3},{2,0},{3,1},{4,6},{5,7},{6,4},{7,5},{8,10},{9,11},{10,... | collective-permute-start | bytes 983048 | tf_op jit(solution)/shard_map/ppermute | solution.py:334
  40.9 17.1 %collective-permute-start.6 = (bf16[128,1280]{1,0:T(8,128)(2,1)S(1)}, bf16[128,1280]{1,0:T(8,128)(2,1)S(1)}, u32[]{:S(2)}, u32[]{:S(2)}) collective-permute-start(bf16[128,1280]{1,0:T(8,128)(2,1)S(1)} %shard_map.105.refs_1_.refs_0_), channel_id=1, source_target_pairs={{0,1},{1,2},{2,3},{3,0},{4,5},{5,6},{6,7},{7,4},{8,9},{9,10},{10,1... | collective-permute-start | bytes 983048 | tf_op jit(solution)/shard_map/ppermute | solution.py:334
  41.2 16.8 %collective-permute-start.5 = (bf16[128,1280]{1,0:T(8,128)(2,1)S(1)}, bf16[128,1280]{1,0:T(8,128)(2,1)S(1)}, u32[]{:S(2)}, u32[]{:S(2)}) collective-permute-start(bf16[128,1280]{1,0:T(8,128)(2,1)S(1)} %shard_map.105.refs_1_.refs_0_), channel_id=1, source_target_pairs={{0,3},{1,0},{2,1},{3,2},{4,7},{5,4},{6,5},{7,6},{8,11},{9,8},{10,9... | collective-permute-start | bytes 983048 | tf_op jit(solution)/shard_map/ppermute | solution.py:334
  48.5 1.2 copy-start.14
  48.5 9.5 %copy-start.7 = (bf16[384,640]{1,0:T(8,128)(2,1)S(1)}, bf16[384,640]{1,0:T(8,128)(2,1)}, u32[]{:S(2)}) copy-start(bf16[384,640]{1,0:T(8,128)(2,1)} %get-tuple-element.53.refs_3_) | copy-start | bytes 1474564
  49.7 15.7 %collective-permute-start.4 = (bf16[128,1280]{1,0:T(8,128)(2,1)S(1)}, bf16[128,1280]{1,0:T(8,128)(2,1)S(1)}, u32[]{:S(2)}, u32[]{:S(2)}) collective-permute-start(bf16[128,1280]{1,0:T(8,128)(2,1)S(1)} %copy-done.14), channel_id=1, source_target_pairs={{0,2},{1,3},{2,0},{3,1},{4,6},{5,7},{6,4},{7,5},{8,10},{9,11},{10,... | collective-permute-start | bytes 983048 | tf_op jit(solution)/shard_map/ppermute | solution.py:334
  52.6 15.7 %collective-permute-start.11 = (bf16[128,1280]{1,0:T(8,128)(2,1)S(1)}, bf16[128,1280]{1,0:T(8,128)(2,1)S(1)}, u32[]{:S(2)}, u32[]{:S(2)}) collective-permute-start(bf16[128,1280]{1,0:T(8,128)(2,1)S(1)} %get-tuple-element.57), channel_id=1, source_target_pairs={{0,2},{1,3},{2,0},{3,1},{4,6},{5,7},{6,4},{7,5},{8,10},{9,11},{10,... | collective-permute-start | bytes 983048 | tf_op jit(solution)/shard_map/ppermute | solution.py:334
  58.0 7.4 %copy-start.8 = (bf16[128,1280]{1,0:T(8,128)(2,1)S(1)}, bf16[128,1280]{1,0:T(8,128)(2,1)}, u32[]{:S(2)}) copy-start(bf16[128,1280]{1,0:T(8,128)(2,1)} %get-tuple-element.37.refs_0_) | copy-start | bytes 983044
  61.8 17.0 %copy-start.4 = (bf16[512,640]{1,0:T(8,128)(2,1)S(1)}, bf16[512,640]{1,0:T(8,128)(2,1)}, u32[]{:S(2)}) copy-start(bf16[512,640]{1,0:T(8,128)(2,1)} %get-tuple-element.50.refs_0_) | copy-start | bytes 1966084
  61.8 15.6 %collective-permute-start.9 = (bf16[128,1280]{1,0:T(8,128)(2,1)S(1)}, bf16[128,1280]{1,0:T(8,128)(2,1)S(1)}, u32[]{:S(2)}, u32[]{:S(2)}) collective-permute-start(bf16[128,1280]{1,0:T(8,128)(2,1)S(1)} %get-tuple-element.55), channel_id=1, source_target_pairs={{0,1},{1,2},{2,3},{3,0},{4,5},{5,6},{6,7},{7,4},{8,9},{9,10},{10,1... | collective-permute-start | bytes 983048 | tf_op jit(solution)/shard_map/ppermute | solution.py:334
  63.0 14.4 %collective-permute-start.10 = (bf16[128,1280]{1,0:T(8,128)(2,1)S(1)}, bf16[128,1280]{1,0:T(8,128)(2,1)S(1)}, u32[]{:S(2)}, u32[]{:S(2)}) collective-permute-start(bf16[128,1280]{1,0:T(8,128)(2,1)S(1)} %get-tuple-element.56), channel_id=1, source_target_pairs={{0,3},{1,0},{2,1},{3,2},{4,7},{5,4},{6,5},{7,6},{8,11},{9,8},{10,9... | collective-permute-start | bytes 983048 | tf_op jit(solution)/shard_map/ppermute | solution.py:334
  64.5 16.6 %collective-permute-start.7 = (bf16[64,1280]{1,0:T(8,128)(2,1)S(1)}, bf16[64,1280]{1,0:T(8,128)(2,1)S(1)}, u32[]{:S(2)}, u32[]{:S(2)}) collective-permute-start(bf16[64,1280]{1,0:T(8,128)(2,1)S(1)} %get-tuple-element.65.refs_0_), channel_id=1, source_target_pairs={{0,4},{1,5},{2,6},{3,7},{4,0},{5,1},{6,2},{7,3},{8,12},{9,13},{10,... | collective-permute-start | bytes 491528 | tf_op jit(solution)/shard_map/ppermute | solution.py:337
  66.7 14.4 %collective-permute-start.8 = (bf16[64,1280]{1,0:T(8,128)(2,1)S(1)}, bf16[64,1280]{1,0:T(8,128)(2,1)S(1)}, u32[]{:S(2)}, u32[]{:S(2)}) collective-permute-start(bf16[64,1280]{1,0:T(8,128)(2,1)S(1)} %get-tuple-element.52), channel_id=1, source_target_pairs={{0,4},{1,5},{2,6},{3,7},{4,0},{5,1},{6,2},{7,3},{8,12},{9,13},{10,... | collective-permute-start | bytes 491528 | tf_op jit(solution)/shard_map/ppermute | solution.py:337
  77.6 5.2 %collective-permute-start.12 = (bf16[64,1280]{1,0:T(8,128)(2,1)S(1)}, bf16[64,1280]{1,0:T(8,128)(2,1)S(1)}, u32[]{:S(2)}, u32[]{:S(2)}) collective-permute-start(bf16[64,1280]{1,0:T(8,128)(2,1)S(1)} %get-tuple-element.59), channel_id=1, source_target_pairs={{0,4},{1,5},{2,6},{3,7},{4,0},{5,1},{6,2},{7,3},{8,12},{9,13},{10,... | collective-permute-start | bytes 491528 | tf_op jit(solution)/shard_map/ppermute | solution.py:337
  78.8 23.8 %copy-start.3 = (bf16[2,256,1280]{2,1,0:T(8,128)(2,1)S(1)}, bf16[2,256,1280]{2,1,0:T(8,128)(2,1)}, u32[]{:S(2)}) copy-start(bf16[2,256,1280]{2,1,0:T(8,128)(2,1)} %refs_2_.3) | copy-start | bytes 3932164
  81.1 21.6 %copy-start.2 = (bf16[2,256,1280]{2,1,0:T(8,128)(2,1)S(1)}, bf16[2,256,1280]{2,1,0:T(8,128)(2,1)}, u32[]{:S(2)}) copy-start(bf16[2,256,1280]{2,1,0:T(8,128)(2,1)} %refs_3_.2) | copy-start | bytes 3932164
  81.1 21.6 %copy-start.9 = (f32[2,32,256]{2,1,0:T(8,128)S(1)}, f32[2,32,256]{2,1,0:T(8,128)}, u32[]{:S(2)}) copy-start(f32[2,32,256]{2,1,0:T(8,128)} %refs_1_.3) | copy-start | bytes 196612
  102.7 18.9 %copy-start.12 = (bf16[64,1280]{1,0:T(8,128)(2,1)S(1)}, bf16[64,1280]{1,0:T(8,128)(2,1)}, u32[]{:S(2)}) copy-start(bf16[64,1280]{1,0:T(8,128)(2,1)} %copy-done.11) | copy-start | bytes 491524
  102.7 22.3 %copy-start.13 = (bf16[32,1280]{1,0:T(8,128)(2,1)S(1)}, bf16[32,1280]{1,0:T(8,128)(2,1)}, u32[]{:S(2)}) copy-start(bf16[32,1280]{1,0:T(8,128)(2,1)} %refs_3_.3) | copy-start | bytes 245764
  117.9 21.9 %copy-start.6 = (bf16[384,640]{1,0:T(8,128)(2,1)S(1)}, bf16[384,640]{1,0:T(8,128)(2,1)}, u32[]{:S(2)}) copy-start(bf16[384,640]{1,0:T(8,128)(2,1)} %copy-done.5) | copy-start | bytes 1474564
  117.9 13.5 %all-to-all-start.3 = ((bf16[16,8,384]{2,1,0:T(8,128)(2,1)}), bf16[16,8,384]{2,1,0:T(8,128)(2,1)S(1)}, u32[]{:S(2)}, u32[]{:S(2)}) async-start(bf16[16,8,384]{2,1,0:T(8,128)(2,1)} %shard_map.114), calls=%async_computation.3 | async-start | bytes 196608 | tf_op jit(solution)/shard_map/all_to_all | solution.py:415
  121.6 15.1 %collective-permute-start.15 = (bf16[128,1280]{1,0:T(8,128)(2,1)S(1)}, bf16[128,1280]{1,0:T(8,128)(2,1)S(1)}, u32[]{:S(2)}, u32[]{:S(2)}) collective-permute-start(bf16[128,1280]{1,0:T(8,128)(2,1)S(1)} %shard_map.116.refs_0_), channel_id=1, source_target_pairs={{0,2},{1,3},{2,0},{3,1},{4,6},{5,7},{6,4},{7,5},{8,10},{9,11},{10,... | collective-permute-start | bytes 983048 | tf_op jit(solution)/shard_map/ppermute | solution.py:334
  122.3 17.6 %collective-permute-start.14 = (bf16[128,1280]{1,0:T(8,128)(2,1)S(1)}, bf16[128,1280]{1,0:T(8,128)(2,1)S(1)}, u32[]{:S(2)}, u32[]{:S(2)}) collective-permute-start(bf16[128,1280]{1,0:T(8,128)(2,1)S(1)} %shard_map.116.refs_0_), channel_id=1, source_target_pairs={{0,1},{1,2},{2,3},{3,0},{4,5},{5,6},{6,7},{7,4},{8,9},{9,10},{10,1... | collective-permute-start | bytes 983048 | tf_op jit(solution)/shard_map/ppermute | solution.py:334
  122.5 17.4 %collective-permute-start.13 = (bf16[128,1280]{1,0:T(8,128)(2,1)S(1)}, bf16[128,1280]{1,0:T(8,128)(2,1)S(1)}, u32[]{:S(2)}, u32[]{:S(2)}) collective-permute-start(bf16[128,1280]{1,0:T(8,128)(2,1)S(1)} %shard_map.116.refs_0_), channel_id=1, source_target_pairs={{0,3},{1,0},{2,1},{3,2},{4,7},{5,4},{6,5},{7,6},{8,11},{9,8},{10,9... | collective-permute-start | bytes 983048 | tf_op jit(solution)/shard_map/ppermute | solution.py:334
  132.2 11.6 %all-to-all-start.4 = ((f32[16,8,384]{2,1,0:T(8,128)}), f32[16,8,384]{2,1,0:T(8,128)S(1)}, u32[]{:S(2)}, u32[]{:S(2)}) async-start(f32[16,8,384]{2,1,0:T(8,128)} %shard_map.115), calls=%async_computation.4 | async-start | bytes 393216 | tf_op jit(solution)/shard_map/all_to_all | solution.py:415
  (2 other events, 1.7 us)
